TPU v7x, 128 devices: a whole 4x4x4 slice. The times are simulated.
128 devices in a mesh: dp: 4 (over z), ctx: 32 (over x, y, core).
Axes of the slice: x: 4, y: 4, z: 4, core: 2. Of those that a mesh axis runs over, the one named last changes fastest.
Arguments:
- mamba_in: bfloat16 [4, 4096, 3584], P('dp', 'ctx'), may hold values from -30 to 30
- step_raw: float32 [4, 56, 4096], P('dp', None, 'ctx'), may hold values from -3 to 15
- state_in: bfloat16 [4, 4096, 64], P('dp', 'ctx'), may hold values from -0.75 to 0.75
- state_out: bfloat16 [4, 4096, 64], P('dp', 'ctx'), may hold values from -6 to 6
- log_rate: float32 [56], replicated, may hold values from -7.5 to 1.6
- step_bias: float32 [56], replicated, may hold values from -6 to -4.5
- skip_gain: float32 [56], replicated, may hold values from 0.5 to 1.5
- norm_gain: float32 [3584], replicated, may hold values from 0.5 to 1.5
- doc_lengths: int32 [4, 32, 8], P('dp'), may hold values from 1 to 64, as said below
- doc_moved: int32 [4, 32, 8], P('dp'), may hold values from 0 to 1, as said below
- queries: bfloat16 [4, 4096, 3584], P('dp', 'ctx'), may hold values from -16 to 16
- attn_keys: bfloat16 [4, 4096, 3584], P('dp', 'ctx'), may hold values from -16 to 16
- attn_grad: bfloat16 [4, 6144, 3584], P('dp', 'ctx'), may hold values from -12 to 12
Outputs:
- attn_out: bfloat16 [4, 6144, 3584], P('dp', 'ctx')
- grad_queries: bfloat16 [4, 4096, 3584], P('dp', 'ctx')
- grad_keys: bfloat16 [4, 4096, 3584], P('dp', 'ctx')
- grad_mamba_in: bfloat16 [4, 4096, 3584], P('dp', 'ctx')
- grad_state_in: bfloat16 [4, 4096, 64], P('dp', 'ctx')
- grad_state_out: bfloat16 [4, 4096, 64], P('dp', 'ctx')
- grad_step: float32 [4, 56, 4096], P('dp', None, 'ctx')
- grad_heads: float32 [3, 56], replicated
- grad_gain: float32 [3584], replicated
Inputs may be any that keep to these rules, and one draw needn't show every extreme that they name: `doc_lengths`: in every row the 8 lengths sum to 128, and the longest is exactly 64. `doc_moved`: the documents marked 1 in one row hold at most 64 positions together, exactly 64 in some row of every draw.
All inputs are finite; a program needn't handle non-finite values.
Results may differ from a plain program's by a relative error of at most 0.0078.
Values may be sent and summed in bfloat16 or wider, within the bound.
No kernel may reach another device: no remote copies, remote signals or barrier semaphores. Data moves between devices by JAX's collectives and lax.ppermute only.
A program may use at most 192 MiB of HBM per device.

v0:
```python
import math

import jax
import jax.numpy as jnp
from jax import lax
from jax.sharding import PartitionSpec as P

ATTN_HEADS = 16


HIGH = lax.Precision.HIGHEST
EPSILON = 1e-05
MASKED = -1e30


def carried_in(value, axis, combine, identity, reverse):
    devices, mine = (lax.axis_size(axis), lax.axis_index(axis))
    everything = jax.tree.map(lambda part: lax.all_gather(part, axis), value)
    start = jax.tree.map(
        lambda part, zero: jnp.broadcast_to(jnp.asarray(zero, part.dtype), part.shape),
        value,
        identity,
    )

    def hop(k, before):
        at = devices - 1 - k if reverse else k
        reached = at > mine if reverse else at < mine
        new = combine(before, jax.tree.map(lambda part: part[at], everything))
        return jax.tree.map(lambda a, b: jnp.where(reached, a, b), new, before)

    return lax.fori_loop(0, devices, hop, start)


def partner_2(value, axis, apart):
    return lax.ppermute(value, axis, [(i, i ^ 1 << apart) for i in range(lax.axis_size(axis))])


def decay_sums(raw_steps, step_bias, log_rate):
    step_size = jax.nn.softplus(raw_steps + step_bias[:, None])
    rates = -jnp.exp(log_rate)[:, None] * step_size
    return (step_size, jnp.cumsum(rates, axis=1))


def local_states(x_rows, raw_steps, step_bias, log_rate, in_rows):
    tokens, width = x_rows.shape
    heads = raw_steps.shape[0]
    step_size, running = decay_sums(raw_steps, step_bias, log_rate)
    total = jnp.exp(running[:, -1])
    tail = jnp.exp(running[:, -1:] - running) * step_size
    scaled = x_rows.reshape(tokens, heads, width // heads) * jnp.transpose(tail)[:, :, None]
    carry = jnp.einsum("thp,tn->hpn", scaled, in_rows, precision=HIGH)
    return (total, carry)


def local_outputs(
    x_rows, raw_steps, step_bias, log_rate, skip_gain, in_rows, out_rows, start_state
):
    tokens, width = x_rows.shape
    heads = raw_steps.shape[0]
    step_size, running = decay_sums(raw_steps, step_bias, log_rate)
    row_index = jnp.arange(tokens, dtype=jnp.int32)
    causal = row_index[:, None] >= row_index[None, :]
    gaps = jnp.where(causal[None], running[:, :, None] - running[:, None, :], MASKED)
    gram = jnp.dot(out_rows, jnp.transpose(in_rows), precision=HIGH)
    mixing = jnp.exp(gaps) * gram[None] * step_size[:, None, :]
    x_heads = x_rows.reshape(tokens, heads, width // heads)
    inner = jnp.einsum("hts,shp->thp", mixing, x_heads, precision=HIGH)
    carried = jnp.einsum("tn,hpn->thp", out_rows, start_state, precision=HIGH)
    carried = carried * jnp.transpose(jnp.exp(running))[:, :, None]
    result = inner + carried + skip_gain[None, :, None] * x_heads
    return result.reshape(tokens, width)


def normalize(mixed, gain):
    power = jnp.mean(mixed * mixed, axis=-1, keepdims=True)
    return mixed * lax.rsqrt(power + EPSILON) * gain


def link_states(earlier, later):
    return (earlier[0] * later[0], later[0][:, None, None] * earlier[1] + later[1])


def doc_layout(lengths, moved, tokens):
    ends = jnp.cumsum(lengths)
    entry_indices = jnp.arange(tokens, dtype=jnp.int32)
    segments = jnp.sum((entry_indices[:, None] >= ends[None, :]).astype(jnp.int32), axis=1)
    labels = jnp.arange(lengths.shape[0], dtype=jnp.int32)
    moving = jnp.sum(jnp.where(segments[:, None] == labels[None, :], moved[None, :], 0), axis=1)
    slot_index = jnp.cumsum(moving) - 1
    return (segments, moving, slot_index, jnp.sum(moving))


def pick_mask(moving, slot_index, slots):
    targets = jnp.arange(slots, dtype=jnp.int32)
    return (slot_index[None, :] == targets[:, None]) & (moving[None, :] == 1)


def attend(q_rows, k_rows, v_rows, segments, heads):
    rows, width = q_rows.shape
    size = width // heads
    scale = 1.0 / math.sqrt(size)
    q_heads = q_rows.reshape(rows, heads, size)
    k_heads = k_rows.reshape(rows, heads, size)
    v_heads = v_rows.reshape(rows, heads, size)
    scores = (
        jnp.einsum("qhd,khd->hqk", q_heads, k_heads, preferred_element_type=jnp.float32) * scale
    )
    row_index = jnp.arange(rows, dtype=jnp.int32)
    allowed = (segments[:, None] == segments[None, :]) & (row_index[None, :] <= row_index[:, None])
    scores = jnp.where(allowed[None], scores, MASKED)
    peak = jnp.max(scores, axis=-1, keepdims=True)
    weights = jnp.exp(scores - peak)
    probs = weights / jnp.sum(weights, axis=-1, keepdims=True)
    probs_low = probs.astype(jnp.bfloat16)
    mixed = jnp.einsum("hqk,khd->qhd", probs_low, v_heads, preferred_element_type=jnp.float32)
    return (mixed.astype(jnp.bfloat16).reshape(rows, width), probs, probs_low)


def attend_back(q_rows, k_rows, v_rows, probs, probs_low, grad_rows, heads):
    rows, width = q_rows.shape
    size = width // heads
    scale = 1.0 / math.sqrt(size)
    q_heads = q_rows.reshape(rows, heads, size)
    k_heads = k_rows.reshape(rows, heads, size)
    v_heads = v_rows.reshape(rows, heads, size)
    grad_heads = grad_rows.reshape(rows, heads, size)
    dprobs = jnp.einsum("qhd,khd->hqk", grad_heads, v_heads, preferred_element_type=jnp.float32)
    delta = jnp.sum(probs * dprobs, axis=-1, keepdims=True)
    dscores = (probs * (dprobs - delta) * scale).astype(jnp.bfloat16)
    grad_query = jnp.einsum("hqk,khd->qhd", dscores, k_heads, preferred_element_type=jnp.float32)
    grad_key = jnp.einsum("hqk,qhd->khd", dscores, q_heads, preferred_element_type=jnp.float32)
    grad_value = jnp.einsum(
        "hqk,qhd->khd", probs_low, grad_heads, preferred_element_type=jnp.float32
    )
    return (
        grad_query.astype(jnp.bfloat16).reshape(rows, width),
        grad_key.astype(jnp.bfloat16).reshape(rows, width),
        grad_value.astype(jnp.bfloat16).reshape(rows, width),
    )


def local(
    mamba_in,
    step_raw,
    state_in,
    state_out,
    log_rate,
    step_bias,
    skip_gain,
    norm_gain,
    doc_lengths,
    doc_moved,
    queries,
    attn_keys,
    attn_grad,
):
    x_rows = mamba_in[0].astype(jnp.float32)
    raw_steps = step_raw[0]
    in_rows = state_in[0].astype(jnp.float32)
    out_rows = state_out[0].astype(jnp.float32)
    query_rows = queries[0]
    key_rows = attn_keys[0]
    grad_rows = attn_grad[0]
    tokens = x_rows.shape[0]
    sent_rows = grad_rows.shape[0] - tokens
    heads = raw_steps.shape[0]
    shards = lax.axis_size("ctx")
    my_index = lax.axis_index("ctx")
    swap_bit = (shards // 2).bit_length() - 1
    decay_total, local_carry = local_states(x_rows, raw_steps, step_bias, log_rate, in_rows)
    state_back = jax.vjp(local_states, x_rows, raw_steps, step_bias, log_rate, in_rows)[1]
    identity = (jnp.ones((heads,), jnp.float32), jnp.zeros_like(local_carry))
    start_state = carried_in((decay_total, local_carry), "ctx", link_states, identity, False)[1]
    mamba_out, out_back = jax.vjp(
        local_outputs,
        x_rows,
        raw_steps,
        step_bias,
        log_rate,
        skip_gain,
        in_rows,
        out_rows,
        start_state,
    )
    normed, norm_back = jax.vjp(normalize, mamba_out, norm_gain)
    drawn_numbers = normed.astype(jnp.bfloat16)
    own_lengths = lax.dynamic_index_in_dim(doc_lengths[0], my_index, 0, keepdims=False)
    own_moved = lax.dynamic_index_in_dim(doc_moved[0], my_index, 0, keepdims=False)
    own_seg, own_moving, own_slot, own_count = doc_layout(own_lengths, own_moved, tokens)
    kept_mask = own_moving == 0
    own_pick = pick_mask(own_moving, own_slot, sent_rows).astype(jnp.bfloat16)
    partner = jnp.bitwise_xor(my_index, shards // 2)
    part_lengths = lax.dynamic_index_in_dim(doc_lengths[0], partner, 0, keepdims=False)
    part_moved = lax.dynamic_index_in_dim(doc_moved[0], partner, 0, keepdims=False)
    part_seg, part_moving, part_slot, part_count = doc_layout(part_lengths, part_moved, tokens)
    part_pick = pick_mask(part_moving, part_slot, sent_rows)
    arrived_seg = jnp.sum(jnp.where(part_pick, part_seg[None, :], 0), axis=1)
    slot_index = jnp.arange(sent_rows, dtype=jnp.int32)
    arrived_live = slot_index < part_count
    stacked = jnp.stack([query_rows, key_rows, drawn_numbers])
    packed = jnp.einsum(
        "st,ktd->ksd", own_pick, stacked, preferred_element_type=jnp.float32
    ).astype(jnp.bfloat16)
    arrived = partner_2(packed, "ctx", swap_bit)
    kept_rows = kept_mask[:, None]
    layout_query = jnp.concatenate(
        [jnp.where(kept_rows, query_rows, jnp.zeros_like(query_rows)), arrived[0]], axis=0
    )
    layout_key = jnp.concatenate(
        [jnp.where(kept_rows, key_rows, jnp.zeros_like(key_rows)), arrived[1]], axis=0
    )
    layout_value = jnp.concatenate(
        [jnp.where(kept_rows, drawn_numbers, jnp.zeros_like(drawn_numbers)), arrived[2]], axis=0
    )
    row_index = jnp.arange(tokens, dtype=jnp.int32)
    layout_seg = jnp.concatenate(
        [
            jnp.where(kept_mask, own_seg, -1 - row_index),
            jnp.where(arrived_live, own_lengths.shape[0] + arrived_seg, -1 - tokens - slot_index),
        ]
    )
    attn_rows, probs, probs_low = attend(
        layout_query, layout_key, layout_value, layout_seg, ATTN_HEADS
    )
    layout_query_grad, layout_key_grad, layout_value_grad = attend_back(
        layout_query, layout_key, layout_value, probs, probs_low, grad_rows, ATTN_HEADS
    )
    tails = jnp.stack(
        [layout_query_grad[tokens:], layout_key_grad[tokens:], layout_value_grad[tokens:]]
    )
    returned = partner_2(tails, "ctx", swap_bit)
    unpacked = jnp.einsum(
        "st,ksd->ktd", own_pick, returned, preferred_element_type=jnp.float32
    ).astype(jnp.bfloat16)
    grad_query = jnp.where(kept_rows, layout_query_grad[:tokens], unpacked[0])
    grad_key = jnp.where(kept_rows, layout_key_grad[:tokens], unpacked[1])
    grad_value = jnp.where(kept_rows, layout_value_grad[:tokens], unpacked[2])
    grad_mixed, gain_part = norm_back(grad_value.astype(jnp.float32))
    back_out = out_back(grad_mixed)
    state_grad = carried_in((decay_total, back_out[7]), "ctx", link_states, identity, True)[1]
    total_grad = jnp.sum(state_grad * start_state, axis=(1, 2))
    back_states = state_back((total_grad, state_grad))
    grad_x = (back_out[0] + back_states[0]).astype(jnp.bfloat16)
    grad_raw = back_out[1] + back_states[1]
    grad_in = (back_out[5] + back_states[4]).astype(jnp.bfloat16)
    grad_out_map = back_out[6].astype(jnp.bfloat16)
    head_terms = jnp.stack(
        [back_out[3] + back_states[3], back_out[2] + back_states[2], back_out[4]]
    )
    head_sum, gain_sum = lax.psum((head_terms, gain_part), ("dp", "ctx"))
    return (
        attn_rows[None],
        grad_query[None],
        grad_key[None],
        grad_x[None],
        grad_in[None],
        grad_out_map[None],
        grad_raw[None],
        head_sum,
        gain_sum,
    )


def solution(mesh):
    in_specs = (
        P("dp", "ctx", None),
        P("dp", None, "ctx"),
        P("dp", "ctx", None),
        P("dp", "ctx", None),
        P(),
        P(),
        P(),
        P(),
        P("dp", None, None),
        P("dp", None, None),
        P("dp", "ctx", None),
        P("dp", "ctx", None),
        P("dp", "ctx", None),
    )
    out_specs = (
        P("dp", "ctx", None),
        P("dp", "ctx", None),
        P("dp", "ctx", None),
        P("dp", "ctx", None),
        P("dp", "ctx", None),
        P("dp", "ctx", None),
        P("dp", None, "ctx"),
        P(),
        P(),
    )
    return jax.shard_map(local, mesh=mesh, in_specs=in_specs, out_specs=out_specs, check_vma=False)
```

profile of v0, /device:TPU:1, one launch (start us, length us, event | category | flops | bytes accessed | tf_op | source)
XLA Modules:
  0.0 818.6 jit_solution(11049321901450678286)
XLA Ops:
  16.4 66.1 %all-reduce.2 = f32[1792]{0:T(1024)S(1)} all-reduce(f32[1792]{0:T(1024)S(1)} %dynamic-update-slice), channel_id=2, replica_groups=mesh['dp'=4,'ctx'=32] {'ctx'}, use_global_device_ids=true, to_apply=%add.2 | all-reduce | flops 1792 | bytes 14336
  94.0 4.5 reshape_squeeze.3
  98.9 99.3 %all-gather.6.cloned.1.call-done = f32[1792,64,64]{2,1,0:T(8,128)} async-done(((f32[56,64,64]{2,1,0:T(8,128)}), f32[1792,64,64]{2,1,0:T(8,128)}) %all-gather.6.cloned.1.call-update) | async-done | bytes 29360144 | tf_op jit(solution)/shard_map/all_gather | solution.py:18
  198.2 63.1 %while.30 = (s32[]{:T(128)}, f32[56,64,64]{2,1,0:T(8,128)S(1)}, s32[]{:T(128)}, f32[32,56]{1,0:T(8,128)S(1)}, f32[32,56,64,64]{3,2,1,0:T(8,128)}, /*index=5*/s32[]{:T(128)}, s32[]{:T(128)}) while((s32[]{:T(128)}, f32[56,64,64]{2,1,0:T(8,128)S(1)}, s32[]{:T(128)}, f32[32,56]{1,0:T(8,128)S(1)}, f32[32,56,64,64]{3,2,1,0:T(8,128)}, ...), condition=%wide.region_6.8_spmd.clone, body=%wide.region_5.7_spmd.clone.sunk | while | flops 917508 | bytes 2753297 | solution.py:31
  262.3 5.3 multiply_reduce_fusion.3
  267.6 2.7 copy.190
  274.0 2.7 collective-permute-start
  278.3 2.9 copy.189
  281.2 4.0 broadcast_select_fusion.1
  285.3 22.4 %collective-permute-done = bf16[3,64,3584]{2,1,0:T(8,128)(2,1)} collective-permute-done((bf16[3,64,3584]{2,1,0:T(8,128)(2,1)}, bf16[3,64,3584]{2,1,0:T(8,128)(2,1)}, u32[]{:S(2)}, u32[]{:S(2)}) %collective-permute-start) | collective-permute-done | bytes 1376288 | tf_op jit(solution)/shard_map/ppermute | solution.py:35
  312.7 2.6 concatenate.26
  317.2 2.6 concatenate.24
  327.5 2.4 fusion.69
  330.0 7.6 fusion.64
  337.5 7.9 fusion.62
  347.6 2.7 stack.29
  352.4 2.7 stack.28
  357.3 2.7 stack.27
  359.9 2.5 pad_maximum_fusion.3
  362.5 2.4 collective-permute-start.1
  370.8 11.9 %copy.209 = bf16[128,16,224]{0,2,1:T(8,128)(2,1)} copy(bf16[128,16,224]{2,0,1:T(8,128)(2,1)} %slice.82) | data formatting | bytes 1835008 | tf_op jit(solution)/shard_map/slice | solution.py:236
  387.2 7.7 collective-permute-done.1
  406.5 3.0 fusion.61
  411.5 4.4 broadcast_in_dim_reshape.3
  420.5 6.8 fusion.24
  428.0 4.7 fusion.71
  433.5 152.1 %all-gather.8.cloned.1.call-done = f32[1792,64,64]{2,1,0:T(8,128)} async-done(((f32[56,64,64]{2,1,0:T(8,128)}), f32[1792,64,64]{2,1,0:T(8,128)}) %all-gather.8.cloned.1.call-update) | async-done | bytes 29360144 | tf_op jit(solution)/shard_map/all_gather | solution.py:18
  585.6 136.4 %while.31 = (s32[]{:T(128)}, f32[56,64,64]{2,1,0:T(8,128)}, s32[]{:T(128)}, f32[32,56]{1,0:T(8,128)}, f32[32,56,64,64]{3,2,1,0:T(8,128)}, /*index=5*/s32[]{:T(128)}, s32[]{:T(128)}, s32[]{:T(128)}, s32[]{:T(128)}) while((s32[]{:T(128)}, f32[56,64,64]{2,1,0:T(8,128)}, s32[]{:T(128)}, f32[32,56]{1,0:T(8,128)}, ...), condition=%wide.region_20.22_spmd.clone, body=%wide.region_19.21_spmd.clone.sunk | while | flops 917512 | bytes 2753359 | solution.py:31
  586.3 3.0 fusion.150
  590.1 3.6 fusion.150
  594.3 3.6 fusion.150
  598.6 3.6 fusion.150
  602.9 3.6 fusion.150
  607.1 3.6 fusion.150
  611.4 3.6 fusion.150
  615.7 3.6 fusion.150
  620.0 3.6 fusion.150
  624.2 3.6 fusion.150
  628.5 3.6 fusion.150
  632.8 3.6 fusion.150
  637.1 3.6 fusion.150
  641.3 3.6 fusion.150
  645.6 3.6 fusion.150
  649.9 3.6 fusion.150
  654.2 3.6 fusion.150
  658.4 3.6 fusion.150
  662.7 3.6 fusion.150
  667.0 3.6 fusion.150
  671.3 3.6 fusion.150
  675.5 3.6 fusion.150
  679.8 3.6 fusion.150
  684.1 3.6 fusion.150
  688.4 3.6 fusion.150
  692.6 3.6 fusion.150
  696.9 3.6 fusion.150
  701.2 3.6 fusion.150
  705.5 3.6 fusion.150
  709.7 3.6 fusion.150
  714.0 3.6 fusion.150
  718.3 3.6 fusion.150
  722.1 5.9 fusion.30
  733.3 4.7 fusion.74
  738.0 5.6 fusion.32
  746.5 64.8 %all-reduce.3 = (f32[3,56]{1,0:T(4,128)}, f32[3584]{0:T(1024)}) all-reduce(f32[3,56]{1,0:T(4,128)S(1)} %pad_maximum_fusion.10, f32[3584]{0:T(1024)S(1)} %copy-done.20), channel_id=1, replica_groups=mesh['dp'=4,'ctx'=32] {'dp','ctx'}, use_global_device_ids=true, to_apply=%region_36.38 | all-reduce | flops 3752 | bytes 30016 | tf_op jit(solution)/shard_map/psum | solution.py:250
  (303 shorter events, 169.7 us)
Async XLA Ops:
  7.2 4.8 copy-start
  7.2 4.5 copy-start.30
  7.2 191.0 %all-gather.6.cloned.1.call-start = ((), (), s32[]{:S(2)}) async-start(), calls=%async_computation | async-start | bytes 60555264 | tf_op jit(solution)/shard_map/all_gather | solution.py:18
  7.9 3.8 copy-start.37
  14.2 0.7 copy-start.46
  14.2 68.5 %copy-start.28 = (s32[1,32,8]{1,2,0:T(8,128)S(1)}, s32[1,32,8]{1,2,0:T(8,128)}, u32[]{:S(2)}) copy-start(s32[1,32,8]{1,2,0:T(8,128)} %param.27) | copy-start | bytes 3076
  14.2 68.5 %copy-start.29 = (s32[1,32,8]{1,2,0:T(8,128)S(1)}, s32[1,32,8]{1,2,0:T(8,128)}, u32[]{:S(2)}) copy-start(s32[1,32,8]{1,2,0:T(8,128)} %param.26) | copy-start | bytes 3076
  14.2 571.4 %all-gather.8.cloned.1.call-start = ((), (), s32[]{:S(2)}) async-start(), calls=%async_computation.1 | async-start | bytes 60555264 | tf_op jit(solution)/shard_map/all_gather | solution.py:18
  82.7 179.6 %copy-start.22 = (f32[56,128]{1,0:T(8,128)}, f32[56,128]{1,0:T(8,128)S(1)}, u32[]{:S(2)}) copy-start(f32[56,128]{1,0:T(8,128)S(1)} %copy.183) | copy-start | bytes 86020
  88.2 4.5 copy-start.16
  92.7 6.0 copy-start.15
  98.5 163.8 %copy-start.25 = (pred[128,128]{1,0:T(8,128)(4,1)}, pred[128,128]{1,0:T(8,128)(4,1)S(1)}, u32[]{:S(2)}) copy-start(pred[128,128]{1,0:T(8,128)(4,1)S(1)} %iota_compare_fusion.1) | copy-start | bytes 49156
  98.7 298.5 %copy-start.35 = (pred[128]{0:T(512)(128)(4,1)}, pred[128]{0:T(512)(128)(4,1)S(1)}, u32[]{:S(2)}) copy-start(pred[128]{0:T(512)(128)(4,1)S(1)} %get-tuple-element.398) | copy-start | bytes 388
  98.9 163.4 %copy-start.17 = (f32[128,128]{1,0:T(8,128)}, f32[128,128]{1,0:T(8,128)S(1)}, u32[]{:S(2)}) copy-start(f32[128,128]{1,0:T(8,128)S(1)} %fusion.107) | copy-start | bytes 196612
  261.2 1.0 copy-start.24
  261.2 1.1 copy-start.43
  262.3 5.3 copy-start.5
  267.6 2.8 copy-start.44
  270.4 1.9 copy-start.13
  270.4 2.0 copy-start.14
  270.4 10.9 %copy-start.32 = (f32[128]{0:T(128)}, f32[128]{0:T(128)S(1)}, u32[]{:S(2)}) copy-start(f32[128]{0:T(128)S(1)} %fusion.117) | copy-start | bytes 1540
  274.0 33.6 %collective-permute-start = (bf16[3,64,3584]{2,1,0:T(8,128)(2,1)}, bf16[3,64,3584]{2,1,0:T(8,128)(2,1)}, u32[]{:S(2)}, u32[]{:S(2)}) collective-permute-start(bf16[3,64,3584]{2,1,0:T(8,128)(2,1)} %fusion.5), channel_id=1, source_target_pairs={{0,16},{1,17},{2,18},{3,19},{4,20},{5,21},{6,22},{7,23},{8,24},{9,... | collective-permute-start | bytes 4128776 | tf_op jit(solution)/shard_map/ppermute | solution.py:35
  321.0 0.8 copy-start.11
  321.8 2.3 copy-start.21
  324.1 1.4 copy-start.6
  325.1 2.3 copy-start.47
  325.1 12.4 %copy-start.48 = (f32[16,192]{1,0:T(8,128)}, f32[16,192]{1,0:T(8,128)S(1)}, u32[]{:S(2)}) copy-start(f32[16,192]{1,0:T(8,128)S(1)} %get-tuple-element.402) | copy-start | bytes 36868
  325.5 2.0 copy-start.7
  362.5 32.4 %collective-permute-start.1 = (bf16[3,64,3584]{2,1,0:T(8,128)(2,1)}, bf16[3,64,3584]{2,1,0:T(8,128)(2,1)}, u32[]{:S(2)}, u32[]{:S(2)}) collective-permute-start(bf16[3,64,3584]{2,1,0:T(8,128)(2,1)} %pad_maximum_fusion.3), channel_id=1, source_target_pairs={{0,16},{1,17},{2,18},{3,19},{4,20},{5,21},{6,22},{7,23},{8,24},{9,... | collective-permute-start | bytes 4128776 | tf_op jit(solution)/shard_map/ppermute | solution.py:35
  365.0 4.8 copy-start.12
  387.2 10.0 %copy-start.9 = (bf16[128,16,224]{0,2,1:T(8,128)(2,1)S(1)}, bf16[128,16,224]{0,2,1:T(8,128)(2,1)}, u32[]{:S(2)}) copy-start(bf16[128,16,224]{0,2,1:T(8,128)(2,1)} %copy.209) | copy-start | bytes 2752516
  387.2 10.0 %copy-start.10 = (bf16[128,16,224]{0,2,1:T(8,128)(2,1)S(1)}, bf16[128,16,224]{0,2,1:T(8,128)(2,1)}, u32[]{:S(2)}) copy-start(bf16[128,16,224]{0,2,1:T(8,128)(2,1)} %copy.204) | copy-start | bytes 2752516
  397.2 1.9 copy-start.4
  397.2 2.4 copy-start.8
  397.2 2.4 copy-start.33
  399.6 2.1 copy-start.45
  402.2 1.3 copy-start.2
  405.8 0.7 copy-start.49
  415.9 4.6 copy-start.18
  415.9 4.6 copy-start.23
  415.9 4.6 copy-start.26
  722.1 5.9 copy-start.1
  728.0 2.0 copy-start.31
  729.9 0.5 copy-start.34
  730.5 7.5 copy-start.3
  730.5 7.5 copy-start.19
  730.5 7.5 copy-start.27
  743.6 2.8 copy-start.41
  743.6 2.8 copy-start.42
  743.6 2.8 copy-start.38
  743.7 2.8 copy-start.39
  743.7 2.8 copy-start.40
  743.7 2.8 copy-start.36
  743.7 2.9 copy-start.20
Sparse Core Ops, SparseCore 0:
  14.4 183.7 all-gather.5
  405.9 179.6 all-gather.7
where the time goes:
time: 829 us; the launch traced here: 819 us
  waiting for transfers between devices  281 us (34%)
  other arithmetic  199 us (24%)
  blocking collectives  131 us (16%)
  local copies, waits for them, and re-layouts  115 us (14%)
  matrix products  69.2 us (8%)
  between operations  15.9 us (2%)
    all_gather x2, waiting for transfers between devices, carried_in(): everything = jax.tree.map(lambda part: lax.all_gather(part, axis), value)  251 us
    select_n x64, other arithmetic, hop(): return jax.tree.map(lambda a, b: jnp.where(reached, a, b), new, before)  176 us
    unnamed x1, blocking collectives  66.1 us
    psum x1, blocking collectives, local(): head_sum, gain_sum = lax.psum((head_terms, gain_part), ('dp', 'ctx'))  64.8 us
    ppermute x2, waiting for transfers between devices, partner_2(): lax.ppermute(value, axis, [(i, i ^ 1 << apart) for i in range(lax.axis_si...  30 us
    mul x64, local copies, waits for them, and re-layouts, link_states(): later[0][:, None, None] * earlier[1] + later[1]  22.4 us
    unnamed x111, local copies, waits for them, and re-layouts  19.4 us
    dot_general x3, matrix products, local_outputs(): inner = jnp.einsum('hts,shp->thp', mixing, x_heads, precision=HIGH)  17.7 us
  transfers between devices with their start and end apart: 4, of which 4 were waited for; matrix products, arithmetic and copies ran while one was open for 9% of the time, Pallas kernels for 0%

commit v1 on v0

v1 whole, which is shorter than its diff:
```python
import functools
import math

import jax
import jax.numpy as jnp
from jax import lax
from jax.experimental import pallas as pl
from jax.experimental.pallas import tpu as pltpu
from jax.sharding import PartitionSpec as P

F32 = jnp.float32
BF16 = jnp.bfloat16
HIGH = lax.Precision.HIGHEST
EPSILON = 1e-05
MASKED = -1e30

TOK = 128
HEADS = 56
SIZE = 64
GROUPS = 4
GW = 896
GH = 14
AH = 4
ASIZE = 224
WIDTH = GROUPS * GW
SEND = 64
WINDOWS = ((0, 2), (1, 3), (3, 3), (5, 2))

NT = (((1,), (1,)), ((), ()))
TN = (((0,), (0,)), ((), ()))


def dot(a, b, dims=(((1,), (0,)), ((), ())), precision=None):
    return lax.dot_general(a, b, dims, precision=precision, preferred_element_type=F32)


def iota(shape, dim):
    return lax.broadcasted_iota(jnp.int32, shape, dim)


def pad_heads(rows):
    gap = jnp.zeros((2, rows.shape[1]), rows.dtype)
    parts = []
    for g in range(GROUPS):
        parts += [rows[g * GH : (g + 1) * GH], gap]
    return jnp.concatenate(parts, axis=0)


def unpad_heads(rows):
    return jnp.concatenate([rows[16 * g : 16 * g + GH] for g in range(GROUPS)], axis=0)


def columns(*rows):
    stack = jnp.concatenate(list(rows) + [jnp.zeros((8 - len(rows), HEADS), F32)], axis=0)
    stack = jnp.concatenate([stack, jnp.zeros((8, 128 - HEADS), F32)], axis=1)
    turned = pad_heads(jnp.transpose(stack)[:HEADS])
    return [turned[:, i : i + 1] for i in range(len(rows))]


def expander(group, parts=2):
    shape = (64 * parts, GW)
    return jnp.where(
        (iota(shape, 0) & 63) == (iota(shape, 1) >> 6) + 16 * group, 1.0, 0.0
    ).astype(BF16)


def split(value):
    high = value.astype(BF16)
    low = (value - high.astype(F32)).astype(BF16)
    return high, low


def stacked_parts(value):
    high, low = split(value)
    return jnp.transpose(jnp.concatenate([high.astype(F32), low.astype(F32)], axis=0)).astype(BF16)


def decay_sums(raw, bias, rate):
    z = pad_heads(raw) + bias
    step = jnp.maximum(z, 0.0) + jnp.log1p(jnp.exp(-jnp.abs(z)))
    neg = -jnp.exp(rate)
    tri = jnp.where(iota((TOK, TOK), 0) <= iota((TOK, TOK), 1), 1.0, 0.0)
    running = dot(neg * step, tri, precision=HIGH)
    return z, step, neg, running


def lanes(g):
    return pl.ds(pl.multiple_of(g * GW, 128), GW)


def rows64(g):
    return pl.ds(pl.multiple_of(g * SIZE, SIZE), SIZE)


def states_kernel(x_ref, raw_ref, in_ref, rate_ref, bias_ref, out_ref):
    rate, bias = columns(rate_ref[...], bias_ref[...])
    _, step, _, running = decay_sums(raw_ref[...], bias, rate)
    last = running[:, TOK - 1 :]
    tail = stacked_parts(jnp.exp(last - running) * step)
    total = stacked_parts(jnp.broadcast_to(jnp.exp(last), running.shape))[:SIZE]
    turned = jnp.transpose(in_ref[...].astype(F32)).astype(BF16)
    for g in range(GROUPS):
        wide = dot(tail, expander(g))
        scaled = (x_ref[:, g * GW : (g + 1) * GW].astype(F32) * wide).astype(BF16)
        out_ref[g * SIZE : (g + 1) * SIZE, :GW] = dot(turned, scaled).astype(BF16)
        out_ref[g * SIZE : (g + 1) * SIZE, GW:] = total


def scan_kernel(blocks, reverse, carry_ref, total_ref, out_ref, wide_ref):
    group = lax.axis_index("ctx") // 8
    wide_ref[...] = dot(total_ref[:, GW:], expander(group))
    state = jnp.zeros((8, GW), F32)
    pairs = range(blocks // 2)
    for i in reversed(pairs) if reverse else pairs:
        rows = slice(16 * i, 16 * i + 16)
        carry = carry_ref[rows, :GW].astype(F32)
        first = state
        at = slice(8, 16) if reverse else slice(0, 8)
        second = wide_ref[rows][at] * first + carry[at]
        at = slice(0, 8) if reverse else slice(8, 16)
        state = wide_ref[rows][at] * second + carry[at]
        both = [second, first] if reverse else [first, second]
        out_ref[rows, :] = jnp.concatenate(both, axis=0).astype(BF16)


def lane_masks():
    masks = []
    for i, (tile, tiles) in enumerate(WINDOWS):
        at = iota((1, 128 * tiles), 1) + 128 * tile
        masks.append(jnp.where((at >= ASIZE * i) & (at < ASIZE * (i + 1)), 1.0, 0.0).astype(BF16))
    return masks


def join_windows(parts):
    tiles = [None] * 7
    for (tile, count), part in zip(WINDOWS, parts):
        for k in range(count):
            piece = part[:, 128 * k : 128 * (k + 1)]
            tiles[tile + k] = piece if tiles[tile + k] is None else tiles[tile + k] + piece
    return jnp.concatenate(tiles, axis=1)


def pair_rows(tile):
    half = jnp.where(iota((1, 128), 1) < SIZE, 1.0, 0.0).astype(BF16)
    return jnp.concatenate([tile * half, tile * (1 - half)], axis=0)


def main_kernel(
    x_ref,
    raw_ref,
    in_ref,
    out_map_ref,
    rate_ref,
    bias_ref,
    skip_ref,
    gain_ref,
    lengths_ref,
    moved_ref,
    q_ref,
    k_ref,
    grad_ref,
    back_ref,
    start_ref,
    attn_ref,
    packed_ref,
    gq_ref,
    gk_ref,
    dx_ref,
    message_ref,
    flow_ref,
    direct_ref,
    gout_ref,
    gin_ref,
    gain_sum_ref,
    skip_sum_ref,
    y_ref,
    decay_ref,
    probs_ref,
    gv_ref,
    home_ref,
    column_ref,
    row_ref,
):
    block = lax.axis_index("ctx")
    scale = 1.0 / math.sqrt(ASIZE)
    square = (TOK, TOK)
    seg_q = jnp.zeros(square, jnp.int32)
    seg_k = jnp.zeros(square, jnp.int32)
    slot_q = jnp.full(square, -1, jnp.int32)
    slot_k = jnp.full((SEND, TOK), -1, jnp.int32)
    kept = jnp.ones(square, F32)
    at_q, at_k = iota(square, 0), iota(square, 1)
    at_s = iota((SEND, TOK), 1)
    begin, sent = jnp.int32(0), jnp.int32(0)
    for d in range(8):
        length, moved = lengths_ref[0, block, d], moved_ref[0, block, d]
        end = begin + length
        seg_q += jnp.where(at_q >= end, 1, 0)
        seg_k += jnp.where(at_k >= end, 1, 0)
        limit = jnp.where(moved == 1, end, begin)
        in_q = (at_q >= begin) & (at_q < limit)
        in_s = (at_s >= begin) & (at_s < limit)
        slot_q = jnp.where(in_q, at_q + (sent - begin), slot_q)
        slot_k = jnp.where(in_s, at_s + (sent - begin), slot_k)
        kept = jnp.where(in_q, 0.0, kept)
        sent = sent + (limit - begin)
        begin = end
    allowed = (seg_q == seg_k) & (at_k <= at_q)
    pick = jnp.where(slot_k == iota((SEND, TOK), 0), 1.0, 0.0).astype(BF16)
    place = jnp.where(slot_q == at_k, 1.0, 0.0).astype(BF16)[:, :SEND]
    kept = kept.astype(BF16)[:, :1]
    masks = lane_masks()

    rate, bias, skip = columns(rate_ref[...], bias_ref[...], skip_ref[...])
    _, step, _, running = decay_sums(raw_ref[...], bias, rate)
    grown = stacked_parts(jnp.exp(running))
    skips = stacked_parts(jnp.broadcast_to(skip, (SIZE, TOK)))[:16]
    row_ref[...] = running - jnp.log(step)
    column = jnp.transpose(jnp.concatenate([running, running], axis=0))
    for g in range(GROUPS):
        column_ref[g] = pltpu.roll(column, 128 - 16 * g, 1) if g else column
    in_rows, out_rows = in_ref[...], out_map_ref[...]
    gram = jnp.where(at_q >= at_k, dot(out_rows, in_rows, NT), 0.0)

    def forward(g, sums):
        power, along = sums
        at = lanes(g)
        x = x_ref[:, at]
        grad = grad_ref[0:TOK, at] * kept + dot(place, back_ref[:, at]).astype(BF16)
        home_ref[:, at] = grad
        q, k = q_ref[:, at], k_ref[:, at]
        parts = []
        for i, (tile, count) in enumerate(WINDOWS):
            window = slice(128 * tile, 128 * (tile + count))
            scores = dot(q[:, window] * masks[i], k[:, window], NT) * scale
            scores = jnp.where(allowed, scores, MASKED)
            weights = jnp.exp(scores - jnp.max(scores, axis=-1, keepdims=True))
            probs = weights * (1.0 / jnp.sum(weights, axis=-1, keepdims=True))
            probs_ref[AH * g + i] = probs
            parts.append(dot(probs.astype(BF16), grad[:, window] * masks[i], TN))
        gv = join_windows(parts).astype(BF16)
        gv_ref[:, at] = gv
        wide = expander(g)
        y = dot(out_rows, start_ref[rows64(g), :]) * dot(grown, wide)
        y = y + dot(skips, wide)[:1] * x.astype(F32)
        heads = row_ref[pl.ds(pl.multiple_of(16 * g, 16), 16), :]
        column = column_ref[g]
        inner = []
        for i in range(GH // 2):
            mixing = []
            for h in (2 * i, 2 * i + 1):
                decay = jnp.exp(jnp.minimum(column[:, h : h + 1] - heads[h : h + 1], 20.0))
                decay_ref[GH * g + h] = decay
                mixing.append((decay * gram).astype(BF16))
            pair = pair_rows(x[:, 128 * i : 128 * (i + 1)])
            inner.append(dot(jnp.concatenate(mixing, axis=1), pair))
        y = y + jnp.concatenate(inner, axis=1)
        y_ref[:, at] = y
        scaled = gv.astype(F32) * gain_ref[:, at]
        power = power + jnp.sum(y * y, axis=-1, keepdims=True)
        along = along + jnp.sum(scaled * y, axis=-1, keepdims=True)
        return power, along

    zero = jnp.zeros((TOK, 1), F32)
    power, along = lax.fori_loop(0, GROUPS, forward, (zero, zero))
    inverse = lax.rsqrt(power * (1.0 / WIDTH) + EPSILON)
    slope = inverse * inverse * inverse * along * (1.0 / WIDTH)

    gout_ref[...] = jnp.zeros_like(gout_ref)
    flow_ref[...] = jnp.zeros_like(flow_ref)
    direct_ref[...] = jnp.zeros_like(direct_ref)
    turned = jnp.transpose(out_rows.astype(F32)).astype(BF16)

    def backward(g, carry):
        gram_grad, skip_sum = carry
        at = lanes(g)
        x, y = x_ref[:, at], y_ref[:, at]
        gain = gain_ref[:, at]
        gv = gv_ref[:, at].astype(F32)
        normed = y * inverse
        values = (normed * gain).astype(BF16)
        gain_sum_ref[:, at] = jnp.sum(gv * normed, axis=0, keepdims=True)
        mixed_grad = gv * gain * inverse - y * slope
        low_grad = mixed_grad.astype(BF16)
        q, k, grad = q_ref[:, at], k_ref[:, at], home_ref[:, at]
        outs, gqs, gks = [], [], []
        for i, (tile, count) in enumerate(WINDOWS):
            window = slice(128 * tile, 128 * (tile + count))
            probs = probs_ref[AH * g + i]
            vals = values[:, window] * masks[i]
            outs.append(dot(probs.astype(BF16), vals))
            dprobs = dot(grad[:, window], vals, NT)
            delta = jnp.sum(probs * dprobs, axis=-1, keepdims=True)
            dscores = (probs * (dprobs - delta) * scale).astype(BF16)
            gqs.append(dot(dscores, k[:, window] * masks[i]))
            gks.append(dot(dscores, q[:, window] * masks[i], TN))
        head_out = join_windows(outs).astype(BF16)
        attn_ref[0:TOK, at] = head_out * kept
        packed_ref[:, at] = dot(pick, head_out).astype(BF16)
        gq_ref[:, at] = join_windows(gqs).astype(BF16)
        gk_ref[:, at] = join_windows(gks).astype(BF16)
        wide = expander(g)
        grown_grad = (dot(grown, wide) * mixed_grad).astype(BF16)
        message_ref[rows64(g), :] = dot(turned, grown_grad).astype(BF16)
        gout_ref[...] += dot(grown_grad, start_ref[rows64(g), :], NT)
        inner = []
        for i in range(GH // 2):
            tile = slice(128 * i, 128 * (i + 1))
            both = dot(low_grad[:, tile], pair_rows(x[:, tile]), NT)
            mixing = []
            for j in (0, 1):
                decay = decay_ref[GH * g + 2 * i + j]
                gram_grad = gram_grad + both[:, TOK * j : TOK * (j + 1)] * decay
                mixing.append((decay * gram).astype(BF16))
            inner.append(dot(jnp.concatenate(mixing, axis=0), pair_rows(low_grad[:, tile]), TN))
        inner = jnp.concatenate(inner, axis=1)
        wide_skip = dot(skips, wide)[:1]
        x = x.astype(F32)
        dx_ref[:, at] = inner + wide_skip * mixed_grad
        product = x * inner
        high, low = split(low_grad.astype(F32) * (y - wide_skip * x) - product)
        seg = expander(g)
        flow_ref[...] += dot(high, seg, NT) + dot(low, seg, NT)
        high, low = split(product)
        direct_ref[...] += dot(high, seg, NT) + dot(low, seg, NT)
        high, low = split(jnp.broadcast_to(jnp.sum(mixed_grad * x, axis=0, keepdims=True), (16, GW)))
        skip_sum = skip_sum + dot(high, seg, NT) + dot(low, seg, NT)
        return gram_grad, skip_sum

    gram_grad, skip_sum = lax.fori_loop(
        0, GROUPS, backward, (jnp.zeros(square, F32), jnp.zeros((16, TOK), F32))
    )
    skip_sum_ref[...] = skip_sum[:1]
    gram_grad = jnp.where(at_q >= at_k, gram_grad, 0.0).astype(BF16)
    gout_ref[...] += dot(gram_grad, in_rows)
    gin_ref[...] = dot(gram_grad, out_rows, TN)


def late_kernel(
    x_ref,
    raw_ref,
    in_ref,
    rate_ref,
    bias_ref,
    start_ref,
    grad_ref,
    dx_ref,
    flow_ref,
    direct_ref,
    gin_ref,
    arrived_ref,
    attn_in_ref,
    gx_ref,
    gin_out_ref,
    step_ref,
    heads_ref,
    attn_ref,
    sem,
):
    del attn_in_ref
    copy = pltpu.make_async_copy(arrived_ref, attn_ref.at[pl.ds(TOK, SEND), :], sem)
    copy.start()
    rate, bias = columns(rate_ref[...], bias_ref[...])
    z, step, neg, running = decay_sums(raw_ref[...], bias, rate)
    last = running[:, TOK - 1 :]
    tail = stacked_parts(jnp.exp(last - running) * step)
    in_rows = in_ref[...]
    tail_sum = jnp.zeros((TOK, TOK), F32)
    overlap = jnp.zeros((16, TOK), F32)
    gin = gin_ref[...]
    for g in range(GROUPS):
        at = slice(g * GW, (g + 1) * GW)
        rows = slice(g * SIZE, (g + 1) * SIZE)
        grad = grad_ref[rows, :]
        wide = expander(g)
        weight = dot(tail, wide)
        x = x_ref[:, at].astype(F32)
        late = dot(in_rows, grad) * weight
        gx_ref[:, at] = (dx_ref[:, at] + late).astype(BF16)
        gin = gin + dot((x * weight).astype(BF16), grad, NT)
        high, low = split(x * late)
        tail_sum = tail_sum + dot(high, wide, NT) + dot(low, wide, NT)
        both = jnp.sum(start_ref[rows, :].astype(F32) * grad.astype(F32), axis=0, keepdims=True)
        high, low = split(jnp.broadcast_to(both, (16, GW)))
        overlap = overlap + dot(high, wide, NT) + dot(low, wide, NT)
    gin_out_ref[...] = gin.astype(BF16)
    tail_sum = jnp.transpose(tail_sum)[:SIZE]
    flow = jnp.transpose(flow_ref[...])[:SIZE]
    direct = jnp.transpose(direct_ref[...])[:SIZE]
    overlap = jnp.transpose(jnp.broadcast_to(overlap[:1], (TOK, TOK)))[:SIZE]
    tri = jnp.where(iota((TOK, TOK), 0) >= iota((TOK, TOK), 1), 1.0, 0.0)
    ahead = dot(flow - tail_sum, tri, precision=HIGH)
    ahead = ahead + jnp.sum(tail_sum, axis=1, keepdims=True) + jnp.exp(last) * overlap
    step_grad = (direct + tail_sum) / step + neg * ahead
    raw_grad = step_grad * (1.0 / (1.0 + jnp.exp(-z)))
    step_ref[...] = unpad_heads(raw_grad)
    rate_grad = jnp.sum(neg * step * ahead, axis=1, keepdims=True)
    bias_grad = jnp.sum(raw_grad, axis=1, keepdims=True)
    both = jnp.concatenate([rate_grad, bias_grad], axis=0)
    heads_ref[:, 0, :] = jnp.transpose(jnp.broadcast_to(both, (TOK, TOK)))
    copy.wait()


def vmem(count):
    return [pl.BlockSpec(memory_space=pltpu.VMEM)] * count


PARAMS = pltpu.CompilerParams(vmem_limit_bytes=56 * 1024 * 1024)


def shape(dims, dtype):
    return jax.ShapeDtypeStruct(dims, dtype)


def local(
    mamba_in,
    step_raw,
    state_in,
    state_out,
    log_rate,
    step_bias,
    skip_gain,
    norm_gain,
    doc_lengths,
    doc_moved,
    queries,
    attn_keys,
    attn_grad,
):
    x, raw, in_rows, out_rows = mamba_in[0], step_raw[0], state_in[0], state_out[0]
    rate, bias, skip = log_rate[None], step_bias[None], skip_gain[None]
    blocks = lax.axis_size("ctx")
    devices = blocks * lax.axis_size("dp")
    rows = 8 * blocks
    swap = [(i, i ^ (blocks // 2)) for i in range(blocks)]

    def exchange(value):
        value = value.reshape(blocks, 8, value.shape[1])
        value = lax.all_to_all(value, "ctx", 0, 0, tiled=True)
        return value.reshape(rows, value.shape[2])

    def scan(reverse, carry, total):
        return pl.pallas_call(
            functools.partial(scan_kernel, blocks, reverse),
            out_shape=shape((rows, GW), BF16),
            in_specs=vmem(2),
            out_specs=pl.BlockSpec(memory_space=pltpu.VMEM),
            scratch_shapes=[pltpu.VMEM((rows, GW), F32)],
            compiler_params=PARAMS,
        )(carry, total)

    back = lax.ppermute(attn_grad[0, TOK:], "ctx", swap)
    message = pl.pallas_call(
        states_kernel,
        out_shape=shape((rows, GW + 128), BF16),
        in_specs=vmem(5),
        out_specs=pl.BlockSpec(memory_space=pltpu.VMEM),
        compiler_params=PARAMS,
    )(x, raw, in_rows, rate, bias)
    gathered = exchange(message)
    start = exchange(scan(False, gathered, gathered))

    outs = pl.pallas_call(
        main_kernel,
        out_shape=(
            shape((TOK + SEND, WIDTH), BF16),
            shape((SEND, WIDTH), BF16),
            shape((TOK, WIDTH), BF16),
            shape((TOK, WIDTH), BF16),
            shape((TOK, WIDTH), F32),
            shape((rows, GW), BF16),
            shape((TOK, TOK), F32),
            shape((TOK, TOK), F32),
            shape((TOK, SIZE), F32),
            shape((TOK, SIZE), F32),
            shape((1, WIDTH), F32),
            shape((1, TOK), F32),
        ),
        in_specs=vmem(8) + [pl.BlockSpec(memory_space=pltpu.SMEM)] * 2 + vmem(5),
        out_specs=tuple(vmem(12)),
        scratch_shapes=[
            pltpu.VMEM((TOK, WIDTH), F32),
            pltpu.VMEM((HEADS, TOK, TOK), F32),
            pltpu.VMEM((GROUPS * AH, TOK, TOK), F32),
            pltpu.VMEM((TOK, WIDTH), BF16),
            pltpu.VMEM((TOK, WIDTH), BF16),
            pltpu.VMEM((GROUPS, TOK, TOK), F32),
            pltpu.VMEM((SIZE, TOK), F32),
        ],
        compiler_params=PARAMS,
    )(
        x,
        raw,
        in_rows,
        out_rows,
        rate,
        bias,
        skip,
        norm_gain[None],
        doc_lengths,
        doc_moved,
        queries[0],
        attn_keys[0],
        attn_grad[0],
        back,
        start,
    )
    attn, packed, gq, gk, dx, message, flow, direct, gout, gin, gain_part, skip_part = outs
    arrived = lax.ppermute(packed, "ctx", swap)
    gain_sum, skip_sum = lax.psum((gain_part[0], skip_part[0]), ("dp", "ctx"))
    state_grad = exchange(scan(True, exchange(message), gathered))

    hbm = pl.BlockSpec(memory_space=pl.ANY)
    gx, gin, gstep, heads, attn = pl.pallas_call(
        late_kernel,
        out_shape=(
            shape((TOK, WIDTH), BF16),
            shape((TOK, SIZE), BF16),
            shape((HEADS, TOK), F32),
            shape((devices, 1, TOK), F32),
            shape((TOK + SEND, WIDTH), BF16),
        ),
        in_specs=vmem(11) + [hbm, hbm],
        out_specs=tuple(vmem(4)) + (hbm,),
        scratch_shapes=[pltpu.SemaphoreType.DMA],
        input_output_aliases={12: 4},
        compiler_params=PARAMS,
    )(x, raw, in_rows, rate, bias, start, state_grad, dx, flow, direct, gin, arrived, attn)
    heads = lax.all_to_all(heads, ("dp", "ctx"), 0, 0, tiled=True)
    heads = jnp.sum(heads, axis=(0, 1))
    head_sum = jnp.concatenate([heads.reshape(2, SIZE), skip_sum[None, :SIZE]], axis=0)
    head_sum = head_sum.reshape(3, GROUPS, 16)[:, :, :GH].reshape(3, HEADS)
    return (
        attn[None],
        gq[None],
        gk[None],
        gx[None],
        gin[None],
        gout.astype(BF16)[None],
        gstep[None],
        head_sum,
        gain_sum,
    )


def solution(mesh):
    in_specs = (
        P("dp", "ctx", None),
        P("dp", None, "ctx"),
        P("dp", "ctx", None),
        P("dp", "ctx", None),
        P(),
        P(),
        P(),
        P(),
        P("dp", None, None),
        P("dp", None, None),
        P("dp", "ctx", None),
        P("dp", "ctx", None),
        P("dp", "ctx", None),
    )
    out_specs = (
        P("dp", "ctx", None),
        P("dp", "ctx", None),
        P("dp", "ctx", None),
        P("dp", "ctx", None),
        P("dp", "ctx", None),
        P("dp", "ctx", None),
        P("dp", None, "ctx"),
        P(),
        P(),
    )
    return jax.shard_map(local, mesh=mesh, in_specs=in_specs, out_specs=out_specs, check_vma=False)
```

time: 829 us -> 212 us (0.26); the launches traced: 819 us -> 211 us
  waiting for transfers between devices: 281 us -> 35 us
  other arithmetic: 199 us -> 0.2 us
  local copies, waits for them, and re-layouts: 115 us -> 11.3 us
  matrix products: 69.2 us -> 0 us
  blocking collectives: 131 us -> 67.4 us
  Pallas kernels: 0 us -> 51.5 us
  starting transfers between devices: 5.18 us -> 45.1 us
  between operations: 15.9 us -> 0.81 us
    all_gather x2 -> x0, waiting for transfers between devices: 251 us -> none  [carried_in(): everything = jax.tree.map(lambda part: lax.all_gather(part, axis), value)]
    select_n x69 -> x0, other arithmetic: 182 us -> none  [the longest x64 176 us: hop(): return jax.tree.map(lambda a, b: jnp.where(reached, a, b), new, before)]
    dot_general x20 -> x0, matrix products: 69.2 us -> none  [the longest x3 17.7 us: local_outputs(): inner = jnp.einsum('hts,shp->thp', mixing, x_heads, precision=HIGH)]
    unnamed x1 -> x0, blocking collectives: 66.1 us -> none
    pallas_call x0 -> x5, Pallas kernels: none -> 51.5 us  [the longest x1 25.4 us: local(): pl.pallas_call(main_kernel, out_shape=(shape((TOK + SEND, WIDTH), BF16),...]
    all_to_all x0 -> x5, starting transfers between devices: none -> 39.3 us  [the longest x4 32.8 us: exchange(): value = lax.all_to_all(value, 'ctx', 0, 0, tiled=True)]
    all_to_all x0 -> x5, waiting for transfers between devices: none -> 35 us  [the longest x4 35 us: exchange(): value = lax.all_to_all(value, 'ctx', 0, 0, tiled=True)]
    slice x14 -> x0, local copies, waits for them, and re-layouts: 31.2 us -> none  [the longest x2 14.4 us: local(): grad_key = jnp.where(kept_rows, layout_key_grad[:tokens], unpacked[1])]
  transfers between devices with their start and end apart: 4 -> 7, of which waited for: 4 -> 4; matrix products, arithmetic and copies ran while one was open for 9% -> 3% of each run, Pallas kernels for 0% -> 2%
where the time goes in v1:
time: 212 us; the launch traced here: 211 us
  blocking collectives  67.4 us (32%)
  Pallas kernels  51.5 us (24%)
  starting transfers between devices  45.1 us (21%)
  waiting for transfers between devices  35 us (17%)
  local copies, waits for them, and re-layouts  11.3 us (5%)
    psum x1, blocking collectives, local(): gain_sum, skip_sum = lax.psum((gain_part[0], skip_part[0]), ('dp', 'ctx'))  67.4 us
    all_to_all x4, waiting for transfers between devices, exchange(): value = lax.all_to_all(value, 'ctx', 0, 0, tiled=True)  35 us
    all_to_all x4, starting transfers between devices, exchange(): value = lax.all_to_all(value, 'ctx', 0, 0, tiled=True)  32.8 us
    pallas_call x1, Pallas kernels, local(): pl.pallas_call(main_kernel, out_shape=(shape((TOK + SEND, WIDTH), BF16),...  25.4 us
    pallas_call x1, Pallas kernels, local(): pl.pallas_call(late_kernel, out_shape=(shape((TOK, WIDTH), BF16), shape((...  18 us
    unnamed x32, local copies, waits for them, and re-layouts  8.75 us
    all_to_all x1, starting transfers between devices, local(): heads = lax.all_to_all(heads, ('dp', 'ctx'), 0, 0, tiled=True)  6.52 us
    pallas_call x2, Pallas kernels, scan(): pl.pallas_call(functools.partial(scan_kernel, blocks, reverse), out_shape...  4.62 us
  transfers between devices with their start and end apart: 7, of which 4 were waited for; matrix products, arithmetic and copies ran while one was open for 3% of the time, Pallas kernels for 2%

profile of v1, /device:TPU:1, one launch (start us, length us, event | category | flops | bytes accessed | tf_op | source)
XLA Modules:
  0.0 211.3 jit_solution(16409067236477628278)
XLA Ops:
  0.6 1.4 copy.23
  2.1 3.5 %shard_map.196 = bf16[256,1024]{1,0:T(8,128)(2,1)} custom-call(bf16[128,3584]{1,0:T(8,128)(2,1)} %bitcast.33, f32[56,128]{1,0:T(8,128)} %bitcast.51, bf16[128,64]{1,0:T(8,128)(2,1)} %bitcast.47, f32[1,56]{1,0:T(1,128)} %bitcast.56, f32[1,56]{1,0:T(1,128)} %bitcast.59), custom_call_target="tpu_custom_call" | custom-call | tf_op jit(solution)/shard_map/pallas_call | solution.py:453
  5.6 8.6 %all-to-all-start = ((bf16[32,8,1024]{2,1,0:T(8,128)(2,1)}), bf16[32,8,1024]{2,1,0:T(8,128)(2,1)S(1)}, u32[]{:S(2)}, u32[]{:S(2)}) async-start(bf16[32,8,1024]{2,1,0:T(8,128)(2,1)} %bitcast.39), calls=%async_computation | async-start | bytes 1048576 | tf_op jit(solution)/shard_map/all_to_all | solution.py:439
  14.2 1.1 slice_bitcast_fusion
  15.2 0.0 copy-start.8
  15.3 0.0 copy-start.10
  15.3 0.0 copy-start.11
  15.3 0.0 copy-start.7
  15.3 3.0 %collective-permute-start = (bf16[64,3584]{1,0:T(8,128)(2,1)S(1)}, bf16[64,3584]{1,0:T(8,128)(2,1)S(1)}, u32[]{:S(2)}, u32[]{:S(2)}) collective-permute-start(bf16[64,3584]{1,0:T(8,128)(2,1)S(1)} %slice_bitcast_fusion), channel_id=1, source_target_pairs={{0,16},{1,17},{2,18},{3,19},{4,20},{5,21},{6,22},{7,23},{8,24},{9,... | collective-permute-start | bytes 1376264 | tf_op jit(solution)/shard_map/ppermute | solution.py:452
  18.3 7.7 %all-to-all-done = bf16[32,8,1024]{2,1,0:T(8,128)(2,1)S(1)} async-done(((bf16[32,8,1024]{2,1,0:T(8,128)(2,1)}), bf16[32,8,1024]{2,1,0:T(8,128)(2,1)S(1)}, u32[]{:S(2)}, u32[]{:S(2)}) %all-to-all-start) | async-done | bytes 524320 | tf_op jit(solution)/shard_map/all_to_all | solution.py:439
  25.9 0.0 copy-start
  25.9 0.8 copy-done
  26.7 2.3 %shard_map.197 = bf16[256,896]{1,0:T(8,128)(2,1)} custom-call(bf16[256,1024]{1,0:T(8,128)(2,1)} %bitcast.30, bf16[256,1024]{1,0:T(8,128)(2,1)} %bitcast.31), custom_call_target="tpu_custom_call" | custom-call | tf_op jit(solution)/shard_map/pallas_call | solution.py:443
  29.0 10.3 %all-to-all-start.1 = ((bf16[32,8,896]{2,1,0:T(8,128)(2,1)}), bf16[32,8,896]{2,1,0:T(8,128)(2,1)S(1)}, u32[]{:S(2)}, u32[]{:S(2)}) async-start(bf16[32,8,896]{2,1,0:T(8,128)(2,1)} %bitcast.41), calls=%async_computation.1 | async-start | bytes 917504 | tf_op jit(solution)/shard_map/all_to_all | solution.py:439
  39.4 0.0 copy-done.8
  39.4 0.6 broadcast_in_dim.37.gain_ref
  40.0 0.0 copy-done.10
  40.0 0.7 copy.25.lengths_ref
  40.7 0.0 copy-done.11
  40.7 0.7 copy.26.moved_ref
  41.3 0.0 copy-done.7
  41.3 0.7 copy.24
  42.1 0.0 collective-permute-done.back_ref
  42.1 0.0 copy-start.4
  42.1 8.3 %all-to-all-done.1 = bf16[32,8,896]{2,1,0:T(8,128)(2,1)S(1)} async-done(((bf16[32,8,896]{2,1,0:T(8,128)(2,1)}), bf16[32,8,896]{2,1,0:T(8,128)(2,1)S(1)}, u32[]{:S(2)}, u32[]{:S(2)}) %all-to-all-start.1) | async-done | bytes 458784 | tf_op jit(solution)/shard_map/all_to_all | solution.py:439
  50.3 0.0 copy-start.1
  50.3 0.0 copy-done.4
  50.3 0.8 copy-done.1
  51.1 25.4 %shard_map.198 = (bf16[192,3584]{1,0:T(8,128)(2,1)}, bf16[64,3584]{1,0:T(8,128)(2,1)}, bf16[128,3584]{1,0:T(8,128)(2,1)}, bf16[128,3584]{1,0:T(8,128)(2,1)}, f32...) custom-call(bf16[128,3584]{1,0:T(8,128)(2,1)} %bitcast.34, ...), custom_call_target="tpu_custom_call" | custom-call | tf_op jit(solution)/shard_map/pallas_call | solution.py:463
  76.4 3.7 %all-to-all-start.2 = ((bf16[32,8,896]{2,1,0:T(8,128)(2,1)}), bf16[32,8,896]{2,1,0:T(8,128)(2,1)S(1)}, u32[]{:S(2)}, u32[]{:S(2)}) async-start(bf16[32,8,896]{2,1,0:T(8,128)(2,1)} %bitcast.50), calls=%async_computation.2 | async-start | bytes 917504 | tf_op jit(solution)/shard_map/all_to_all | solution.py:439
  80.1 2.9 %collective-permute-start.1 = (bf16[64,3584]{1,0:T(8,128)(2,1)}, bf16[64,3584]{1,0:T(8,128)(2,1)S(1)}, u32[]{:S(2)}, u32[]{:S(2)}) collective-permute-start(bf16[64,3584]{1,0:T(8,128)(2,1)} %get-tuple-element.31), channel_id=1, source_target_pairs={{0,16},{1,17},{2,18},{3,19},{4,20},{5,21},{6,22},{7,23},{8,24},{9,... | collective-permute-start | bytes 1376264 | tf_op jit(solution)/shard_map/ppermute | solution.py:509
  83.0 8.2 %all-to-all-done.2 = bf16[32,8,896]{2,1,0:T(8,128)(2,1)S(1)} async-done(((bf16[32,8,896]{2,1,0:T(8,128)(2,1)}), bf16[32,8,896]{2,1,0:T(8,128)(2,1)S(1)}, u32[]{:S(2)}, u32[]{:S(2)}) %all-to-all-start.2) | async-done | bytes 458784 | tf_op jit(solution)/shard_map/all_to_all | solution.py:439
  91.2 0.0 copy-start.2
  91.2 0.8 copy-done.2
  91.9 2.3 %shard_map.199 = bf16[256,896]{1,0:T(8,128)(2,1)} custom-call(bf16[256,896]{1,0:T(8,128)(2,1)} %bitcast.40, bf16[256,1024]{1,0:T(8,128)(2,1)} %bitcast.32), custom_call_target="tpu_custom_call" | custom-call | tf_op jit(solution)/shard_map/pallas_call | solution.py:443
  94.2 10.2 %all-to-all-start.3 = ((bf16[32,8,896]{2,1,0:T(8,128)(2,1)}), bf16[32,8,896]{2,1,0:T(8,128)(2,1)S(1)}, u32[]{:S(2)}, u32[]{:S(2)}) async-start(bf16[32,8,896]{2,1,0:T(8,128)(2,1)} %bitcast.42), calls=%async_computation.3 | async-start | bytes 917504 | tf_op jit(solution)/shard_map/all_to_all | solution.py:439
  104.4 0.0 collective-permute-done.1.arrived_ref
  104.4 0.0 copy-start.5
  104.4 10.9 %all-to-all-done.3 = bf16[32,8,896]{2,1,0:T(8,128)(2,1)S(1)} async-done(((bf16[32,8,896]{2,1,0:T(8,128)(2,1)}), bf16[32,8,896]{2,1,0:T(8,128)(2,1)S(1)}, u32[]{:S(2)}, u32[]{:S(2)}) %all-to-all-start.3) | async-done | bytes 458784 | tf_op jit(solution)/shard_map/all_to_all | solution.py:439
  115.4 0.0 copy-start.3
  115.4 0.0 copy-done.5
  115.4 0.8 copy-done.3
  116.1 0.0 copy-start.6
  116.1 0.0 copy-start.9
  116.1 0.0 copy-start.12
  116.1 18.0 %shard_map.200 = (bf16[128,3584]{1,0:T(8,128)(2,1)}, bf16[128,64]{1,0:T(8,128)(2,1)}, f32[56,128]{1,0:T(8,128)}, f32[128,1,128]{2,1,0:T(1,128)}, bf16[192,3584]{1,0:T(8,128)(2,1)}) custom-call(bf16[128,3584]{1,0:T(8,128)(2,1)} %bitcast.35, f32[56,128]{1,0:T(8,128)} %bitcast.53, bf16[128,64]{1,0:T(8,128)(2,1)} %bitcast.49, ...), custom_call_target="tpu_custom_call", output_to_operand_aliasing={{4}: (12, {})} | custom-call | tf_op jit(solution)/shard_map/pallas_call | solution.py:514
  134.2 6.5 %all-to-all-start.4 = ((f32[128,1,128]{2,1,0:T(1,128)}), f32[128,1,128]{2,1,0:T(1,128)S(1)}, u32[]{:S(2)}, u32[]{:S(2)}) async-start(f32[128,1,128]{2,1,0:T(1,128)} %get-tuple-element.40), calls=%async_computation.4 | async-start | bytes 131072 | tf_op jit(solution)/shard_map/all_to_all | solution.py:529
  140.7 0.0 copy-done.6
  140.7 0.0 copy-done.9
  140.8 0.0 copy-done.12
  140.8 67.4 %all-reduce = (f32[128]{0:T(128)S(1)}, f32[3584]{0:T(1024)}) all-reduce(f32[128]{0:T(128)S(1)} %bitcast.63, f32[3584]{0:T(1024)S(1)} %reduce), channel_id=1, replica_groups=mesh['dp'=4,'ctx'=32] {'dp','ctx'}, use_global_device_ids=true, to_apply=%region_1.0 | all-reduce | flops 3712 | bytes 29696 | tf_op jit(solution)/shard_map/psum | solution.py:510
  208.2 0.1 concatenate.9
  208.2 0.7 copy.28
  208.9 1.4 copy.27
  210.4 0.0 all-to-all-done.4
  210.4 0.2 reduce_sum.9
  210.5 0.1 concatenate.8
  210.6 0.7 reshape.65
  (3 shorter events, 0.1 us)
Async XLA Ops:
  5.6 20.3 %all-to-all-start = ((bf16[32,8,1024]{2,1,0:T(8,128)(2,1)}), bf16[32,8,1024]{2,1,0:T(8,128)(2,1)S(1)}, u32[]{:S(2)}, u32[]{:S(2)}) async-start(bf16[32,8,1024]{2,1,0:T(8,128)(2,1)} %bitcast.39), calls=%async_computation | async-start | bytes 1048576 | tf_op jit(solution)/shard_map/all_to_all | solution.py:439
  15.2 24.1 %copy-start.8 = (f32[3584]{0:T(1024)S(1)}, f32[3584]{0:T(1024)}, u32[]{:S(2)}) copy-start(f32[3584]{0:T(1024)} %param.20) | copy-start | bytes 43012
  15.3 24.7 %copy-start.10 = (s32[1,32,8]{1,2,0:T(8,128)S(1)}, s32[1,32,8]{1,2,0:T(8,128)}, u32[]{:S(2)}) copy-start(s32[1,32,8]{1,2,0:T(8,128)} %param.21) | copy-start | bytes 3076
  15.3 25.4 %copy-start.11 = (s32[1,32,8]{1,2,0:T(8,128)S(1)}, s32[1,32,8]{1,2,0:T(8,128)}, u32[]{:S(2)}) copy-start(s32[1,32,8]{1,2,0:T(8,128)} %param.22) | copy-start | bytes 3076
  15.3 26.1 %copy-start.7 = (bf16[1,128,64]{1,2,0:T(8,128)(2,1)S(1)}, bf16[1,128,64]{1,2,0:T(8,128)(2,1)}, u32[]{:S(2)}) copy-start(bf16[1,128,64]{1,2,0:T(8,128)(2,1)} %param.16) | copy-start | bytes 49156
  15.3 26.8 %collective-permute-start = (bf16[64,3584]{1,0:T(8,128)(2,1)S(1)}, bf16[64,3584]{1,0:T(8,128)(2,1)S(1)}, u32[]{:S(2)}, u32[]{:S(2)}) collective-permute-start(bf16[64,3584]{1,0:T(8,128)(2,1)S(1)} %slice_bitcast_fusion), channel_id=1, source_target_pairs={{0,16},{1,17},{2,18},{3,19},{4,20},{5,21},{6,22},{7,23},{8,24},{9,... | collective-permute-start | bytes 1376264 | tf_op jit(solution)/shard_map/ppermute | solution.py:452
  25.9 0.8 copy-start
  29.0 21.3 %all-to-all-start.1 = ((bf16[32,8,896]{2,1,0:T(8,128)(2,1)}), bf16[32,8,896]{2,1,0:T(8,128)(2,1)S(1)}, u32[]{:S(2)}, u32[]{:S(2)}) async-start(bf16[32,8,896]{2,1,0:T(8,128)(2,1)} %bitcast.41), calls=%async_computation.1 | async-start | bytes 917504 | tf_op jit(solution)/shard_map/all_to_all | solution.py:439
  42.1 8.3 %copy-start.4 = (bf16[64,3584]{1,0:T(8,128)(2,1)}, bf16[64,3584]{1,0:T(8,128)(2,1)S(1)}, u32[]{:S(2)}) copy-start(bf16[64,3584]{1,0:T(8,128)(2,1)S(1)} %collective-permute-done.back_ref) | copy-start | bytes 1376260
  50.3 0.8 copy-start.1
  76.4 14.7 %all-to-all-start.2 = ((bf16[32,8,896]{2,1,0:T(8,128)(2,1)}), bf16[32,8,896]{2,1,0:T(8,128)(2,1)S(1)}, u32[]{:S(2)}, u32[]{:S(2)}) async-start(bf16[32,8,896]{2,1,0:T(8,128)(2,1)} %bitcast.50), calls=%async_computation.2 | async-start | bytes 917504 | tf_op jit(solution)/shard_map/all_to_all | solution.py:439
  80.1 24.3 %collective-permute-start.1 = (bf16[64,3584]{1,0:T(8,128)(2,1)}, bf16[64,3584]{1,0:T(8,128)(2,1)S(1)}, u32[]{:S(2)}, u32[]{:S(2)}) collective-permute-start(bf16[64,3584]{1,0:T(8,128)(2,1)} %get-tuple-element.31), channel_id=1, source_target_pairs={{0,16},{1,17},{2,18},{3,19},{4,20},{5,21},{6,22},{7,23},{8,24},{9,... | collective-permute-start | bytes 1376264 | tf_op jit(solution)/shard_map/ppermute | solution.py:509
  91.2 0.8 copy-start.2
  94.2 21.2 %all-to-all-start.3 = ((bf16[32,8,896]{2,1,0:T(8,128)(2,1)}), bf16[32,8,896]{2,1,0:T(8,128)(2,1)S(1)}, u32[]{:S(2)}, u32[]{:S(2)}) async-start(bf16[32,8,896]{2,1,0:T(8,128)(2,1)} %bitcast.42), calls=%async_computation.3 | async-start | bytes 917504 | tf_op jit(solution)/shard_map/all_to_all | solution.py:439
  104.4 11.0 %copy-start.5 = (bf16[64,3584]{1,0:T(8,128)(2,1)}, bf16[64,3584]{1,0:T(8,128)(2,1)S(1)}, u32[]{:S(2)}) copy-start(bf16[64,3584]{1,0:T(8,128)(2,1)S(1)} %collective-permute-done.1.arrived_ref) | copy-start | bytes 1376260
  115.4 0.8 copy-start.3
  116.1 24.6 %copy-start.6 = (f32[128,64]{1,0:T(8,128)S(1)}, f32[128,64]{1,0:T(8,128)}, u32[]{:S(2)}) copy-start(f32[128,64]{1,0:T(8,128)} %get-tuple-element.38) | copy-start | bytes 98308
  116.1 24.6 %copy-start.9 = (f32[1,3584]{1,0:T(1,128)S(1)}, f32[1,3584]{1,0:T(1,128)}, u32[]{:S(2)}) copy-start(f32[1,3584]{1,0:T(1,128)} %get-tuple-element.42) | copy-start | bytes 43012
  116.1 24.6 %copy-start.12 = (f32[1,128]{1,0:T(1,128)S(1)}, f32[1,128]{1,0:T(1,128)}, u32[]{:S(2)}) copy-start(f32[1,128]{1,0:T(1,128)} %get-tuple-element.41) | copy-start | bytes 1540
  134.2 76.2 %all-to-all-start.4 = ((f32[128,1,128]{2,1,0:T(1,128)}), f32[128,1,128]{2,1,0:T(1,128)S(1)}, u32[]{:S(2)}, u32[]{:S(2)}) async-start(f32[128,1,128]{2,1,0:T(1,128)} %get-tuple-element.40), calls=%async_computation.4 | async-start | bytes 131072 | tf_op jit(solution)/shard_map/all_to_all | solution.py:529

commit v2 on v1

v2 whole, which is shorter than its diff:
```python
import functools
import math

import jax
import jax.numpy as jnp
from jax import lax
from jax.experimental import pallas as pl
from jax.experimental.pallas import tpu as pltpu
from jax.sharding import PartitionSpec as P

F32 = jnp.float32
BF16 = jnp.bfloat16
HIGH = lax.Precision.HIGHEST
EPSILON = 1e-05
MASKED = -1e30

TOK = 128
HEADS = 56
SIZE = 64
GROUPS = 4
GW = 896
GH = 14
AH = 4
ASIZE = 224
WIDTH = GROUPS * GW
SEND = 64
WINDOWS = ((0, 2), (1, 3), (3, 3), (5, 2))

NT = (((1,), (1,)), ((), ()))
TN = (((0,), (0,)), ((), ()))


def dot(a, b, dims=(((1,), (0,)), ((), ())), precision=None):
    return lax.dot_general(a, b, dims, precision=precision, preferred_element_type=F32)


def iota(shape, dim):
    return lax.broadcasted_iota(jnp.int32, shape, dim)


def pad_heads(rows):
    gap = jnp.zeros((2, rows.shape[1]), rows.dtype)
    parts = []
    for g in range(GROUPS):
        parts += [rows[g * GH : (g + 1) * GH], gap]
    return jnp.concatenate(parts, axis=0)


def unpad_heads(rows):
    return jnp.concatenate([rows[16 * g : 16 * g + GH] for g in range(GROUPS)], axis=0)


def columns(*rows):
    stack = jnp.concatenate(list(rows) + [jnp.zeros((8 - len(rows), HEADS), F32)], axis=0)
    stack = jnp.concatenate([stack, jnp.zeros((8, 128 - HEADS), F32)], axis=1)
    turned = pad_heads(jnp.transpose(stack)[:HEADS])
    return [turned[:, i : i + 1] for i in range(len(rows))]


def expander(group, parts=2):
    shape = (64 * parts, GW)
    return jnp.where(
        (iota(shape, 0) & 63) == (iota(shape, 1) >> 6) + 16 * group, 1.0, 0.0
    ).astype(BF16)


def split(value):
    high = value.astype(BF16)
    low = (value - high.astype(F32)).astype(BF16)
    return high, low


def stacked_parts(value):
    high, low = split(value)
    return jnp.transpose(jnp.concatenate([high.astype(F32), low.astype(F32)], axis=0)).astype(BF16)


def decay_sums(raw, bias, rate):
    z = pad_heads(raw) + bias
    step = jnp.maximum(z, 0.0) + jnp.log1p(jnp.exp(-jnp.abs(z)))
    neg = -jnp.exp(rate)
    tri = jnp.where(iota((TOK, TOK), 0) <= iota((TOK, TOK), 1), 1.0, 0.0)
    running = dot(neg * step, tri, precision=HIGH)
    return z, step, neg, running


def lanes(g):
    return pl.ds(pl.multiple_of(g * GW, 128), GW)


def rows64(g):
    return pl.ds(pl.multiple_of(g * SIZE, SIZE), SIZE)


def states_kernel(x_ref, raw_ref, in_ref, rate_ref, bias_ref, out_ref):
    rate, bias = columns(rate_ref[...], bias_ref[...])
    _, step, _, running = decay_sums(raw_ref[...], bias, rate)
    last = running[:, TOK - 1 :]
    tail = stacked_parts(jnp.exp(last - running) * step)
    total = stacked_parts(jnp.broadcast_to(jnp.exp(last), running.shape))[:SIZE]
    in_map = in_ref[...]
    for g in range(GROUPS):
        wide = dot(tail, expander(g))
        scaled = (x_ref[:, g * GW : (g + 1) * GW].astype(F32) * wide).astype(BF16)
        out_ref[g * SIZE : (g + 1) * SIZE, :GW] = dot(in_map, scaled).astype(BF16)
        out_ref[g * SIZE : (g + 1) * SIZE, GW:] = total


def scan_kernel(blocks, reverse, *refs):
    if reverse:
        carry_ref, total_ref, out_ref, sum_ref, wide_ref = refs
        ones = jnp.ones((16, 8 * blocks), BF16)
        sum_ref[...] = dot(ones, carry_ref[:, GW:])[:1]
    else:
        carry_ref, out_ref, wide_ref = refs
        total_ref = carry_ref
    group = lax.axis_index("ctx") // 8
    wide_ref[...] = dot(total_ref[:, GW:], expander(group))
    state = jnp.zeros((8, GW), F32)
    pairs = range(blocks // 2)
    for i in reversed(pairs) if reverse else pairs:
        rows = slice(16 * i, 16 * i + 16)
        carry = carry_ref[rows, :GW].astype(F32)
        first = state
        at = slice(8, 16) if reverse else slice(0, 8)
        second = wide_ref[rows][at] * first + carry[at]
        at = slice(0, 8) if reverse else slice(8, 16)
        state = wide_ref[rows][at] * second + carry[at]
        both = [second, first] if reverse else [first, second]
        out_ref[rows, :] = jnp.concatenate(both, axis=0).astype(BF16)


def lane_masks():
    masks = []
    for i, (tile, tiles) in enumerate(WINDOWS):
        at = iota((1, 128 * tiles), 1) + 128 * tile
        masks.append(jnp.where((at >= ASIZE * i) & (at < ASIZE * (i + 1)), 1.0, 0.0).astype(BF16))
    return masks


def join_windows(parts):
    tiles = [None] * 7
    for (tile, count), part in zip(WINDOWS, parts):
        for k in range(count):
            piece = part[:, 128 * k : 128 * (k + 1)]
            tiles[tile + k] = piece if tiles[tile + k] is None else tiles[tile + k] + piece
    return jnp.concatenate(tiles, axis=1)


def pair_rows(tile):
    half = jnp.where(iota((1, 128), 1) < SIZE, 1.0, 0.0).astype(BF16)
    return jnp.concatenate([tile * half, tile * (1 - half)], axis=0)


def documents(lengths_ref, moved_ref):
    block = lax.axis_index("ctx")
    begin, sent, docs = jnp.int32(0), jnp.int32(0), []
    for d in range(8):
        length, moved = lengths_ref[d, block], moved_ref[d, block]
        end = begin + length
        limit = jnp.where(moved == 1, end, begin)
        docs.append((begin, end, limit, sent))
        sent = sent + (limit - begin)
        begin = end
    return docs


def place_slots(docs, dims, dim):
    at = iota(dims, dim)
    slots = jnp.full(dims, -1, jnp.int32)
    for begin, _, limit, sent in docs:
        slots = jnp.where((at >= begin) & (at < limit), at + (sent - begin), slots)
    return slots


def columns_of(running):
    turned = jnp.transpose(jnp.concatenate([running, running], axis=0))
    return [turned] + [pltpu.roll(turned, TOK - 16 * g, 1) for g in range(1, GROUPS)]


def local_decay(column, heads, h):
    return jnp.exp(jnp.minimum(column[:, h : h + 1] - heads[h : h + 1], 20.0))


def inner_kernel(
    x_ref,
    raw_ref,
    in_ref,
    map_ref,
    rate_ref,
    bias_ref,
    skip_ref,
    lengths_ref,
    moved_ref,
    q_ref,
    k_ref,
    y_ref,
    probs_ref,
    column_ref,
    row_ref,
):
    scale = 1.0 / math.sqrt(ASIZE)
    square = (TOK, TOK)
    at_q, at_k = iota(square, 0), iota(square, 1)
    docs = documents(lengths_ref, moved_ref)
    seg_q = jnp.zeros(square, jnp.int32)
    seg_k = jnp.zeros(square, jnp.int32)
    for _, end, _, _ in docs:
        seg_q += jnp.where(at_q >= end, 1, 0)
        seg_k += jnp.where(at_k >= end, 1, 0)
    allowed = (seg_q == seg_k) & (at_k <= at_q)
    masks = lane_masks()
    rate, bias, skip = columns(rate_ref[...], bias_ref[...], skip_ref[...])
    _, step, _, running = decay_sums(raw_ref[...], bias, rate)
    skips = stacked_parts(jnp.broadcast_to(skip, (SIZE, TOK)))[:16]
    row_ref[...] = running - jnp.log(step)
    for g, column in enumerate(columns_of(running)):
        column_ref[g] = column
    gram = jnp.where(at_q >= at_k, dot(map_ref[...], in_ref[...], TN), 0.0)

    def group(g, carry):
        at = lanes(g)
        x, q, k = x_ref[:, at], q_ref[:, at], k_ref[:, at]
        for i, (tile, count) in enumerate(WINDOWS):
            window = slice(128 * tile, 128 * (tile + count))
            scores = dot(q[:, window] * masks[i], k[:, window], NT) * scale
            scores = jnp.where(allowed, scores, MASKED)
            weights = jnp.exp(scores - jnp.max(scores, axis=-1, keepdims=True))
            total = jnp.sum(weights, axis=-1, keepdims=True)
            probs_ref[AH * g + i] = weights * (1.0 / total)
        heads = row_ref[pl.ds(pl.multiple_of(16 * g, 16), 16), :]
        column = column_ref[g]
        inner = []
        for i in range(GH // 2):
            pair = [(local_decay(column, heads, h) * gram).astype(BF16) for h in (2 * i, 2 * i + 1)]
            rows = pair_rows(x[:, 128 * i : 128 * (i + 1)])
            inner.append(dot(jnp.concatenate(pair, axis=1), rows))
        y_ref[:, at] = jnp.concatenate(inner, axis=1) + dot(skips, expander(g))[:1] * x.astype(F32)
        return carry

    lax.fori_loop(0, GROUPS, group, 0)


def value_grad_kernel(lengths_ref, moved_ref, probs_ref, grad_ref, back_ref, gv_ref, home_ref):
    docs = documents(lengths_ref, moved_ref)
    slots = place_slots(docs, (TOK, TOK), 0)
    place = jnp.where(slots == iota((TOK, TOK), 1), 1.0, 0.0).astype(BF16)[:, :SEND]
    kept = jnp.where(slots < 0, 1.0, 0.0).astype(BF16)[:, :1]
    masks = lane_masks()

    def group(g, carry):
        at = lanes(g)
        grad = grad_ref[0:TOK, at] * kept + dot(place, back_ref[:, at]).astype(BF16)
        home_ref[:, at] = grad
        parts = []
        for i, (tile, count) in enumerate(WINDOWS):
            window = slice(128 * tile, 128 * (tile + count))
            parts.append(dot(probs_ref[AH * g + i].astype(BF16), grad[:, window] * masks[i], TN))
        gv_ref[:, at] = join_windows(parts).astype(BF16)
        return carry

    lax.fori_loop(0, GROUPS, group, 0)


def norm_kernel(
    raw_ref,
    map_ref,
    rate_ref,
    bias_ref,
    gain_ref,
    start_ref,
    inner_ref,
    gv_ref,
    y_ref,
    values_ref,
    low_ref,
    message_ref,
    wide_ref,
    sums_ref,
):
    rate, bias = columns(rate_ref[...], bias_ref[...])
    _, _, _, running = decay_sums(raw_ref[...], bias, rate)
    grown = stacked_parts(jnp.exp(running))
    map_in = map_ref[...]
    out_rows = jnp.transpose(map_in.astype(F32)).astype(BF16)
    power = jnp.zeros((TOK, 1), F32)
    along = jnp.zeros((TOK, 1), F32)
    for g in range(GROUPS):
        at = slice(g * GW, (g + 1) * GW)
        wide = dot(grown, expander(g))
        wide_ref[:, at] = wide
        y = inner_ref[:, at] + dot(out_rows, start_ref[g * SIZE : (g + 1) * SIZE, :]) * wide
        y_ref[:, at] = y
        power = power + jnp.sum(y * y, axis=-1, keepdims=True)
        scaled = gv_ref[:, at].astype(F32) * gain_ref[:, at]
        along = along + jnp.sum(scaled * y, axis=-1, keepdims=True)
    inverse = lax.rsqrt(power * (1.0 / WIDTH) + EPSILON)
    slope = inverse * inverse * inverse * along * (1.0 / WIDTH)
    sums_ref[...] = jnp.zeros_like(sums_ref)
    for g in range(GROUPS):
        at = slice(g * GW, (g + 1) * GW)
        rows = slice(g * SIZE, (g + 1) * SIZE)
        y, gain, gv = y_ref[:, at], gain_ref[:, at], gv_ref[:, at].astype(F32)
        normed = y * inverse
        values_ref[:, at] = (normed * gain).astype(BF16)
        gain_sum = jnp.sum(gv * normed, axis=0, keepdims=True)
        for i in range(7):
            sums_ref[7 * g + i : 7 * g + i + 1, :] = gain_sum[:, 128 * i : 128 * (i + 1)]
        mixed_grad = gv * gain * inverse - y * slope
        low_ref[:, at] = mixed_grad.astype(BF16)
        grown_grad = (wide_ref[:, at] * mixed_grad).astype(BF16)
        message_ref[rows, :GW] = dot(map_in, grown_grad).astype(BF16)
    sums = sums_ref[...]
    high, low = split(sums)
    lowest = (sums - high.astype(F32) - low.astype(F32)).astype(BF16)
    dims = (message_ref.shape[0], 96)
    at, source = iota(dims, 0), iota(dims, 1)
    spread = jnp.where((at >> 3 == source & 31) & (at & 7 == source >> 5), 1.0, 0.0).astype(BF16)
    message_ref[:, GW:] = dot(spread, jnp.concatenate([high, low, lowest], axis=0)).astype(BF16)


def attention_kernel(
    lengths_ref,
    moved_ref,
    q_ref,
    k_ref,
    values_ref,
    probs_ref,
    home_ref,
    attn_ref,
    packed_ref,
    gq_ref,
    gk_ref,
):
    scale = 1.0 / math.sqrt(ASIZE)
    docs = documents(lengths_ref, moved_ref)
    pick = place_slots(docs, (SEND, TOK), 1) == iota((SEND, TOK), 0)
    pick = jnp.where(pick, 1.0, 0.0).astype(BF16)
    kept = jnp.where(place_slots(docs, (TOK, TOK), 0) < 0, 1.0, 0.0).astype(BF16)[:, :1]
    masks = lane_masks()

    def group(g, carry):
        at = lanes(g)
        q, k, grad, values = q_ref[:, at], k_ref[:, at], home_ref[:, at], values_ref[:, at]
        outs, gqs, gks = [], [], []
        for i, (tile, count) in enumerate(WINDOWS):
            window = slice(128 * tile, 128 * (tile + count))
            probs = probs_ref[AH * g + i]
            vals = values[:, window] * masks[i]
            outs.append(dot(probs.astype(BF16), vals))
            dprobs = dot(grad[:, window], vals, NT)
            delta = jnp.sum(probs * dprobs, axis=-1, keepdims=True)
            dscores = (probs * (dprobs - delta) * scale).astype(BF16)
            gqs.append(dot(dscores, k[:, window] * masks[i]))
            gks.append(dot(dscores, q[:, window] * masks[i], TN))
        head_out = join_windows(outs).astype(BF16)
        attn_ref[0:TOK, at] = head_out * kept
        packed_ref[:, at] = dot(pick, head_out).astype(BF16)
        gq_ref[:, at] = join_windows(gqs).astype(BF16)
        gk_ref[:, at] = join_windows(gks).astype(BF16)
        return carry

    lax.fori_loop(0, GROUPS, group, 0)


def inner_back_kernel(
    x_ref,
    raw_ref,
    in_ref,
    map_ref,
    rate_ref,
    bias_ref,
    skip_ref,
    start_ref,
    y_ref,
    low_ref,
    dx_ref,
    flow_ref,
    direct_ref,
    gout_ref,
    gin_ref,
    skip_sum_ref,
    column_ref,
    row_ref,
    sum_ref,
):
    square = (TOK, TOK)
    causal = iota(square, 0) >= iota(square, 1)
    rate, bias, skip = columns(rate_ref[...], bias_ref[...], skip_ref[...])
    _, step, _, running = decay_sums(raw_ref[...], bias, rate)
    skips = stacked_parts(jnp.broadcast_to(skip, (SIZE, TOK)))[:16]
    grown = stacked_parts(jnp.exp(running))
    row_ref[...] = running - jnp.log(step)
    for g, column in enumerate(columns_of(running)):
        column_ref[g] = column
    in_map, map_in = in_ref[...], map_ref[...]
    gram = jnp.where(causal, dot(map_in, in_map, TN), 0.0)
    flow_ref[...] = jnp.zeros_like(flow_ref)
    direct_ref[...] = jnp.zeros_like(direct_ref)
    sum_ref[...] = jnp.zeros_like(sum_ref)

    def group(g, carry):
        gram_grad, skip_sum = carry
        at = lanes(g)
        x, low_grad = x_ref[:, at], low_ref[:, at]
        mixed_grad = low_grad.astype(F32)
        wide = expander(g)
        grown_grad = (dot(grown, wide) * mixed_grad).astype(BF16)
        sum_ref[...] += dot(start_ref[rows64(g), :], grown_grad, NT)
        heads = row_ref[pl.ds(pl.multiple_of(16 * g, 16), 16), :]
        column = column_ref[g]
        inner = []
        for i in range(GH // 2):
            tile = slice(128 * i, 128 * (i + 1))
            both = dot(low_grad[:, tile], pair_rows(x[:, tile]), NT)
            pair = []
            for j in (0, 1):
                decay = local_decay(column, heads, 2 * i + j)
                gram_grad = gram_grad + both[:, TOK * j : TOK * (j + 1)] * decay
                pair.append((decay * gram).astype(BF16))
            inner.append(dot(jnp.concatenate(pair, axis=0), pair_rows(low_grad[:, tile]), TN))
        inner = jnp.concatenate(inner, axis=1)
        wide_skip = dot(skips, wide)[:1]
        x = x.astype(F32)
        dx_ref[:, at] = inner + wide_skip * mixed_grad
        product = x * inner
        high, low = split(mixed_grad * (y_ref[:, at] - wide_skip * x) - product)
        flow_ref[...] += dot(high, wide, NT) + dot(low, wide, NT)
        high, low = split(product)
        direct_ref[...] += dot(high, wide, NT) + dot(low, wide, NT)
        high, low = split(jnp.broadcast_to(jnp.sum(mixed_grad * x, axis=0, keepdims=True), (16, GW)))
        skip_sum = skip_sum + dot(high, wide, NT) + dot(low, wide, NT)
        return gram_grad, skip_sum

    gram_grad, skip_sum = lax.fori_loop(
        0, GROUPS, group, (jnp.zeros(square, F32), jnp.zeros((16, TOK), F32))
    )
    skip_sum_ref[...] = skip_sum[:1]
    gram_grad = jnp.where(causal, gram_grad, 0.0).astype(BF16)
    gout_ref[...] = (sum_ref[...] + dot(in_map, gram_grad, NT)).astype(BF16)
    gin_ref[...] = dot(map_in, gram_grad)


def late_kernel(
    x_ref,
    raw_ref,
    in_ref,
    rate_ref,
    bias_ref,
    start_ref,
    grad_ref,
    dx_ref,
    flow_ref,
    direct_ref,
    gin_ref,
    skip_sum_ref,
    gain_sum_ref,
    gx_ref,
    gin_out_ref,
    step_ref,
    sums_ref,
):
    rate, bias = columns(rate_ref[...], bias_ref[...])
    z, step, neg, running = decay_sums(raw_ref[...], bias, rate)
    last = running[:, TOK - 1 :]
    tail = stacked_parts(jnp.exp(last - running) * step)
    in_rows = jnp.transpose(in_ref[...].astype(F32)).astype(BF16)
    tail_sum = jnp.zeros((TOK, TOK), F32)
    overlap = jnp.zeros((16, TOK), F32)
    gin = gin_ref[...]
    for g in range(GROUPS):
        at = slice(g * GW, (g + 1) * GW)
        rows = slice(g * SIZE, (g + 1) * SIZE)
        grad = grad_ref[rows, :]
        wide = expander(g)
        weight = dot(tail, wide)
        x = x_ref[:, at].astype(F32)
        late = dot(in_rows, grad) * weight
        gx_ref[:, at] = (dx_ref[:, at] + late).astype(BF16)
        gin = gin + dot(grad, (x * weight).astype(BF16), NT)
        high, low = split(x * late)
        tail_sum = tail_sum + dot(high, wide, NT) + dot(low, wide, NT)
        both = jnp.sum(start_ref[rows, :].astype(F32) * grad.astype(F32), axis=0, keepdims=True)
        high, low = split(jnp.broadcast_to(both, (16, GW)))
        overlap = overlap + dot(high, wide, NT) + dot(low, wide, NT)
    gin_out_ref[...] = gin.astype(BF16)
    tail_sum = jnp.transpose(tail_sum)[:SIZE]
    flow = jnp.transpose(flow_ref[...])[:SIZE]
    direct = jnp.transpose(direct_ref[...])[:SIZE]
    overlap = jnp.transpose(jnp.broadcast_to(overlap[:1], (TOK, TOK)))[:SIZE]
    tri = jnp.where(iota((TOK, TOK), 0) >= iota((TOK, TOK), 1), 1.0, 0.0)
    ahead = dot(flow - tail_sum, tri, precision=HIGH)
    ahead = ahead + jnp.sum(tail_sum, axis=1, keepdims=True) + jnp.exp(last) * overlap
    step_grad = (direct + tail_sum) / step + neg * ahead
    raw_grad = step_grad * (1.0 / (1.0 + jnp.exp(-z)))
    step_ref[...] = unpad_heads(raw_grad)
    rate_grad = jnp.sum(neg * step * ahead, axis=1, keepdims=True)
    bias_grad = jnp.sum(raw_grad, axis=1, keepdims=True)
    both = jnp.concatenate([rate_grad, bias_grad], axis=0)
    devices = sums_ref.shape[0]
    sums_ref[:, 0, 0:TOK] = jnp.transpose(jnp.broadcast_to(both, (TOK, TOK)))[:devices]
    sums_ref[:, 0, TOK : 2 * TOK] = jnp.broadcast_to(skip_sum_ref[...], (devices, TOK))
    sums_ref[:, 0, 2 * TOK :] = jnp.broadcast_to(gain_sum_ref[...], (devices, TOK))


def last_kernel(blocks, sums_ref, heads_ref, gain_ref):
    total = jnp.sum(sums_ref[:, 0, : 2 * TOK], axis=0, keepdims=True)
    for row, at in enumerate((0, SIZE, TOK)):
        for g in range(GROUPS):
            piece = total[:, at + 16 * g : at + 16 * g + GH]
            heads_ref[row : row + 1, GH * g : GH * (g + 1)] = piece
    gains = sums_ref[:, 0, 2 * TOK :]
    parts = gains.shape[0] // blocks
    gains = sum(gains[blocks * d : blocks * (d + 1)] for d in range(parts))
    for i in range(WIDTH // TOK):
        gain_ref[:, TOK * i : TOK * (i + 1)] = gains[i : i + 1]


def shape(dims, dtype):
    return jax.ShapeDtypeStruct(dims, dtype)


MIB = 1024 * 1024
VMEM = pl.BlockSpec(memory_space=pltpu.VMEM)
SMEM = pl.BlockSpec(memory_space=pltpu.SMEM)


def call(kernel, outs, args, scratch=(), tables=(), mib=32, us=5):
    single = not isinstance(outs, tuple)
    return pl.pallas_call(
        kernel,
        out_shape=outs,
        in_specs=[SMEM if i in tables else VMEM for i in range(len(args))],
        out_specs=VMEM if single else (VMEM,) * len(outs),
        scratch_shapes=list(scratch),
        compiler_params=pltpu.CompilerParams(vmem_limit_bytes=mib * MIB),
        cost_estimate=pl.CostEstimate(flops=int(us * 1e9), bytes_accessed=8 * MIB, transcendentals=0),
    )(*args)


def local(
    mamba_in,
    step_raw,
    state_in,
    state_out,
    log_rate,
    step_bias,
    skip_gain,
    norm_gain,
    doc_lengths,
    doc_moved,
    queries,
    attn_keys,
    attn_grad,
):
    x, raw, q, k = mamba_in[0], step_raw[0], queries[0], attn_keys[0]
    in_map, map_in = jnp.transpose(state_in[0]), jnp.transpose(state_out[0])
    lengths, moved = jnp.transpose(doc_lengths[0]), jnp.transpose(doc_moved[0])
    rate, bias, skip = log_rate[None], step_bias[None], skip_gain[None]
    blocks = lax.axis_size("ctx")
    devices = blocks * lax.axis_size("dp")
    rows = 8 * blocks
    swap = [(i, i ^ (blocks // 2)) for i in range(blocks)]
    wide = (TOK, WIDTH)
    decay_scratch = [pltpu.VMEM((GROUPS, TOK, TOK), F32), pltpu.VMEM((SIZE, TOK), F32)]
    probs_shape = (GROUPS * AH, TOK, TOK)

    def exchange(value):
        value = value.reshape(blocks, 8, value.shape[1])
        value = lax.all_to_all(value, "ctx", 0, 0, tiled=True)
        return value.reshape(rows, value.shape[2])

    back = lax.ppermute(attn_grad[0, TOK:], "ctx", swap)
    message = call(
        states_kernel, shape((rows, GW + 128), BF16), (x, raw, in_map, rate, bias), mib=8
    )
    gathered = exchange(message)
    wide_scratch = [pltpu.VMEM((rows, GW), F32)]
    firsts = call(
        functools.partial(scan_kernel, blocks, False),
        shape((rows, GW), BF16),
        (gathered,),
        wide_scratch,
        mib=8,
        us=2,
    )
    start = exchange(firsts)
    inner, probs = call(
        inner_kernel,
        (shape(wide, F32), shape(probs_shape, F32)),
        (x, raw, in_map, map_in, rate, bias, skip, lengths, moved, q, k),
        decay_scratch,
        tables=(7, 8),
        us=8,
    )
    gv, home = call(
        value_grad_kernel,
        (shape(wide, BF16), shape(wide, BF16)),
        (lengths, moved, probs, attn_grad[0], back),
        tables=(0, 1),
        us=5,
    )
    y, values, low, message = call(
        norm_kernel,
        (shape(wide, F32), shape(wide, BF16), shape(wide, BF16), shape((rows, GW + 128), BF16)),
        (raw, map_in, rate, bias, norm_gain[None], start, inner, gv),
        [pltpu.VMEM(wide, F32), pltpu.VMEM((32, TOK), F32)],
        us=7,
    )
    attn, packed, gq, gk = call(
        attention_kernel,
        (shape((TOK + SEND, WIDTH), BF16), shape((SEND, WIDTH), BF16), shape(wide, BF16), shape(wide, BF16)),
        (lengths, moved, q, k, values, probs, home),
        tables=(0, 1),
        us=8,
    )
    arrived = lax.ppermute(packed, "ctx", swap)
    lasts, gain_sum = call(
        functools.partial(scan_kernel, blocks, True),
        (shape((rows, GW), BF16), shape((1, TOK), F32)),
        (exchange(message), gathered),
        wide_scratch,
        mib=8,
        us=2,
    )
    state_grad = exchange(lasts)
    dx, flow, direct, gout, gin, skip_sum = call(
        inner_back_kernel,
        (
            shape(wide, F32),
            shape((TOK, TOK), F32),
            shape((TOK, TOK), F32),
            shape((SIZE, TOK), BF16),
            shape((SIZE, TOK), F32),
            shape((1, TOK), F32),
        ),
        (x, raw, in_map, map_in, rate, bias, skip, start, y, low),
        decay_scratch + [pltpu.VMEM((SIZE, TOK), F32)],
        us=8,
    )
    gx, gin, gstep, sums = call(
        late_kernel,
        (
            shape(wide, BF16),
            shape((SIZE, TOK), BF16),
            shape((HEADS, TOK), F32),
            shape((devices, 1, 3 * TOK), F32),
        ),
        (x, raw, in_map, rate, bias, start, state_grad, dx, flow, direct, gin, skip_sum, gain_sum),
        us=6,
    )
    sums = lax.all_to_all(sums, ("dp", "ctx"), 0, 0, tiled=True)
    attn = lax.dynamic_update_slice(attn, arrived, (TOK, 0))
    heads, gain = call(
        functools.partial(last_kernel, blocks),
        (shape((3, HEADS), F32), shape((1, WIDTH), F32)),
        (sums,),
        mib=4,
        us=1,
    )
    return (
        attn[None],
        gq[None],
        gk[None],
        gx[None],
        jnp.transpose(gin)[None],
        jnp.transpose(gout)[None],
        gstep[None],
        heads,
        gain[0],
    )


def solution(mesh):
    in_specs = (
        P("dp", "ctx", None),
        P("dp", None, "ctx"),
        P("dp", "ctx", None),
        P("dp", "ctx", None),
        P(),
        P(),
        P(),
        P(),
        P("dp", None, None),
        P("dp", None, None),
        P("dp", "ctx", None),
        P("dp", "ctx", None),
        P("dp", "ctx", None),
    )
    out_specs = (
        P("dp", "ctx", None),
        P("dp", "ctx", None),
        P("dp", "ctx", None),
        P("dp", "ctx", None),
        P("dp", "ctx", None),
        P("dp", "ctx", None),
        P("dp", None, "ctx"),
        P(),
        P(),
    )
    return jax.shard_map(local, mesh=mesh, in_specs=in_specs, out_specs=out_specs, check_vma=False)
```

time: 212 us -> 120 us (0.57)
  blocking collectives: 67.4 us -> 0 us
  waiting for transfers between devices: 35 us -> 18.5 us
  local copies, waits for them, and re-layouts: 11.3 us -> 26.7 us
  Pallas kernels: 51.5 us -> 37.5 us
  starting transfers between devices: 45.1 us -> 34.8 us
    psum x1 -> x0, blocking collectives: 67.4 us -> none  [local(): gain_sum, skip_sum = lax.psum((gain_part[0], skip_part[0]), ('dp', 'ctx'))]
    all_to_all x4, waiting for transfers between devices: 35 us -> 9.75 us  [exchange(): value = lax.all_to_all(value, 'ctx', 0, 0, tiled=True)]
    unnamed x32 -> x76, local copies, waits for them, and re-layouts: 8.75 us -> 23 us
    pallas_call x5 -> x10, Pallas kernels: 51.5 us -> 37.5 us  [call(): pl.pallas_call(kernel, out_shape=outs, in_specs=[SMEM if i in tables else...]
    all_to_all x4, starting transfers between devices: 32.8 us -> 19.6 us  [exchange(): value = lax.all_to_all(value, 'ctx', 0, 0, tiled=True)]
    all_to_all x1, waiting for transfers between devices: 0.01 us -> 8.71 us  [local(): sums = lax.all_to_all(sums, ('dp', 'ctx'), 0, 0, tiled=True)]
    all_to_all x1, starting transfers between devices: 6.52 us -> 8.83 us  [local(): sums = lax.all_to_all(sums, ('dp', 'ctx'), 0, 0, tiled=True)]
  transfers between devices with their start and end apart: 7 -> 7, of which waited for: 4 -> 4; matrix products, arithmetic and copies ran while one was open for 3% -> 2% of each run, Pallas kernels for 2% -> 28%
where the time goes in v2:
time: 120 us; the launch traced here: 119 us
  Pallas kernels  37.5 us (31%)
  starting transfers between devices  34.8 us (29%)
  local copies, waits for them, and re-layouts  26.7 us (22%)
  waiting for transfers between devices  18.5 us (15%)
    pallas_call x10, Pallas kernels, call(): pl.pallas_call(kernel, out_shape=outs, in_specs=[SMEM if i in tables else...  37.5 us
    unnamed x76, local copies, waits for them, and re-layouts  23 us
    all_to_all x4, starting transfers between devices, exchange(): value = lax.all_to_all(value, 'ctx', 0, 0, tiled=True)  19.6 us
    all_to_all x4, waiting for transfers between devices, exchange(): value = lax.all_to_all(value, 'ctx', 0, 0, tiled=True)  9.75 us
    all_to_all x1, starting transfers between devices, local(): sums = lax.all_to_all(sums, ('dp', 'ctx'), 0, 0, tiled=True)  8.83 us
    all_to_all x1, waiting for transfers between devices, local(): sums = lax.all_to_all(sums, ('dp', 'ctx'), 0, 0, tiled=True)  8.71 us
    ppermute x1, starting transfers between devices, local(): back = lax.ppermute(attn_grad[0, TOK:], 'ctx', swap)  3.57 us
    ppermute x1, starting transfers between devices, local(): arrived = lax.ppermute(packed, 'ctx', swap)  2.81 us
  transfers between devices with their start and end apart: 7, of which 4 were waited for; matrix products, arithmetic and copies ran while one was open for 2% of the time, Pallas kernels for 28%

profile of v2, /device:TPU:1, one launch (start us, length us, event | category | flops | bytes accessed | tf_op | source)
XLA Modules:
  0.0 119.1 jit_solution(3647306973012743981)
XLA Ops:
  0.6 1.8 %slice_bitcast_fusion = bf16[64,3584]{1,0:T(8,128)(2,1)} fusion(bf16[1,192,3584]{2,1,0:T(8,128)(2,1)} %param.25), kind=kLoop, calls=%fused_computation.1 | loop fusion | bytes 917504 | tf_op jit(solution)/shard_map/squeeze | solution.py:573
  2.5 3.6 %collective-permute-start = (bf16[64,3584]{1,0:T(8,128)(2,1)}, bf16[64,3584]{1,0:T(8,128)(2,1)}, u32[]{:S(2)}, u32[]{:S(2)}) collective-permute-start(bf16[64,3584]{1,0:T(8,128)(2,1)} %slice_bitcast_fusion), channel_id=1, source_target_pairs={{0,16},{1,17},{2,18},{3,19},{4,20},{5,21},{6,22},{7,23},{8,24},{9,... | collective-permute-start | bytes 1376264 | tf_op jit(solution)/shard_map/ppermute | solution.py:573
  6.0 1.2 copy-done.5
  7.2 0.7 copy-done.8
  8.0 0.7 copy-done.11
  8.7 0.7 copy-done.16
  9.3 0.7 copy-done.18
  10.0 0.0 copy-start.10
  10.0 0.0 copy-start.13
  10.0 0.0 copy-start.14
  10.0 0.0 copy-start.15
  10.1 2.3 %shard_map.196 = bf16[256,1024]{1,0:T(8,128)(2,1)} custom-call(bf16[128,3584]{1,0:T(8,128)(2,1)S(1)} %bitcast.55, f32[56,128]{1,0:T(8,128)S(1)} %bitcast.59, bf16[64,128]{1,0:T(8,128)(2,1)S(1)} %bitcast.67, f32[1,56]{1,0:T(1,128)S(1)} %bitcast.79, f32[1,56]{1,0:T(1,128)S(1)} %bitcast.84), custom_call_target="tpu_custom_call" | custom-call | flops 5000000000 | bytes 8388608 | tf_op jit(solution)/shard_map/pallas_call | solution.py:530
  12.4 6.2 %all-to-all-start = ((bf16[32,8,1024]{2,1,0:T(8,128)(2,1)}), bf16[32,8,1024]{2,1,0:T(8,128)(2,1)S(1)}, u32[]{:S(2)}, u32[]{:S(2)}) async-start(bf16[32,8,1024]{2,1,0:T(8,128)(2,1)} %bitcast.14), calls=%async_computation | async-start | bytes 1048576 | tf_op jit(solution)/shard_map/all_to_all | solution.py:570
  18.6 0.0 copy-done.1
  18.6 0.0 copy-done.3
  18.6 0.0 copy-done.6
  18.6 0.0 copy-done.9
  18.6 0.0 copy-done.10
  18.6 0.0 copy-done.12
  18.6 0.0 copy-done.13
  18.7 0.0 copy-start.37
  18.7 5.9 %shard_map.198 = (f32[128,3584]{1,0:T(8,128)S(1)}, f32[16,128,128]{2,1,0:T(8,128)S(1)}) custom-call(bf16[128,3584]{1,0:T(8,128)(2,1)S(1)} %bitcast.56, f32[56,128]{1,0:T(8,128)S(1)} %bitcast.60, bf16[64,128]{1,0:T(8,128)(2,1)S(1)} %bitcast.68, bf16[64,128]{1,0:T(8,128)(2,1)S(1)} %bitcast.64, f32[1,56]{1,0:T(1,128)S(1)} %bitcast.80, f32[1,56]{1,0:T(1,128)S(1)} %bitcast.85, ...), custom_call_target="tpu_custom_call" | custom-call | flops 8000000000 | bytes 8388608 | tf_op jit(solution)/shard_map/pallas_call | solution.py:530
  24.6 0.0 copy-start.22
  24.6 1.0 copy-done.22
  25.6 1.3 %copy-done.31 = f32[128,3584]{1,0:T(8,128)} copy-done((f32[128,3584]{1,0:T(8,128)}, f32[128,3584]{1,0:T(8,128)S(1)}, u32[]{:S(2)}) %copy-start.31) | copy-done | bytes 1835032
  26.9 3.3 %all-to-all-done = bf16[32,8,1024]{2,1,0:T(8,128)(2,1)S(1)} async-done(((bf16[32,8,1024]{2,1,0:T(8,128)(2,1)}), bf16[32,8,1024]{2,1,0:T(8,128)(2,1)S(1)}, u32[]{:S(2)}, u32[]{:S(2)}) %all-to-all-start) | async-done | bytes 524320 | tf_op jit(solution)/shard_map/all_to_all | solution.py:570
  30.2 1.1 shard_map.197
  31.3 4.1 %all-to-all-start.1 = ((bf16[32,8,896]{2,1,0:T(8,128)(2,1)}), bf16[32,8,896]{2,1,0:T(8,128)(2,1)S(1)}, u32[]{:S(2)}, u32[]{:S(2)}) async-start(bf16[32,8,896]{2,1,0:T(8,128)(2,1)} %bitcast.16), calls=%async_computation.1 | async-start | bytes 917504 | tf_op jit(solution)/shard_map/all_to_all | solution.py:570
  35.4 0.0 collective-permute-done.back_ref
  35.4 0.0 copy-start.23
  35.4 1.2 %copy-done.23 = f32[16,128,128]{2,1,0:T(8,128)S(1)} copy-done((f32[16,128,128]{2,1,0:T(8,128)S(1)}, f32[16,128,128]{2,1,0:T(8,128)}, u32[]{:S(2)}) %copy-start.23) | copy-done | bytes 1048600
  36.7 2.8 %shard_map.199 = (bf16[128,3584]{1,0:T(8,128)(2,1)S(1)}, bf16[128,3584]{1,0:T(8,128)(2,1)S(1)}) custom-call(s32[8,32]{1,0:T(8,128)S(1)} %bitcast.72, s32[8,32]{1,0:T(8,128)S(1)} %bitcast.75, f32[16,128,128]{2,1,0:T(8,128)S(1)} %copy-done.23, bf16[192,3584]{1,0:T(8,128)(2,1)S(1)} %bitcast.50, bf16[64,3584]{1,0:T(8,128)(2,1)} %collective-permute-done.back_ref), custom_call_target="tpu_custom_call" | custom-call | flops 5000000000 | bytes 8388608 | tf_op jit(solution)/shard_map/pallas_call | solution.py:530
  39.5 0.0 copy-start.25
  39.5 0.9 copy-done.25
  40.4 0.9 copy-done.27
  41.4 5.0 %all-to-all-done.1 = bf16[32,8,896]{2,1,0:T(8,128)(2,1)S(1)} async-done(((bf16[32,8,896]{2,1,0:T(8,128)(2,1)}), bf16[32,8,896]{2,1,0:T(8,128)(2,1)S(1)}, u32[]{:S(2)}, u32[]{:S(2)}) %all-to-all-start.1) | async-done | bytes 458784 | tf_op jit(solution)/shard_map/all_to_all | solution.py:570
  46.4 1.2 copy-done.28
  47.6 1.5 %copy-done.32 = f32[128,3584]{1,0:T(8,128)S(1)} copy-done((f32[128,3584]{1,0:T(8,128)S(1)}, f32[128,3584]{1,0:T(8,128)}, u32[]{:S(2)}) %copy-start.32) | copy-done | bytes 1835032
  49.1 3.2 %shard_map.200 = (f32[128,3584]{1,0:T(8,128)S(1)}, bf16[128,3584]{1,0:T(8,128)(2,1)S(1)}, bf16[128,3584]{1,0:T(8,128)(2,1)S(1)}, bf16[256,1024]{1,0:T(8,128)(2,1)}) custom-call(f32[56,128]{1,0:T(8,128)S(1)} %bitcast.61, bf16[64,128]{1,0:T(8,128)(2,1)S(1)} %bitcast.65, f32[1,56]{1,0:T(1,128)S(1)} %bitcast.81, f32[1,56]{1,0:T(1,128)S(1)} %bitcast.86, ...), custom_call_target="tpu_custom_call" | custom-call | flops 7000000000 | bytes 8388608 | tf_op jit(solution)/shard_map/pallas_call | solution.py:530
  52.3 1.3 %copy-done.29 = f32[128,3584]{1,0:T(8,128)} copy-done((f32[128,3584]{1,0:T(8,128)}, f32[128,3584]{1,0:T(8,128)S(1)}, u32[]{:S(2)}) %copy-start.29) | copy-done | bytes 1835032
  53.6 0.9 copy-done.33
  54.5 0.9 copy-done.35
  55.5 3.7 %all-to-all-start.2 = ((bf16[32,8,1024]{2,1,0:T(8,128)(2,1)}), bf16[32,8,1024]{2,1,0:T(8,128)(2,1)S(1)}, u32[]{:S(2)}, u32[]{:S(2)}) async-start(bf16[32,8,1024]{2,1,0:T(8,128)(2,1)} %bitcast.29), calls=%async_computation.2 | async-start | bytes 1048576 | tf_op jit(solution)/shard_map/all_to_all | solution.py:570
  59.2 0.0 copy-start.24
  59.2 1.2 %copy-done.24 = f32[16,128,128]{2,1,0:T(8,128)S(1)} copy-done((f32[16,128,128]{2,1,0:T(8,128)S(1)}, f32[16,128,128]{2,1,0:T(8,128)}, u32[]{:S(2)}) %copy-start.24) | copy-done | bytes 1048600
  60.4 1.2 copy-done.26
  61.6 1.2 copy-done.36
  62.7 8.5 %shard_map.201 = (bf16[192,3584]{1,0:T(8,128)(2,1)}, bf16[64,3584]{1,0:T(8,128)(2,1)}, bf16[128,3584]{1,0:T(8,128)(2,1)}, bf16[128,3584]{1,0:T(8,128)(2,1)}) custom-call(s32[8,32]{1,0:T(8,128)S(1)} %bitcast.73, s32[8,32]{1,0:T(8,128)S(1)} %bitcast.76, bf16[128,3584]{1,0:T(8,128)(2,1)S(1)} %bitcast.52, bf16[128,3584]{1,0:T(8,128)(2,1)S(1)} %bitcast.54, ...), custom_call_target="tpu_custom_call" | custom-call | flops 8000000000 | bytes 8388608 | tf_op jit(solution)/shard_map/pallas_call | solution.py:530
  71.3 2.8 %collective-permute-start.1 = (bf16[64,3584]{1,0:T(8,128)(2,1)}, bf16[64,3584]{1,0:T(8,128)(2,1)}, u32[]{:S(2)}, u32[]{:S(2)}) collective-permute-start(bf16[64,3584]{1,0:T(8,128)(2,1)} %get-tuple-element.41), channel_id=1, source_target_pairs={{0,16},{1,17},{2,18},{3,19},{4,20},{5,21},{6,22},{7,23},{8,24},{9,... | collective-permute-start | bytes 1376264 | tf_op jit(solution)/shard_map/ppermute | solution.py:617
  74.1 0.0 all-to-all-done.2
  74.1 1.1 shard_map.202
  75.2 5.7 %all-to-all-start.3 = ((bf16[32,8,896]{2,1,0:T(8,128)(2,1)}), bf16[32,8,896]{2,1,0:T(8,128)(2,1)S(1)}, u32[]{:S(2)}, u32[]{:S(2)}) async-start(bf16[32,8,896]{2,1,0:T(8,128)(2,1)} %bitcast.31), calls=%async_computation.3 | async-start | bytes 917504 | tf_op jit(solution)/shard_map/all_to_all | solution.py:570
  80.9 1.5 %copy-done.30 = f32[128,3584]{1,0:T(8,128)S(1)} copy-done((f32[128,3584]{1,0:T(8,128)S(1)}, f32[128,3584]{1,0:T(8,128)}, u32[]{:S(2)}) %copy-start.30) | copy-done | bytes 1835032
  82.4 7.6 %shard_map.203 = (f32[128,3584]{1,0:T(8,128)S(1)}, f32[128,128]{1,0:T(8,128)S(1)}, f32[128,128]{1,0:T(8,128)S(1)}, bf16[64,128]{1,0:T(8,128)(2,1)}, f32[64,128]{1,0:T(8,128)S(1)}, /*index=5*/f32[1,128]{1,0:T(1,128)S(1)}) custom-call(bf16[128,3584]{1,0:T(8,128)(2,1)S(1)} %bitcast.57, f32[56,128]{1,0:T(8,128)S(1)} %bitcast.62, bf16[64,128]{1,0:T(8,128)(2,1)S(1)} %bitcast.69, ...), custom_call_target="tpu_custom_call" | custom-call | flops 8000000000 | bytes 8388608 | tf_op jit(solution)/shard_map/pallas_call | solution.py:530
  90.0 1.3 %copy-done.20 = f32[128,3584]{1,0:T(8,128)} copy-done((f32[128,3584]{1,0:T(8,128)}, f32[128,3584]{1,0:T(8,128)S(1)}, u32[]{:S(2)}) %copy-start.20) | copy-done | bytes 1835032
  91.3 1.5 %all-to-all-done.3 = bf16[32,8,896]{2,1,0:T(8,128)(2,1)S(1)} async-done(((bf16[32,8,896]{2,1,0:T(8,128)(2,1)}), bf16[32,8,896]{2,1,0:T(8,128)(2,1)S(1)}, u32[]{:S(2)}, u32[]{:S(2)}) %all-to-all-start.3) | async-done | bytes 458784 | tf_op jit(solution)/shard_map/all_to_all | solution.py:570
  92.7 1.5 %copy-done.21 = f32[128,3584]{1,0:T(8,128)S(1)} copy-done((f32[128,3584]{1,0:T(8,128)S(1)}, f32[128,3584]{1,0:T(8,128)}, u32[]{:S(2)}) %copy-start.21) | copy-done | bytes 1835032
  94.2 4.0 %shard_map.204 = (bf16[128,3584]{1,0:T(8,128)(2,1)}, bf16[64,128]{1,0:T(8,128)(2,1)}, f32[56,128]{1,0:T(8,128)}, f32[128,1,384]{2,1,0:T(1,128)}) custom-call(bf16[128,3584]{1,0:T(8,128)(2,1)S(1)} %bitcast.58, f32[56,128]{1,0:T(8,128)S(1)} %bitcast.63, bf16[64,128]{1,0:T(8,128)(2,1)S(1)} %bitcast.70, f32[1,56]{1,0:T(1,128)S(1)} %bitcast.83, ...), custom_call_target="tpu_custom_call" | custom-call | flops 6000000000 | bytes 8388608 | tf_op jit(solution)/shard_map/pallas_call | solution.py:530
  98.3 8.8 %all-to-all-start.4 = ((f32[128,1,384]{2,1,0:T(1,128)}), f32[128,1,384]{2,1,0:T(1,128)S(1)}, u32[]{:S(2)}, u32[]{:S(2)}) async-start(f32[128,1,384]{2,1,0:T(1,128)} %get-tuple-element.58), calls=%async_computation.4 | async-start | bytes 393216 | tf_op jit(solution)/shard_map/all_to_all | solution.py:652
  107.1 0.0 collective-permute-done.1
  107.1 1.8 %bitcast_dynamic-update-slice_fusion = bf16[1,192,3584]{2,1,0:T(8,128)(2,1)} fusion(bf16[1,192,3584]{2,1,0:T(8,128)(2,1)} %bitcast.89, bf16[64,3584]{1,0:T(8,128)(2,1)} %collective-permute-done.1), kind=kLoop, calls=%fused_computation | loop fusion | bytes 917504 | tf_op jit(solution)/shard_map/dynamic_update_slice | solution.py:653
  108.9 8.7 %all-to-all-done.4.sums_ref = f32[128,1,384]{2,1,0:T(1,128)S(1)} async-done(((f32[128,1,384]{2,1,0:T(1,128)}), f32[128,1,384]{2,1,0:T(1,128)S(1)}, u32[]{:S(2)}, u32[]{:S(2)}) %all-to-all-start.4) | async-done | bytes 196640 | tf_op jit(solution)/shard_map/all_to_all | solution.py:652
  117.6 0.8 shard_map.205
  118.4 0.6 reduce
  (40 shorter events, 0.1 us)
Async XLA Ops:
  2.5 33.0 %collective-permute-start = (bf16[64,3584]{1,0:T(8,128)(2,1)}, bf16[64,3584]{1,0:T(8,128)(2,1)}, u32[]{:S(2)}, u32[]{:S(2)}) collective-permute-start(bf16[64,3584]{1,0:T(8,128)(2,1)} %slice_bitcast_fusion), channel_id=1, source_target_pairs={{0,16},{1,17},{2,18},{3,19},{4,20},{5,21},{6,22},{7,23},{8,24},{9,... | collective-permute-start | bytes 1376264 | tf_op jit(solution)/shard_map/ppermute | solution.py:573
  6.0 1.2 copy-start.5
  7.2 0.7 copy-start.8
  8.0 0.7 copy-start.11
  8.7 0.7 copy-start.16
  9.3 0.7 copy-start.18
  10.0 8.6 %copy-start.1 = (bf16[1,128,3584]{2,1,0:T(8,128)(2,1)S(1)}, bf16[1,128,3584]{2,1,0:T(8,128)(2,1)}, u32[]{:S(2)}) copy-start(bf16[1,128,3584]{2,1,0:T(8,128)(2,1)} %param.23) | copy-start | bytes 2752516
  10.0 8.6 %copy-start.3 = (bf16[1,128,3584]{2,1,0:T(8,128)(2,1)S(1)}, bf16[1,128,3584]{2,1,0:T(8,128)(2,1)}, u32[]{:S(2)}) copy-start(bf16[1,128,3584]{2,1,0:T(8,128)(2,1)} %param.24) | copy-start | bytes 2752516
  10.0 8.6 %copy-start.6 = (bf16[1,128,3584]{2,1,0:T(8,128)(2,1)S(1)}, bf16[1,128,3584]{2,1,0:T(8,128)(2,1)}, u32[]{:S(2)}) copy-start(bf16[1,128,3584]{2,1,0:T(8,128)(2,1)} %param.13) | copy-start | bytes 2752516
  10.0 8.6 %copy-start.9 = (f32[1,56,128]{2,1,0:T(8,128)S(1)}, f32[1,56,128]{2,1,0:T(8,128)}, u32[]{:S(2)}) copy-start(f32[1,56,128]{2,1,0:T(8,128)} %param.14) | copy-start | bytes 86020
  10.0 8.6 %copy-start.10 = (bf16[1,128,64]{1,2,0:T(8,128)(2,1)S(1)}, bf16[1,128,64]{1,2,0:T(8,128)(2,1)}, u32[]{:S(2)}) copy-start(bf16[1,128,64]{1,2,0:T(8,128)(2,1)} %param.16) | copy-start | bytes 49156
  10.0 8.6 %copy-start.12 = (bf16[1,128,64]{1,2,0:T(8,128)(2,1)S(1)}, bf16[1,128,64]{1,2,0:T(8,128)(2,1)}, u32[]{:S(2)}) copy-start(bf16[1,128,64]{1,2,0:T(8,128)(2,1)} %param.15) | copy-start | bytes 49156
  10.0 8.6 %copy-start.13 = (s32[1,32,8]{1,2,0:T(8,128)S(1)}, s32[1,32,8]{1,2,0:T(8,128)}, u32[]{:S(2)}) copy-start(s32[1,32,8]{1,2,0:T(8,128)} %param.21) | copy-start | bytes 3076
  10.0 8.6 %copy-start.14 = (s32[1,32,8]{1,2,0:T(8,128)S(1)}, s32[1,32,8]{1,2,0:T(8,128)}, u32[]{:S(2)}) copy-start(s32[1,32,8]{1,2,0:T(8,128)} %param.22) | copy-start | bytes 3076
  10.0 8.6 %copy-start.15 = (f32[56]{0:T(128)S(1)}, f32[56]{0:T(128)}, u32[]{:S(2)}) copy-start(f32[56]{0:T(128)} %param.19) | copy-start | bytes 676
  10.1 8.6 %copy-start.17 = (f32[56]{0:T(128)S(1)}, f32[56]{0:T(128)}, u32[]{:S(2)}) copy-start(f32[56]{0:T(128)} %param.17) | copy-start | bytes 676
  10.1 8.6 %copy-start.19 = (f32[56]{0:T(128)S(1)}, f32[56]{0:T(128)}, u32[]{:S(2)}) copy-start(f32[56]{0:T(128)} %param.18) | copy-start | bytes 676
  12.4 17.8 %all-to-all-start = ((bf16[32,8,1024]{2,1,0:T(8,128)(2,1)}), bf16[32,8,1024]{2,1,0:T(8,128)(2,1)S(1)}, u32[]{:S(2)}, u32[]{:S(2)}) async-start(bf16[32,8,1024]{2,1,0:T(8,128)(2,1)} %bitcast.14), calls=%async_computation | async-start | bytes 1048576 | tf_op jit(solution)/shard_map/all_to_all | solution.py:570
  18.7 8.2 %copy-start.37 = (f32[3584]{0:T(1024)S(1)}, f32[3584]{0:T(1024)}, u32[]{:S(2)}) copy-start(f32[3584]{0:T(1024)} %param.20) | copy-start | bytes 43012
  24.6 1.0 copy-start.22
  25.6 1.3 %copy-start.31 = (f32[128,3584]{1,0:T(8,128)}, f32[128,3584]{1,0:T(8,128)S(1)}, u32[]{:S(2)}) copy-start(f32[128,3584]{1,0:T(8,128)S(1)} %get-tuple-element.35.inner_ref) | copy-start | bytes 5505028
  30.2 5.2 %copy-start = (bf16[1,192,3584]{2,1,0:T(8,128)(2,1)S(1)}, bf16[1,192,3584]{2,1,0:T(8,128)(2,1)}, u32[]{:S(2)}) copy-start(bf16[1,192,3584]{2,1,0:T(8,128)(2,1)} %param.25) | copy-start | bytes 4128772
  31.3 15.1 %all-to-all-start.1 = ((bf16[32,8,896]{2,1,0:T(8,128)(2,1)}), bf16[32,8,896]{2,1,0:T(8,128)(2,1)S(1)}, u32[]{:S(2)}, u32[]{:S(2)}) async-start(bf16[32,8,896]{2,1,0:T(8,128)(2,1)} %bitcast.16), calls=%async_computation.1 | async-start | bytes 917504 | tf_op jit(solution)/shard_map/all_to_all | solution.py:570
  35.4 1.2 %copy-start.23 = (f32[16,128,128]{2,1,0:T(8,128)S(1)}, f32[16,128,128]{2,1,0:T(8,128)}, u32[]{:S(2)}) copy-start(f32[16,128,128]{2,1,0:T(8,128)} %copy-done.22) | copy-start | bytes 3145732
  39.5 0.9 copy-start.25
  40.4 0.9 copy-start.27
  46.4 1.2 copy-start.28
  47.6 1.5 %copy-start.32 = (f32[128,3584]{1,0:T(8,128)S(1)}, f32[128,3584]{1,0:T(8,128)}, u32[]{:S(2)}) copy-start(f32[128,3584]{1,0:T(8,128)} %copy-done.31) | copy-start | bytes 5505028
  49.1 10.1 %copy-start.2 = (bf16[1,128,3584]{2,1,0:T(8,128)(2,1)S(1)}, bf16[1,128,3584]{2,1,0:T(8,128)(2,1)}, u32[]{:S(2)}) copy-start(bf16[1,128,3584]{2,1,0:T(8,128)(2,1)} %param.23) | copy-start | bytes 2752516
  49.1 10.1 %copy-start.4 = (bf16[1,128,3584]{2,1,0:T(8,128)(2,1)S(1)}, bf16[1,128,3584]{2,1,0:T(8,128)(2,1)}, u32[]{:S(2)}) copy-start(bf16[1,128,3584]{2,1,0:T(8,128)(2,1)} %param.24) | copy-start | bytes 2752516
  52.3 1.3 %copy-start.29 = (f32[128,3584]{1,0:T(8,128)}, f32[128,3584]{1,0:T(8,128)S(1)}, u32[]{:S(2)}) copy-start(f32[128,3584]{1,0:T(8,128)S(1)} %get-tuple-element.46.y_ref) | copy-start | bytes 5505028
  53.6 0.9 copy-start.33
  54.5 0.9 copy-start.35
  55.5 18.6 %all-to-all-start.2 = ((bf16[32,8,1024]{2,1,0:T(8,128)(2,1)}), bf16[32,8,1024]{2,1,0:T(8,128)(2,1)S(1)}, u32[]{:S(2)}, u32[]{:S(2)}) async-start(bf16[32,8,1024]{2,1,0:T(8,128)(2,1)} %bitcast.29), calls=%async_computation.2 | async-start | bytes 1048576 | tf_op jit(solution)/shard_map/all_to_all | solution.py:570
  59.2 1.2 %copy-start.24 = (f32[16,128,128]{2,1,0:T(8,128)S(1)}, f32[16,128,128]{2,1,0:T(8,128)}, u32[]{:S(2)}) copy-start(f32[16,128,128]{2,1,0:T(8,128)} %copy-done.22) | copy-start | bytes 3145732
  60.4 1.2 copy-start.26
  61.6 1.2 copy-start.36
  71.3 35.8 %collective-permute-start.1 = (bf16[64,3584]{1,0:T(8,128)(2,1)}, bf16[64,3584]{1,0:T(8,128)(2,1)}, u32[]{:S(2)}, u32[]{:S(2)}) collective-permute-start(bf16[64,3584]{1,0:T(8,128)(2,1)} %get-tuple-element.41), channel_id=1, source_target_pairs={{0,16},{1,17},{2,18},{3,19},{4,20},{5,21},{6,22},{7,23},{8,24},{9,... | collective-permute-start | bytes 1376264 | tf_op jit(solution)/shard_map/ppermute | solution.py:617
  74.1 6.8 %copy-start.7 = (bf16[1,128,3584]{2,1,0:T(8,128)(2,1)S(1)}, bf16[1,128,3584]{2,1,0:T(8,128)(2,1)}, u32[]{:S(2)}) copy-start(bf16[1,128,3584]{2,1,0:T(8,128)(2,1)} %param.13) | copy-start | bytes 2752516
  74.1 6.8 %copy-start.34 = (bf16[128,3584]{1,0:T(8,128)(2,1)S(1)}, bf16[128,3584]{1,0:T(8,128)(2,1)}, u32[]{:S(2)}) copy-start(bf16[128,3584]{1,0:T(8,128)(2,1)} %copy-done.33) | copy-start | bytes 2752516
  75.2 17.5 %all-to-all-start.3 = ((bf16[32,8,896]{2,1,0:T(8,128)(2,1)}), bf16[32,8,896]{2,1,0:T(8,128)(2,1)S(1)}, u32[]{:S(2)}, u32[]{:S(2)}) async-start(bf16[32,8,896]{2,1,0:T(8,128)(2,1)} %bitcast.31), calls=%async_computation.3 | async-start | bytes 917504 | tf_op jit(solution)/shard_map/all_to_all | solution.py:570
  80.9 1.5 %copy-start.30 = (f32[128,3584]{1,0:T(8,128)S(1)}, f32[128,3584]{1,0:T(8,128)}, u32[]{:S(2)}) copy-start(f32[128,3584]{1,0:T(8,128)} %copy-done.29) | copy-start | bytes 5505028
  90.0 1.3 %copy-start.20 = (f32[128,3584]{1,0:T(8,128)}, f32[128,3584]{1,0:T(8,128)S(1)}, u32[]{:S(2)}) copy-start(f32[128,3584]{1,0:T(8,128)S(1)} %get-tuple-element.48.dx_ref) | copy-start | bytes 5505028
  92.7 1.5 %copy-start.21 = (f32[128,3584]{1,0:T(8,128)S(1)}, f32[128,3584]{1,0:T(8,128)}, u32[]{:S(2)}) copy-start(f32[128,3584]{1,0:T(8,128)} %copy-done.20) | copy-start | bytes 5505028
  98.3 19.4 %all-to-all-start.4 = ((f32[128,1,384]{2,1,0:T(1,128)}), f32[128,1,384]{2,1,0:T(1,128)S(1)}, u32[]{:S(2)}, u32[]{:S(2)}) async-start(f32[128,1,384]{2,1,0:T(1,128)} %get-tuple-element.58), calls=%async_computation.4 | async-start | bytes 393216 | tf_op jit(solution)/shard_map/all_to_all | solution.py:652

commit v3 on v2

--- a/solution.py
+++ b/solution.py
@@ -84,26 +84,119 @@
     return z, step, neg, running
 
 
+def chunk(g, size):
+    return pl.ds(g * size if isinstance(g, int) else pl.multiple_of(g * size, size), size)
+
+
 def lanes(g):
-    return pl.ds(pl.multiple_of(g * GW, 128), GW)
+    return chunk(g, GW)
 
 
 def rows64(g):
-    return pl.ds(pl.multiple_of(g * SIZE, SIZE), SIZE)
-
-
-def states_kernel(x_ref, raw_ref, in_ref, rate_ref, bias_ref, out_ref):
+    return chunk(g, SIZE)
+
+
+def by_lane(ref, g):
+    return ref.at[:, lanes(g)]
+
+
+def by_lane_top(ref, g):
+    return ref.at[pl.ds(0, TOK), lanes(g)]
+
+
+def by_row(ref, g):
+    return ref.at[rows64(g), :]
+
+
+def by_head(ref, g):
+    return ref.at[pl.ds(AH * g, AH)]
+
+
+def each_group(body, carry):
+    for g in range(GROUPS):
+        carry = body(g, carry)
+    return carry
+
+
+class Copies:
+    def __init__(self, sem, *pairs):
+        self.sem, self.pairs = sem, pairs
+
+    def parts(self, g):
+        made = []
+        for i, (source, target, view, *other) in enumerate(self.pairs):
+            view_to = other[0] if other else view
+            made.append(
+                pltpu.make_async_copy(view(source, g), view_to(target, g), self.sem.at[i, g])
+            )
+        return made
+
+    def start(self, g):
+        for copy in self.parts(g):
+            copy.start()
+
+    def wait(self, g):
+        for copy in self.parts(g):
+            copy.wait()
+
+    def start_all(self, groups=range(GROUPS)):
+        for g in groups:
+            self.start(g)
+
+    def wait_all(self, groups=range(GROUPS)):
+        for g in groups:
+            self.wait(g)
+
+
+def states_kernel(
+    x_hbm,
+    raw_hbm,
+    in_hbm,
+    rate_hbm,
+    bias_hbm,
+    out_hbm,
+    decays_ref,
+    tail_ref,
+    x_ref,
+    raw_ref,
+    in_ref,
+    rate_ref,
+    bias_ref,
+    out_ref,
+    sem,
+    small,
+    out_sem,
+):
+    smalls = [
+        pltpu.make_async_copy(source, target, small.at[i])
+        for i, (source, target) in enumerate(
+            ((raw_hbm, raw_ref), (rate_hbm, rate_ref), (bias_hbm, bias_ref), (in_hbm, in_ref))
+        )
+    ]
+    for copy in smalls:
+        copy.start()
+    fetch = Copies(sem, (x_hbm, x_ref, by_lane))
+    fetch.start_all()
+    put = Copies(out_sem, (out_ref, out_hbm, by_row))
+    for copy in smalls:
+        copy.wait()
     rate, bias = columns(rate_ref[...], bias_ref[...])
-    _, step, _, running = decay_sums(raw_ref[...], bias, rate)
+    z, step, neg, running = decay_sums(raw_ref[...], bias, rate)
     last = running[:, TOK - 1 :]
     tail = stacked_parts(jnp.exp(last - running) * step)
     total = stacked_parts(jnp.broadcast_to(jnp.exp(last), running.shape))[:SIZE]
     in_map = in_ref[...]
     for g in range(GROUPS):
         wide = dot(tail, expander(g))
+        fetch.wait(g)
         scaled = (x_ref[:, g * GW : (g + 1) * GW].astype(F32) * wide).astype(BF16)
         out_ref[g * SIZE : (g + 1) * SIZE, :GW] = dot(in_map, scaled).astype(BF16)
         out_ref[g * SIZE : (g + 1) * SIZE, GW:] = total
+        put.start(g)
+    tail_ref[...] = tail
+    for i, value in enumerate((z, step, jnp.broadcast_to(neg, z.shape), running)):
+        decays_ref[i] = value
+    put.wait_all()
 
 
 def scan_kernel(blocks, reverse, *refs):
@@ -183,22 +276,77 @@
 
 
 def inner_kernel(
-    x_ref,
-    raw_ref,
+    x_hbm,
+    decays_ref,
     in_ref,
     map_ref,
-    rate_ref,
-    bias_ref,
     skip_ref,
+    y_hbm,
+    grown_ref,
+    skips_ref,
+    x_ref,
+    y_ref,
+    column_ref,
+    row_ref,
+    sem,
+    out_sem,
+):
+    fetch = Copies(sem, (x_hbm, x_ref, by_lane))
+    put = Copies(out_sem, (y_ref, y_hbm, by_lane))
+    fetch.start_all()
+    square = (TOK, TOK)
+    (skip,) = columns(skip_ref[...])
+    step, running = decays_ref[1], decays_ref[3]
+    skips = stacked_parts(jnp.broadcast_to(skip, (SIZE, TOK)))[:16]
+    skips_ref[...] = skips
+    grown_ref[...] = stacked_parts(jnp.exp(running))
+    row_ref[...] = running - jnp.log(step)
+    for g, column in enumerate(columns_of(running)):
+        column_ref[g] = column
+    causal = iota(square, 0) >= iota(square, 1)
+    gram = jnp.where(causal, dot(map_ref[...], in_ref[...], TN), 0.0)
+
+    def group(g, carry):
+        at = lanes(g)
+        fetch.wait(g)
+        x = x_ref[:, at]
+        heads = row_ref[chunk(g, 16), :]
+        column = column_ref[g]
+        inner = []
+        for i in range(GH // 2):
+            pair = [(local_decay(column, heads, h) * gram).astype(BF16) for h in (2 * i, 2 * i + 1)]
+            rows = pair_rows(x[:, 128 * i : 128 * (i + 1)])
+            inner.append(dot(jnp.concatenate(pair, axis=1), rows))
+        y_ref[:, at] = jnp.concatenate(inner, axis=1) + dot(skips, expander(g))[:1] * x.astype(F32)
+        put.start(g)
+        return carry
+
+    each_group(group, 0)
+    put.wait_all()
+
+
+def weights_kernel(
     lengths_ref,
     moved_ref,
+    q_hbm,
+    k_hbm,
+    grad_hbm,
+    probs_hbm,
+    moved_hbm,
     q_ref,
     k_ref,
-    y_ref,
+    rows_ref,
     probs_ref,
-    column_ref,
-    row_ref,
+    sem,
+    out_sem,
+    moved_sem,
 ):
+    fetch = Copies(sem, (q_hbm, q_ref, by_lane), (k_hbm, k_ref, by_lane))
+    put = Copies(out_sem, (probs_ref, probs_hbm, by_head))
+    arrive = pltpu.make_async_copy(grad_hbm.at[pl.ds(TOK, SEND), :], rows_ref, moved_sem.at[0])
+    leave = pltpu.make_async_copy(rows_ref, moved_hbm, moved_sem.at[1])
+    arrive.start()
+    fetch.start_all()
     scale = 1.0 / math.sqrt(ASIZE)
     square = (TOK, TOK)
     at_q, at_k = iota(square, 0), iota(square, 1)
@@ -210,17 +358,13 @@
         seg_k += jnp.where(at_k >= end, 1, 0)
     allowed = (seg_q == seg_k) & (at_k <= at_q)
     masks = lane_masks()
-    rate, bias, skip = columns(rate_ref[...], bias_ref[...], skip_ref[...])
-    _, step, _, running = decay_sums(raw_ref[...], bias, rate)
-    skips = stacked_parts(jnp.broadcast_to(skip, (SIZE, TOK)))[:16]
-    row_ref[...] = running - jnp.log(step)
-    for g, column in enumerate(columns_of(running)):
-        column_ref[g] = column
-    gram = jnp.where(at_q >= at_k, dot(map_ref[...], in_ref[...], TN), 0.0)
+    arrive.wait()
+    leave.start()
 
     def group(g, carry):
         at = lanes(g)
-        x, q, k = x_ref[:, at], q_ref[:, at], k_ref[:, at]
+        fetch.wait(g)
+        q, k = q_ref[:, at], k_ref[:, at]
         for i, (tile, count) in enumerate(WINDOWS):
             window = slice(128 * tile, 128 * (tile + count))
             scores = dot(q[:, window] * masks[i], k[:, window], NT) * scale
@@ -228,47 +372,73 @@
             weights = jnp.exp(scores - jnp.max(scores, axis=-1, keepdims=True))
             total = jnp.sum(weights, axis=-1, keepdims=True)
             probs_ref[AH * g + i] = weights * (1.0 / total)
-        heads = row_ref[pl.ds(pl.multiple_of(16 * g, 16), 16), :]
-        column = column_ref[g]
-        inner = []
-        for i in range(GH // 2):
-            pair = [(local_decay(column, heads, h) * gram).astype(BF16) for h in (2 * i, 2 * i + 1)]
-            rows = pair_rows(x[:, 128 * i : 128 * (i + 1)])
-            inner.append(dot(jnp.concatenate(pair, axis=1), rows))
-        y_ref[:, at] = jnp.concatenate(inner, axis=1) + dot(skips, expander(g))[:1] * x.astype(F32)
+        put.start(g)
         return carry
 
-    lax.fori_loop(0, GROUPS, group, 0)
-
-
-def value_grad_kernel(lengths_ref, moved_ref, probs_ref, grad_ref, back_ref, gv_ref, home_ref):
+    each_group(group, 0)
+    leave.wait()
+    put.wait_all()
+
+
+def value_grad_kernel(
+    lengths_ref,
+    moved_ref,
+    probs_hbm,
+    grad_hbm,
+    back_hbm,
+    gv_hbm,
+    home_hbm,
+    probs_ref,
+    grad_ref,
+    back_ref,
+    gv_ref,
+    home_ref,
+    sem,
+    out_sem,
+):
+    fetch = Copies(
+        sem,
+        (back_hbm, back_ref, by_lane),
+        (grad_hbm, grad_ref, by_lane_top, by_lane),
+        (probs_hbm, probs_ref, by_head),
+    )
+    put = Copies(out_sem, (gv_ref, gv_hbm, by_lane), (home_ref, home_hbm, by_lane))
+    fetch.start_all()
+    square = (TOK, TOK)
     docs = documents(lengths_ref, moved_ref)
-    slots = place_slots(docs, (TOK, TOK), 0)
-    place = jnp.where(slots == iota((TOK, TOK), 1), 1.0, 0.0).astype(BF16)[:, :SEND]
+    slots = place_slots(docs, square, 0)
+    place = jnp.where(slots == iota(square, 1), 1.0, 0.0).astype(BF16)[:, :SEND]
     kept = jnp.where(slots < 0, 1.0, 0.0).astype(BF16)[:, :1]
     masks = lane_masks()
 
     def group(g, carry):
         at = lanes(g)
-        grad = grad_ref[0:TOK, at] * kept + dot(place, back_ref[:, at]).astype(BF16)
+        fetch.wait(g)
+        grad = grad_ref[:, at] * kept + dot(place, back_ref[:, at]).astype(BF16)
         home_ref[:, at] = grad
         parts = []
         for i, (tile, count) in enumerate(WINDOWS):
             window = slice(128 * tile, 128 * (tile + count))
             parts.append(dot(probs_ref[AH * g + i].astype(BF16), grad[:, window] * masks[i], TN))
         gv_ref[:, at] = join_windows(parts).astype(BF16)
+        put.start(g)
         return carry
 
-    lax.fori_loop(0, GROUPS, group, 0)
+    each_group(group, 0)
+    put.wait_all()
 
 
 def norm_kernel(
-    raw_ref,
+    grown_ref,
     map_ref,
-    rate_ref,
-    bias_ref,
     gain_ref,
     start_ref,
+    inner_hbm,
+    gv_hbm,
+    y_hbm,
+    values_hbm,
+    low_hbm,
+    message_hbm,
     inner_ref,
     gv_ref,
     y_ref,
@@ -277,10 +447,15 @@
     message_ref,
     wide_ref,
     sums_ref,
+    sem,
+    y_sem,
+    out_sem,
 ):
-    rate, bias = columns(rate_ref[...], bias_ref[...])
-    _, _, _, running = decay_sums(raw_ref[...], bias, rate)
-    grown = stacked_parts(jnp.exp(running))
+    fetch = Copies(sem, (inner_hbm, inner_ref, by_lane), (gv_hbm, gv_ref, by_lane))
+    put_y = Copies(y_sem, (y_ref, y_hbm, by_lane))
+    put = Copies(out_sem, (values_ref, values_hbm, by_lane), (low_ref, low_hbm, by_lane))
+    fetch.start_all()
+    grown = grown_ref[...]
     map_in = map_ref[...]
     out_rows = jnp.transpose(map_in.astype(F32)).astype(BF16)
     power = jnp.zeros((TOK, 1), F32)
@@ -289,8 +464,11 @@
         at = slice(g * GW, (g + 1) * GW)
         wide = dot(grown, expander(g))
         wide_ref[:, at] = wide
-        y = inner_ref[:, at] + dot(out_rows, start_ref[g * SIZE : (g + 1) * SIZE, :]) * wide
+        carried = dot(out_rows, start_ref[g * SIZE : (g + 1) * SIZE, :]) * wide
+        fetch.wait(g)
+        y = inner_ref[:, at] + carried
         y_ref[:, at] = y
+        put_y.start(g)
         power = power + jnp.sum(y * y, axis=-1, keepdims=True)
         scaled = gv_ref[:, at].astype(F32) * gain_ref[:, at]
         along = along + jnp.sum(scaled * y, axis=-1, keepdims=True)
@@ -308,6 +486,7 @@
             sums_ref[7 * g + i : 7 * g + i + 1, :] = gain_sum[:, 128 * i : 128 * (i + 1)]
         mixed_grad = gv * gain * inverse - y * slope
         low_ref[:, at] = mixed_grad.astype(BF16)
+        put.start(g)
         grown_grad = (wide_ref[:, at] * mixed_grad).astype(BF16)
         message_ref[rows, :GW] = dot(map_in, grown_grad).astype(BF16)
     sums = sums_ref[...]
@@ -317,22 +496,45 @@
     at, source = iota(dims, 0), iota(dims, 1)
     spread = jnp.where((at >> 3 == source & 31) & (at & 7 == source >> 5), 1.0, 0.0).astype(BF16)
     message_ref[:, GW:] = dot(spread, jnp.concatenate([high, low, lowest], axis=0)).astype(BF16)
+    last = pltpu.make_async_copy(message_ref, message_hbm, out_sem.at[2, 0])
+    last.start()
+    put_y.wait_all()
+    put.wait_all()
+    last.wait()
 
 
 def attention_kernel(
     lengths_ref,
     moved_ref,
-    q_ref,
-    k_ref,
+    values_hbm,
+    probs_hbm,
+    home_hbm,
+    attn_hbm,
+    packed_hbm,
+    dscores_hbm,
     values_ref,
     probs_ref,
     home_ref,
     attn_ref,
     packed_ref,
-    gq_ref,
-    gk_ref,
+    dscores_ref,
+    sem,
+    out_sem,
 ):
+    fetch = Copies(
+        sem,
+        (probs_hbm, probs_ref, by_head),
+        (values_hbm, values_ref, by_lane),
+        (home_hbm, home_ref, by_lane),
+    )
+    put = Copies(
+        out_sem,
+        (packed_ref, packed_hbm, by_lane),
+        (attn_ref, attn_hbm, by_lane, by_lane_top),
+        (dscores_ref, dscores_hbm, by_head),
+    )
     scale = 1.0 / math.sqrt(ASIZE)
+    fetch.start_all()
     docs = documents(lengths_ref, moved_ref)
     pick = place_slots(docs, (SEND, TOK), 1) == iota((SEND, TOK), 0)
     pick = jnp.where(pick, 1.0, 0.0).astype(BF16)
@@ -341,8 +543,9 @@
 
     def group(g, carry):
         at = lanes(g)
-        q, k, grad, values = q_ref[:, at], k_ref[:, at], home_ref[:, at], values_ref[:, at]
-        outs, gqs, gks = [], [], []
+        fetch.wait(g)
+        values, grad = values_ref[:, at], home_ref[:, at]
+        outs = []
         for i, (tile, count) in enumerate(WINDOWS):
             window = slice(128 * tile, 128 * (tile + count))
             probs = probs_ref[AH * g + i]
@@ -350,46 +553,112 @@
             outs.append(dot(probs.astype(BF16), vals))
             dprobs = dot(grad[:, window], vals, NT)
             delta = jnp.sum(probs * dprobs, axis=-1, keepdims=True)
-            dscores = (probs * (dprobs - delta) * scale).astype(BF16)
+            dscores_ref[AH * g + i] = (probs * (dprobs - delta) * scale).astype(BF16)
+        head_out = join_windows(outs).astype(BF16)
+        attn_ref[:, at] = head_out * kept
+        packed_ref[:, at] = dot(pick, head_out).astype(BF16)
+        put.start(g)
+        return carry
+
+    each_group(group, 0)
+    put.wait_all()
+
+
+def attention_grad_kernel(
+    q_hbm,
+    k_hbm,
+    dscores_hbm,
+    arrived_hbm,
+    attn_in_hbm,
+    gq_hbm,
+    gk_hbm,
+    attn_hbm,
+    q_ref,
+    k_ref,
+    dscores_ref,
+    gq_ref,
+    gk_ref,
+    rows_ref,
+    sem,
+    out_sem,
+    arrived_sem,
+):
+    del attn_in_hbm
+    fetch = Copies(
+        sem,
+        (dscores_hbm, dscores_ref, by_head),
+        (k_hbm, k_ref, by_lane),
+        (q_hbm, q_ref, by_lane),
+    )
+    put = Copies(out_sem, (gq_ref, gq_hbm, by_lane), (gk_ref, gk_hbm, by_lane))
+    fetch.start_all()
+    arrive = pltpu.make_async_copy(arrived_hbm, rows_ref, arrived_sem.at[0])
+    leave = pltpu.make_async_copy(rows_ref, attn_hbm.at[pl.ds(TOK, SEND), :], arrived_sem.at[1])
+    arrive.start()
+    masks = lane_masks()
+
+    arrive.wait()
+    leave.start()
+
+    def group(g, carry):
+        at = lanes(g)
+        fetch.wait(g)
+        q, k = q_ref[:, at], k_ref[:, at]
+        gqs, gks = [], []
+        for i, (tile, count) in enumerate(WINDOWS):
+            window = slice(128 * tile, 128 * (tile + count))
+            dscores = dscores_ref[AH * g + i]
             gqs.append(dot(dscores, k[:, window] * masks[i]))
             gks.append(dot(dscores, q[:, window] * masks[i], TN))
-        head_out = join_windows(outs).astype(BF16)
-        attn_ref[0:TOK, at] = head_out * kept
-        packed_ref[:, at] = dot(pick, head_out).astype(BF16)
         gq_ref[:, at] = join_windows(gqs).astype(BF16)
         gk_ref[:, at] = join_windows(gks).astype(BF16)
+        put.start(g)
         return carry
 
-    lax.fori_loop(0, GROUPS, group, 0)
+    each_group(group, 0)
+    leave.wait()
+    put.wait_all()
 
 
 def inner_back_kernel(
-    x_ref,
-    raw_ref,
+    x_hbm,
+    decays_ref,
     in_ref,
     map_ref,
-    rate_ref,
-    bias_ref,
-    skip_ref,
-    start_ref,
-    y_ref,
-    low_ref,
-    dx_ref,
+    skips_ref,
+    grown_ref,
+    start_hbm,
+    y_hbm,
+    low_hbm,
+    dx_hbm,
     flow_ref,
     direct_ref,
     gout_ref,
     gin_ref,
     skip_sum_ref,
+    x_ref,
+    start_ref,
+    y_ref,
+    low_ref,
+    dx_ref,
     column_ref,
     row_ref,
-    sum_ref,
+    sem,
+    out_sem,
 ):
+    fetch = Copies(
+        sem,
+        (low_hbm, low_ref, by_lane),
+        (x_hbm, x_ref, by_lane),
+        (start_hbm, start_ref, by_row),
+        (y_hbm, y_ref, by_lane),
+    )
+    put = Copies(out_sem, (dx_ref, dx_hbm, by_lane))
+    fetch.start_all()
     square = (TOK, TOK)
     causal = iota(square, 0) >= iota(square, 1)
-    rate, bias, skip = columns(rate_ref[...], bias_ref[...], skip_ref[...])
-    _, step, _, running = decay_sums(raw_ref[...], bias, rate)
-    skips = stacked_parts(jnp.broadcast_to(skip, (SIZE, TOK)))[:16]
-    grown = stacked_parts(jnp.exp(running))
+    step, running = decays_ref[1], decays_ref[3]
+    skips, grown = skips_ref[...], grown_ref[...]
     row_ref[...] = running - jnp.log(step)
     for g, column in enumerate(columns_of(running)):
         column_ref[g] = column
@@ -397,17 +666,18 @@
     gram = jnp.where(causal, dot(map_in, in_map, TN), 0.0)
     flow_ref[...] = jnp.zeros_like(flow_ref)
     direct_ref[...] = jnp.zeros_like(direct_ref)
-    sum_ref[...] = jnp.zeros_like(sum_ref)
+    gout_ref[...] = jnp.zeros_like(gout_ref)
 
     def group(g, carry):
         gram_grad, skip_sum = carry
         at = lanes(g)
+        fetch.wait(g)
         x, low_grad = x_ref[:, at], low_ref[:, at]
         mixed_grad = low_grad.astype(F32)
         wide = expander(g)
         grown_grad = (dot(grown, wide) * mixed_grad).astype(BF16)
-        sum_ref[...] += dot(start_ref[rows64(g), :], grown_grad, NT)
-        heads = row_ref[pl.ds(pl.multiple_of(16 * g, 16), 16), :]
+        gout_ref[...] += dot(start_ref[rows64(g), :], grown_grad, NT)
+        heads = row_ref[chunk(g, 16), :]
         column = column_ref[g]
         inner = []
         for i in range(GH // 2):
@@ -423,6 +693,7 @@
         wide_skip = dot(skips, wide)[:1]
         x = x.astype(F32)
         dx_ref[:, at] = inner + wide_skip * mixed_grad
+        put.start(g)
         product = x * inner
         high, low = split(mixed_grad * (y_ref[:, at] - wide_skip * x) - product)
         flow_ref[...] += dot(high, wide, NT) + dot(low, wide, NT)
@@ -432,38 +703,51 @@
         skip_sum = skip_sum + dot(high, wide, NT) + dot(low, wide, NT)
         return gram_grad, skip_sum
 
-    gram_grad, skip_sum = lax.fori_loop(
-        0, GROUPS, group, (jnp.zeros(square, F32), jnp.zeros((16, TOK), F32))
-    )
+    gram_grad, skip_sum = each_group(group, (jnp.zeros(square, F32), jnp.zeros((16, TOK), F32)))
     skip_sum_ref[...] = skip_sum[:1]
     gram_grad = jnp.where(causal, gram_grad, 0.0).astype(BF16)
-    gout_ref[...] = (sum_ref[...] + dot(in_map, gram_grad, NT)).astype(BF16)
+    gout_ref[...] += dot(in_map, gram_grad, NT)
     gin_ref[...] = dot(map_in, gram_grad)
+    put.wait_all()
 
 
 def late_kernel(
-    x_ref,
-    raw_ref,
+    x_hbm,
+    decays_ref,
+    tail_ref,
     in_ref,
-    rate_ref,
-    bias_ref,
-    start_ref,
+    start_hbm,
     grad_ref,
-    dx_ref,
+    dx_hbm,
     flow_ref,
     direct_ref,
+    gout_ref,
     gin_ref,
-    skip_sum_ref,
+    skip_ref,
     gain_sum_ref,
-    gx_ref,
+    gx_hbm,
     gin_out_ref,
+    gout_out_ref,
     step_ref,
     sums_ref,
+    x_ref,
+    start_ref,
+    dx_ref,
+    gx_ref,
+    sem,
+    out_sem,
 ):
-    rate, bias = columns(rate_ref[...], bias_ref[...])
-    z, step, neg, running = decay_sums(raw_ref[...], bias, rate)
+    fetch = Copies(
+        sem,
+        (x_hbm, x_ref, by_lane),
+        (start_hbm, start_ref, by_row),
+        (dx_hbm, dx_ref, by_lane),
+    )
+    put = Copies(out_sem, (gx_ref, gx_hbm, by_lane))
+    fetch.start_all()
+    z, step, neg, running = (decays_ref[i] for i in range(4))
     last = running[:, TOK - 1 :]
-    tail = stacked_parts(jnp.exp(last - running) * step)
+    tail = tail_ref[...]
     in_rows = jnp.transpose(in_ref[...].astype(F32)).astype(BF16)
     tail_sum = jnp.zeros((TOK, TOK), F32)
     overlap = jnp.zeros((16, TOK), F32)
@@ -474,9 +758,11 @@
         grad = grad_ref[rows, :]
         wide = expander(g)
         weight = dot(tail, wide)
+        late = dot(in_rows, grad) * weight
+        fetch.wait(g)
         x = x_ref[:, at].astype(F32)
-        late = dot(in_rows, grad) * weight
         gx_ref[:, at] = (dx_ref[:, at] + late).astype(BF16)
+        put.start(g)
         gin = gin + dot(grad, (x * weight).astype(BF16), NT)
         high, low = split(x * late)
         tail_sum = tail_sum + dot(high, wide, NT) + dot(low, wide, NT)
@@ -484,6 +770,7 @@
         high, low = split(jnp.broadcast_to(both, (16, GW)))
         overlap = overlap + dot(high, wide, NT) + dot(low, wide, NT)
     gin_out_ref[...] = gin.astype(BF16)
+    gout_out_ref[...] = gout_ref[...].astype(BF16)
     tail_sum = jnp.transpose(tail_sum)[:SIZE]
     flow = jnp.transpose(flow_ref[...])[:SIZE]
     direct = jnp.transpose(direct_ref[...])[:SIZE]
@@ -498,9 +785,11 @@
     bias_grad = jnp.sum(raw_grad, axis=1, keepdims=True)
     both = jnp.concatenate([rate_grad, bias_grad], axis=0)
     devices = sums_ref.shape[0]
+    skip_sum = skip_ref[...]
     sums_ref[:, 0, 0:TOK] = jnp.transpose(jnp.broadcast_to(both, (TOK, TOK)))[:devices]
-    sums_ref[:, 0, TOK : 2 * TOK] = jnp.broadcast_to(skip_sum_ref[...], (devices, TOK))
+    sums_ref[:, 0, TOK : 2 * TOK] = jnp.broadcast_to(skip_sum, (devices, TOK))
     sums_ref[:, 0, 2 * TOK :] = jnp.broadcast_to(gain_sum_ref[...], (devices, TOK))
+    put.wait_all()
 
 
 def last_kernel(blocks, sums_ref, heads_ref, gain_ref):
@@ -513,29 +802,37 @@
     parts = gains.shape[0] // blocks
     gains = sum(gains[blocks * d : blocks * (d + 1)] for d in range(parts))
     for i in range(WIDTH // TOK):
-        gain_ref[:, TOK * i : TOK * (i + 1)] = gains[i : i + 1]
-
-
-def shape(dims, dtype):
-    return jax.ShapeDtypeStruct(dims, dtype)
+        gain_ref[pl.ds(TOK * i, TOK)] = gains[i]
 
 
 MIB = 1024 * 1024
+SMEM = pl.BlockSpec(memory_space=pltpu.SMEM)
 VMEM = pl.BlockSpec(memory_space=pltpu.VMEM)
-SMEM = pl.BlockSpec(memory_space=pltpu.SMEM)
-
-
-def call(kernel, outs, args, scratch=(), tables=(), mib=32, us=5):
-    single = not isinstance(outs, tuple)
+
+
+def call(kernel, args, outs, scratch=(), mib=32, us=5, aliases=None):
+    specs = {
+        "v": VMEM,
+        "h": pl.BlockSpec(memory_space=pltpu.HBM),
+        "a": VMEM,
+        "s": SMEM,
+    }
+    kept = {"v": pltpu.VMEM, "h": pltpu.HBM}
+    made = {"v": pltpu.VMEM, "h": pltpu.HBM, "a": jax.ShapeDtypeStruct}
+    arrays = [
+        pltpu.with_memory_space_constraint(array, kept[space]) if space in kept else array
+        for space, array in args
+    ]
     return pl.pallas_call(
         kernel,
-        out_shape=outs,
-        in_specs=[SMEM if i in tables else VMEM for i in range(len(args))],
-        out_specs=VMEM if single else (VMEM,) * len(outs),
+        out_shape=tuple(made[space](dims, dtype) for space, dims, dtype in outs),
+        in_specs=[specs[space] for space, _ in args],
+        out_specs=tuple(specs[space] for space, _, _ in outs),
         scratch_shapes=list(scratch),
+        input_output_aliases=aliases or {},
         compiler_params=pltpu.CompilerParams(vmem_limit_bytes=mib * MIB),
         cost_estimate=pl.CostEstimate(flops=int(us * 1e9), bytes_accessed=8 * MIB, transcendentals=0),
-    )(*args)
+    )(*arrays)
 
 
 def local(
@@ -553,108 +850,206 @@
     attn_keys,
     attn_grad,
 ):
-    x, raw, q, k = mamba_in[0], step_raw[0], queries[0], attn_keys[0]
+    x, raw, q, k, grad = mamba_in[0], step_raw[0], queries[0], attn_keys[0], attn_grad[0]
     in_map, map_in = jnp.transpose(state_in[0]), jnp.transpose(state_out[0])
-    lengths, moved = jnp.transpose(doc_lengths[0]), jnp.transpose(doc_moved[0])
+    tables = [("s", jnp.transpose(doc_lengths[0])), ("s", jnp.transpose(doc_moved[0]))]
     rate, bias, skip = log_rate[None], step_bias[None], skip_gain[None]
     blocks = lax.axis_size("ctx")
     devices = blocks * lax.axis_size("dp")
     rows = 8 * blocks
     swap = [(i, i ^ (blocks // 2)) for i in range(blocks)]
-    wide = (TOK, WIDTH)
-    decay_scratch = [pltpu.VMEM((GROUPS, TOK, TOK), F32), pltpu.VMEM((SIZE, TOK), F32)]
-    probs_shape = (GROUPS * AH, TOK, TOK)
+    wide, square, sent = (TOK, WIDTH), (TOK, TOK), (SEND, WIDTH)
+    maps, probs_shape = (SIZE, TOK), (GROUPS * AH, TOK, TOK)
+    message_shape, states_shape = (rows, GW + 128), (rows, GW)
+    decay_scratch = [pltpu.VMEM((GROUPS, TOK, TOK), F32), pltpu.VMEM(maps, F32)]
+
+    def vmem(dims, dtype=BF16):
+        return pltpu.VMEM(dims, dtype)
+
+    def sems(*dims):
+        return pltpu.SemaphoreType.DMA(dims)
 
     def exchange(value):
         value = value.reshape(blocks, 8, value.shape[1])
         value = lax.all_to_all(value, "ctx", 0, 0, tiled=True)
         return value.reshape(rows, value.shape[2])
 
-    back = lax.ppermute(attn_grad[0, TOK:], "ctx", swap)
-    message = call(
-        states_kernel, shape((rows, GW + 128), BF16), (x, raw, in_map, rate, bias), mib=8
+    decays_shape = (4, SIZE, TOK)
+    message, decays, tail = call(
+        states_kernel,
+        [("h", x), ("h", raw), ("h", in_map), ("h", rate), ("h", bias)],
+        [("h", message_shape, BF16), ("a", decays_shape, F32), ("a", square, BF16)],
+        [
+            vmem(wide),
+            vmem((HEADS, TOK), F32),
+            vmem(maps),
+            vmem((1, HEADS), F32),
+            vmem((1, HEADS), F32),
+            vmem(message_shape),
+            sems(1, GROUPS),
+            sems(4),
+            sems(1, GROUPS),
+        ],
+        us=3,
     )
     gathered = exchange(message)
-    wide_scratch = [pltpu.VMEM((rows, GW), F32)]
-    firsts = call(
+    probs, moving = call(
+        weights_kernel,
+        tables + [("h", q), ("h", k), ("h", grad)],
+        [("h", probs_shape, F32), ("h", sent, BF16)],
+        [
+            vmem(wide),
+            vmem(wide),
+            vmem(sent),
+            vmem(probs_shape, F32),
+            sems(2, GROUPS),
+            sems(1, GROUPS),
+            sems(2),
+        ],
+        us=5,
+    )
+    back = lax.ppermute(moving, "ctx", swap)
+    (firsts,) = call(
         functools.partial(scan_kernel, blocks, False),
-        shape((rows, GW), BF16),
-        (gathered,),
-        wide_scratch,
+        [("a", gathered)],
+        [("a", states_shape, BF16)],
+        [vmem(states_shape, F32)],
         mib=8,
         us=2,
     )
     start = exchange(firsts)
-    inner, probs = call(
+    decays, tail = ("a", decays), ("a", tail)
+    inner, grown, skips = call(
         inner_kernel,
-        (shape(wide, F32), shape(probs_shape, F32)),
-        (x, raw, in_map, map_in, rate, bias, skip, lengths, moved, q, k),
-        decay_scratch,
-        tables=(7, 8),
-        us=8,
+        [("h", x), decays, ("a", in_map), ("a", map_in), ("a", skip)],
+        [("h", wide, F32), ("a", square, BF16), ("a", (16, TOK), BF16)],
+        [vmem(wide), vmem(wide, F32)] + decay_scratch + [sems(1, GROUPS), sems(1, GROUPS)],
+        us=5,
     )
     gv, home = call(
         value_grad_kernel,
-        (shape(wide, BF16), shape(wide, BF16)),
-        (lengths, moved, probs, attn_grad[0], back),
-        tables=(0, 1),
-        us=5,
+        tables + [("h", probs), ("h", grad), ("h", back)],
+        [("h", wide, BF16), ("h", wide, BF16)],
+        [
+            vmem(probs_shape, F32),
+            vmem(wide),
+            vmem(sent),
+            vmem(wide),
+            vmem(wide),
+            sems(3, GROUPS),
+            sems(2, GROUPS),
+        ],
+        us=4,
     )
     y, values, low, message = call(
         norm_kernel,
-        (shape(wide, F32), shape(wide, BF16), shape(wide, BF16), shape((rows, GW + 128), BF16)),
-        (raw, map_in, rate, bias, norm_gain[None], start, inner, gv),
-        [pltpu.VMEM(wide, F32), pltpu.VMEM((32, TOK), F32)],
-        us=7,
-    )
-    attn, packed, gq, gk = call(
+        [
+            ("a", grown),
+            ("a", map_in),
+            ("a", norm_gain[None]),
+            ("a", start),
+            ("h", inner),
+            ("h", gv),
+        ],
+        [("h", wide, F32), ("h", wide, BF16), ("h", wide, BF16), ("h", message_shape, BF16)],
+        [
+            vmem(wide, F32),
+            vmem(wide),
+            vmem(wide, F32),
+            vmem(wide),
+            vmem(wide),
+            vmem(message_shape),
+            vmem(wide, F32),
+            vmem((32, TOK), F32),
+            sems(2, GROUPS),
+            sems(1, GROUPS),
+            sems(3, GROUPS),
+        ],
+        us=4,
+    )
+    attn, packed, dscores = call(
         attention_kernel,
-        (shape((TOK + SEND, WIDTH), BF16), shape((SEND, WIDTH), BF16), shape(wide, BF16), shape(wide, BF16)),
-        (lengths, moved, q, k, values, probs, home),
-        tables=(0, 1),
-        us=8,
+        tables + [("h", values), ("h", probs), ("h", home)],
+        [("h", (TOK + SEND, WIDTH), BF16), ("h", sent, BF16), ("h", probs_shape, BF16)],
+        [
+            vmem(wide),
+            vmem(probs_shape, F32),
+            vmem(wide),
+            vmem(wide),
+            vmem(sent),
+            vmem(probs_shape),
+            sems(3, GROUPS),
+            sems(3, GROUPS),
+        ],
+        us=5,
     )
     arrived = lax.ppermute(packed, "ctx", swap)
+    received = exchange(message)
     lasts, gain_sum = call(
         functools.partial(scan_kernel, blocks, True),
-        (shape((rows, GW), BF16), shape((1, TOK), F32)),
-        (exchange(message), gathered),
-        wide_scratch,
+        [("a", received), ("a", gathered)],
+        [("a", states_shape, BF16), ("a", (1, TOK), F32)],
+        [vmem(states_shape, F32)],
         mib=8,
         us=2,
     )
     state_grad = exchange(lasts)
-    dx, flow, direct, gout, gin, skip_sum = call(
+    dx, *partial = call(
         inner_back_kernel,
-        (
-            shape(wide, F32),
-            shape((TOK, TOK), F32),
-            shape((TOK, TOK), F32),
-            shape((SIZE, TOK), BF16),
-            shape((SIZE, TOK), F32),
-            shape((1, TOK), F32),
-        ),
-        (x, raw, in_map, map_in, rate, bias, skip, start, y, low),
-        decay_scratch + [pltpu.VMEM((SIZE, TOK), F32)],
+        [("h", x), decays, ("a", in_map), ("a", map_in), ("a", skips), ("a", grown)]
+        + [("h", start), ("h", y), ("h", low)],
+        [
+            ("h", wide, F32),
+            ("a", square, F32),
+            ("a", square, F32),
+            ("a", maps, F32),
+            ("a", maps, F32),
+            ("a", (1, TOK), F32),
+        ],
+        [vmem(wide), vmem(states_shape), vmem(wide, F32), vmem(wide), vmem(wide, F32)]
+        + decay_scratch
+        + [sems(4, GROUPS), sems(1, GROUPS)],
         us=8,
     )
-    gx, gin, gstep, sums = call(
+    gx, gin, gout, gstep, sums = call(
         late_kernel,
-        (
-            shape(wide, BF16),
-            shape((SIZE, TOK), BF16),
-            shape((HEADS, TOK), F32),
-            shape((devices, 1, 3 * TOK), F32),
-        ),
-        (x, raw, in_map, rate, bias, start, state_grad, dx, flow, direct, gin, skip_sum, gain_sum),
+        [("h", x), decays, tail, ("a", in_map), ("h", start)]
+        + [("a", state_grad), ("h", dx)]
+        + [("a", part) for part in partial]
+        + [("a", gain_sum)],
+        [
+            ("h", wide, BF16),
+            ("a", maps, BF16),
+            ("a", maps, BF16),
+            ("a", (HEADS, TOK), F32),
+            ("a", (devices, 1, 3 * TOK), F32),
+        ],
+        [vmem(wide), vmem(states_shape), vmem(wide, F32), vmem(wide), sems(3, GROUPS), sems(1, GROUPS)],
+        us=5,
+    )
+    sums = lax.all_to_all(sums, ("dp", "ctx"), 0, 0, tiled=True)
+    gq, gk, attn = call(
+        attention_grad_kernel,
+        [("h", q), ("h", k), ("h", dscores), ("h", arrived), ("h", attn)],
+        [("h", wide, BF16), ("h", wide, BF16), ("h", (TOK + SEND, WIDTH), BF16)],
+        [
+            vmem(wide),
+            vmem(wide),
+            vmem(probs_shape),
+            vmem(wide),
+            vmem(wide),
+            vmem(sent),
+            sems(3, GROUPS),
+            sems(2, GROUPS),
+            sems(2),
+        ],
         us=6,
-    )
-    sums = lax.all_to_all(sums, ("dp", "ctx"), 0, 0, tiled=True)
-    attn = lax.dynamic_update_slice(attn, arrived, (TOK, 0))
+        aliases={4: 2},
+    )
     heads, gain = call(
         functools.partial(last_kernel, blocks),
-        (shape((3, HEADS), F32), shape((1, WIDTH), F32)),
-        (sums,),
+        [("a", sums)],
+        [("a", (3, HEADS), F32), ("a", (WIDTH,), F32)],
         mib=4,
         us=1,
     )
@@ -667,7 +1062,7 @@
         jnp.transpose(gout)[None],
         gstep[None],
         heads,
-        gain[0],
+        gain,
     )
 
 

time: 120 us -> 102 us (0.85)
  local copies, waits for them, and re-layouts: 26.7 us -> 1.57 us
  Pallas kernels: 37.5 us -> 46.5 us
    unnamed x76 -> x18, local copies, waits for them, and re-layouts: 23 us -> 1.56 us
    pallas_call x10 -> x12, Pallas kernels: 37.5 us -> 46.5 us  [call(): pl.pallas_call(kernel, out_shape=tuple((made[space](dims, dtype) for spac...]
    all_to_all x1, waiting for transfers between devices: 8.71 us -> 5.56 us  [local(): sums = lax.all_to_all(sums, ('dp', 'ctx'), 0, 0, tiled=True)]
    all_to_all x4, waiting for transfers between devices: 9.75 us -> 12.5 us  [exchange(): value = lax.all_to_all(value, 'ctx', 0, 0, tiled=True)]
    all_to_all x4, starting transfers between devices: 19.6 us -> 21.6 us  [exchange(): value = lax.all_to_all(value, 'ctx', 0, 0, tiled=True)]
    dynamic_update_slice x1 -> x0, local copies, waits for them, and re-layouts: 1.82 us -> none  [local(): attn = lax.dynamic_update_slice(attn, arrived, (TOK, 0))]
    squeeze x1 -> x0, local copies, waits for them, and re-layouts: 1.82 us -> none  [local(): back = lax.ppermute(attn_grad[0, TOK:], 'ctx', swap)]
    all_to_all x1, starting transfers between devices: 8.83 us -> 7.13 us  [local(): sums = lax.all_to_all(sums, ('dp', 'ctx'), 0, 0, tiled=True)]
  transfers between devices with their start and end apart: 7 -> 7, of which waited for: 4 -> 5; matrix products, arithmetic and copies ran while one was open for 2% -> 0% of each run, Pallas kernels for 28% -> 37%
where the time goes in v3:
time: 102 us
  Pallas kernels  46.5 us (46%)
  starting transfers between devices  34.7 us (34%)
  waiting for transfers between devices  18 us (18%)
  local copies, waits for them, and re-layouts  1.57 us (2%)
    pallas_call x12, Pallas kernels, call(): pl.pallas_call(kernel, out_shape=tuple((made[space](dims, dtype) for spac...  46.5 us
    all_to_all x4, starting transfers between devices, exchange(): value = lax.all_to_all(value, 'ctx', 0, 0, tiled=True)  21.6 us
    all_to_all x4, waiting for transfers between devices, exchange(): value = lax.all_to_all(value, 'ctx', 0, 0, tiled=True)  12.5 us
    all_to_all x1, starting transfers between devices, local(): sums = lax.all_to_all(sums, ('dp', 'ctx'), 0, 0, tiled=True)  7.13 us
    all_to_all x1, waiting for transfers between devices, local(): sums = lax.all_to_all(sums, ('dp', 'ctx'), 0, 0, tiled=True)  5.56 us
    ppermute x1, starting transfers between devices, local(): back = lax.ppermute(moving, 'ctx', swap)  2.98 us
    ppermute x1, starting transfers between devices, local(): arrived = lax.ppermute(packed, 'ctx', swap)  2.98 us
  transfers between devices with their start and end apart: 7, of which 5 were waited for; matrix products, arithmetic and copies ran while one was open for 0% of the time, Pallas kernels for 37%

profile of v3, /device:TPU:1, one launch (start us, length us, event | category | flops | bytes accessed | tf_op | source)
XLA Modules:
  0.0 101.7 jit_solution(10878717408887242656)
XLA Ops:
  0.6 0.0 copy-start.3
  0.7 0.0 copy-start.4
  0.7 3.5 %shard_map.196 = (bf16[256,1024]{1,0:T(8,128)(2,1)}, f32[4,64,128]{2,1,0:T(8,128)S(1)}, bf16[128,128]{1,0:T(8,128)(2,1)S(1)}) custom-call(bf16[128,3584]{1,0:T(8,128)(2,1)} %bitcast.64, f32[56,128]{1,0:T(8,128)} %bitcast.72, bf16[64,128]{1,0:T(8,128)(2,1)} %bitcast.49, f32[1,56]{1,0:T(1,128)} %bitcast.73, f32[1,56]{1,0:T(1,128)} %bitcast.74), custom_call_target="tpu_custom_call" | custom-call | flops 3000000000 | bytes 8388608 | tf_op jit(solution)/shard_map/pallas_call | solution.py:826
  4.2 8.6 %all-to-all-start = ((bf16[32,8,1024]{2,1,0:T(8,128)(2,1)}), bf16[32,8,1024]{2,1,0:T(8,128)(2,1)S(1)}, u32[]{:S(2)}, u32[]{:S(2)}) async-start(bf16[32,8,1024]{2,1,0:T(8,128)(2,1)} %bitcast.61), calls=%async_computation | async-start | bytes 1048576 | tf_op jit(solution)/shard_map/all_to_all | solution.py:874
  12.8 0.0 copy-done.3
  12.8 0.0 copy-done.4
  12.8 4.9 %shard_map.199 = (f32[16,128,128]{2,1,0:T(8,128)}, bf16[64,3584]{1,0:T(8,128)(2,1)}) custom-call(s32[8,32]{1,0:T(8,128)S(1)} %bitcast.53, s32[8,32]{1,0:T(8,128)S(1)} %bitcast.56, bf16[128,3584]{1,0:T(8,128)(2,1)} %bitcast.68, bf16[128,3584]{1,0:T(8,128)(2,1)} %bitcast.70, bf16[192,3584]{1,0:T(8,128)(2,1)} %bitcast.62), custom_call_target="tpu_custom_call" | custom-call | flops 5000000000 | bytes 8388608 | tf_op jit(solution)/shard_map/pallas_call | solution.py:826
  17.8 3.0 %collective-permute-start = (bf16[64,3584]{1,0:T(8,128)(2,1)}, bf16[64,3584]{1,0:T(8,128)(2,1)S(1)}, u32[]{:S(2)}, u32[]{:S(2)}) collective-permute-start(bf16[64,3584]{1,0:T(8,128)(2,1)} %get-tuple-element.49), channel_id=1, source_target_pairs={{0,16},{1,17},{2,18},{3,19},{4,20},{5,21},{6,22},{7,23},{8,24},{9,... | collective-permute-start | bytes 1376264 | tf_op jit(solution)/shard_map/ppermute | solution.py:911
  20.8 3.7 %all-to-all-done = bf16[32,8,1024]{2,1,0:T(8,128)(2,1)S(1)} async-done(((bf16[32,8,1024]{2,1,0:T(8,128)(2,1)}), bf16[32,8,1024]{2,1,0:T(8,128)(2,1)S(1)}, u32[]{:S(2)}, u32[]{:S(2)}) %all-to-all-start) | async-done | bytes 524320 | tf_op jit(solution)/shard_map/all_to_all | solution.py:874
  24.4 0.0 copy-start.1
  24.5 0.0 copy-start.2
  24.5 0.0 copy-start.5
  24.5 1.1 %shard_map.198 = bf16[256,896]{1,0:T(8,128)(2,1)} custom-call(bf16[256,1024]{1,0:T(8,128)(2,1)S(1)} %bitcast.39), custom_call_target="tpu_custom_call" | custom-call | flops 2000000000 | bytes 8388608 | tf_op jit(solution)/shard_map/pallas_call | solution.py:826
  25.5 3.7 %all-to-all-start.1 = ((bf16[32,8,896]{2,1,0:T(8,128)(2,1)}), bf16[32,8,896]{2,1,0:T(8,128)(2,1)S(1)}, u32[]{:S(2)}, u32[]{:S(2)}) async-start(bf16[32,8,896]{2,1,0:T(8,128)(2,1)} %bitcast.17), calls=%async_computation.1 | async-start | bytes 917504 | tf_op jit(solution)/shard_map/all_to_all | solution.py:874
  29.2 0.0 copy-done.1
  29.2 0.0 copy-done.2
  29.2 0.0 copy-done.5
  29.2 0.0 copy-start.6
  29.3 4.0 %shard_map.197 = (f32[128,3584]{1,0:T(8,128)}, bf16[128,128]{1,0:T(8,128)(2,1)S(1)}, bf16[16,128]{1,0:T(8,128)(2,1)S(1)}) custom-call(bf16[128,3584]{1,0:T(8,128)(2,1)} %bitcast.65, f32[4,64,128]{2,1,0:T(8,128)S(1)} %get-tuple-element.44.decays_ref, bf16[64,128]{1,0:T(8,128)(2,1)S(1)} %bitcast.50, bf16[64,128]{1,0:T(8,128)(2,1)S(1)} %bitcast.46, ...), custom_call_target="tpu_custom_call" | custom-call | flops 5000000000 | bytes 8388608 | tf_op jit(solution)/shard_map/pallas_call | solution.py:826
  33.2 0.0 copy-done.6
  33.3 0.0 collective-permute-done.back_hbm
  33.3 0.0 copy-start.8
  33.3 0.8 copy-done.8
  34.0 4.4 %shard_map.200 = (bf16[128,3584]{1,0:T(8,128)(2,1)}, bf16[128,3584]{1,0:T(8,128)(2,1)}) custom-call(s32[8,32]{1,0:T(8,128)S(1)} %bitcast.54, s32[8,32]{1,0:T(8,128)S(1)} %bitcast.57, f32[16,128,128]{2,1,0:T(8,128)} %get-tuple-element.48.probs_hbm, bf16[192,3584]{1,0:T(8,128)(2,1)} %bitcast.63, bf16[64,3584]{1,0:T(8,128)(2,1)} %copy-done.8), custom_call_target="tpu_custom_call" | custom-call | flops 4000000000 | bytes 8388608 | tf_op jit(solution)/shard_map/pallas_call | solution.py:826
  38.4 1.7 %all-to-all-done.1 = bf16[32,8,896]{2,1,0:T(8,128)(2,1)S(1)} async-done(((bf16[32,8,896]{2,1,0:T(8,128)(2,1)}), bf16[32,8,896]{2,1,0:T(8,128)(2,1)S(1)}, u32[]{:S(2)}, u32[]{:S(2)}) %all-to-all-start.1) | async-done | bytes 458784 | tf_op jit(solution)/shard_map/all_to_all | solution.py:874
  40.1 0.0 copy-start
  40.1 4.5 %shard_map.201 = (f32[128,3584]{1,0:T(8,128)}, bf16[128,3584]{1,0:T(8,128)(2,1)}, bf16[128,3584]{1,0:T(8,128)(2,1)}, bf16[256,1024]{1,0:T(8,128)(2,1)}) custom-call(bf16[128,128]{1,0:T(8,128)(2,1)S(1)} %get-tuple-element.45.grown_ref, bf16[64,128]{1,0:T(8,128)(2,1)S(1)} %bitcast.47, f32[1,3584]{1,0:T(1,128)S(1)} %broadcast_in_dim.36.gain_ref, ...), custom_call_target="tpu_custom_call" | custom-call | flops 4000000000 | bytes 8388608 | tf_op jit(solution)/shard_map/pallas_call | solution.py:826
  44.6 0.0 copy-done
  44.6 5.7 %all-to-all-start.2 = ((bf16[32,8,1024]{2,1,0:T(8,128)(2,1)}), bf16[32,8,1024]{2,1,0:T(8,128)(2,1)S(1)}, u32[]{:S(2)}, u32[]{:S(2)}) async-start(bf16[32,8,1024]{2,1,0:T(8,128)(2,1)} %bitcast.60), calls=%async_computation.2 | async-start | bytes 1048576 | tf_op jit(solution)/shard_map/all_to_all | solution.py:874
  50.3 4.7 %shard_map.202 = (bf16[192,3584]{1,0:T(8,128)(2,1)}, bf16[64,3584]{1,0:T(8,128)(2,1)}, bf16[16,128,128]{2,1,0:T(8,128)(2,1)}) custom-call(s32[8,32]{1,0:T(8,128)S(1)} %bitcast.55, s32[8,32]{1,0:T(8,128)S(1)} %bitcast.58, bf16[128,3584]{1,0:T(8,128)(2,1)} %get-tuple-element.51.values_hbm, f32[16,128,128]{2,1,0:T(8,128)} %get-tuple-element.48.probs_hbm, ...), custom_call_target="tpu_custom_call" | custom-call | flops 5000000000 | bytes 8388608 | tf_op jit(solution)/shard_map/pallas_call | solution.py:826
  55.0 3.0 %collective-permute-start.1 = (bf16[64,3584]{1,0:T(8,128)(2,1)}, bf16[64,3584]{1,0:T(8,128)(2,1)S(1)}, u32[]{:S(2)}, u32[]{:S(2)}) collective-permute-start(bf16[64,3584]{1,0:T(8,128)(2,1)} %get-tuple-element.54), channel_id=1, source_target_pairs={{0,16},{1,17},{2,18},{3,19},{4,20},{5,21},{6,22},{7,23},{8,24},{9,... | collective-permute-start | bytes 1376264 | tf_op jit(solution)/shard_map/ppermute | solution.py:986
  58.0 3.9 %all-to-all-done.2 = bf16[32,8,1024]{2,1,0:T(8,128)(2,1)S(1)} async-done(((bf16[32,8,1024]{2,1,0:T(8,128)(2,1)}), bf16[32,8,1024]{2,1,0:T(8,128)(2,1)S(1)}, u32[]{:S(2)}, u32[]{:S(2)}) %all-to-all-start.2) | async-done | bytes 524320 | tf_op jit(solution)/shard_map/all_to_all | solution.py:874
  61.9 1.2 %shard_map.204 = (bf16[256,896]{1,0:T(8,128)(2,1)}, f32[1,128]{1,0:T(1,128)S(1)}) custom-call(bf16[256,1024]{1,0:T(8,128)(2,1)S(1)} %bitcast.41, bf16[256,1024]{1,0:T(8,128)(2,1)S(1)} %bitcast.40), custom_call_target="tpu_custom_call" | custom-call | flops 2000000000 | bytes 8388608 | tf_op jit(solution)/shard_map/pallas_call | solution.py:826
  63.1 3.7 %all-to-all-start.3 = ((bf16[32,8,896]{2,1,0:T(8,128)(2,1)}), bf16[32,8,896]{2,1,0:T(8,128)(2,1)S(1)}, u32[]{:S(2)}, u32[]{:S(2)}) async-start(bf16[32,8,896]{2,1,0:T(8,128)(2,1)} %bitcast.28), calls=%async_computation.3 | async-start | bytes 917504 | tf_op jit(solution)/shard_map/all_to_all | solution.py:874
  66.7 7.7 %shard_map.205 = (f32[128,3584]{1,0:T(8,128)}, f32[128,128]{1,0:T(8,128)S(1)}, f32[128,128]{1,0:T(8,128)S(1)}, f32[64,128]{1,0:T(8,128)S(1)}, f32[64,128]{1,0:T(8,128)S(1)}, /*index=5*/f32[1,128]{1,0:T(1,128)S(1)}) custom-call(bf16[128,3584]{1,0:T(8,128)(2,1)} %bitcast.66, f32[4,64,128]{2,1,0:T(8,128)S(1)} %get-tuple-element.44.decays_ref, ...), custom_call_target="tpu_custom_call" | custom-call | flops 8000000000 | bytes 8388608 | tf_op jit(solution)/shard_map/pallas_call | solution.py:826
  74.5 3.2 %all-to-all-done.3 = bf16[32,8,896]{2,1,0:T(8,128)(2,1)S(1)} async-done(((bf16[32,8,896]{2,1,0:T(8,128)(2,1)}), bf16[32,8,896]{2,1,0:T(8,128)(2,1)S(1)}, u32[]{:S(2)}, u32[]{:S(2)}) %all-to-all-start.3) | async-done | bytes 458784 | tf_op jit(solution)/shard_map/all_to_all | solution.py:874
  77.7 5.6 %shard_map.206 = (bf16[128,3584]{1,0:T(8,128)(2,1)}, bf16[64,128]{1,0:T(8,128)(2,1)}, bf16[64,128]{1,0:T(8,128)(2,1)}, f32[56,128]{1,0:T(8,128)}, f32[128,1,384]{2,1,0:T(1,128)}) custom-call(bf16[128,3584]{1,0:T(8,128)(2,1)} %bitcast.67, f32[4,64,128]{2,1,0:T(8,128)S(1)} %get-tuple-element.44.decays_ref, bf16[128,128]{1,0:T(8,128)(2,1)S(1)} %get-tuple-element.59.tail_ref, ...), custom_call_target="tpu_custom_call" | custom-call | flops 5000000000 | bytes 8388608 | tf_op jit(solution)/shard_map/pallas_call | solution.py:826
  83.3 7.1 %all-to-all-start.4 = ((f32[128,1,384]{2,1,0:T(1,128)}), f32[128,1,384]{2,1,0:T(1,128)S(1)}, u32[]{:S(2)}, u32[]{:S(2)}) async-start(f32[128,1,384]{2,1,0:T(1,128)} %get-tuple-element.76), calls=%async_computation.4 | async-start | bytes 393216 | tf_op jit(solution)/shard_map/all_to_all | solution.py:1030
  90.4 0.0 collective-permute-done.1.arrived_hbm
  90.4 0.0 copy-start.7
  90.5 0.8 copy-done.7
  91.2 4.2 %shard_map.203 = (bf16[128,3584]{1,0:T(8,128)(2,1)}, bf16[128,3584]{1,0:T(8,128)(2,1)}, bf16[192,3584]{1,0:T(8,128)(2,1)}) custom-call(bf16[128,3584]{1,0:T(8,128)(2,1)} %bitcast.69, bf16[128,3584]{1,0:T(8,128)(2,1)} %bitcast.71, bf16[16,128,128]{2,1,0:T(8,128)(2,1)} %get-tuple-element.53.dscores_hbm, ...), custom_call_target="tpu_custom_call", output_to_operand_aliasing={{2}: (4, {})} | custom-call | flops 6000000000 | bytes 8388608 | tf_op jit(solution)/shard_map/pallas_call | solution.py:826
  95.4 5.6 %all-to-all-done.4.sums_ref = f32[128,1,384]{2,1,0:T(1,128)S(1)} async-done(((f32[128,1,384]{2,1,0:T(1,128)}), f32[128,1,384]{2,1,0:T(1,128)S(1)}, u32[]{:S(2)}, u32[]{:S(2)}) %all-to-all-start.4) | async-done | bytes 196640 | tf_op jit(solution)/shard_map/all_to_all | solution.py:1030
  101.0 0.7 shard_map.207
  (1 shorter events, 0.0 us)
Async XLA Ops:
  0.6 12.2 %copy-start.3 = (s32[1,32,8]{1,2,0:T(8,128)S(1)}, s32[1,32,8]{1,2,0:T(8,128)}, u32[]{:S(2)}) copy-start(s32[1,32,8]{1,2,0:T(8,128)} %param.21) | copy-start | bytes 3076
  0.7 12.2 %copy-start.4 = (s32[1,32,8]{1,2,0:T(8,128)S(1)}, s32[1,32,8]{1,2,0:T(8,128)}, u32[]{:S(2)}) copy-start(s32[1,32,8]{1,2,0:T(8,128)} %param.22) | copy-start | bytes 3076
  4.2 20.2 %all-to-all-start = ((bf16[32,8,1024]{2,1,0:T(8,128)(2,1)}), bf16[32,8,1024]{2,1,0:T(8,128)(2,1)S(1)}, u32[]{:S(2)}, u32[]{:S(2)}) async-start(bf16[32,8,1024]{2,1,0:T(8,128)(2,1)} %bitcast.61), calls=%async_computation | async-start | bytes 1048576 | tf_op jit(solution)/shard_map/all_to_all | solution.py:874
  17.8 15.5 %collective-permute-start = (bf16[64,3584]{1,0:T(8,128)(2,1)}, bf16[64,3584]{1,0:T(8,128)(2,1)S(1)}, u32[]{:S(2)}, u32[]{:S(2)}) collective-permute-start(bf16[64,3584]{1,0:T(8,128)(2,1)} %get-tuple-element.49), channel_id=1, source_target_pairs={{0,16},{1,17},{2,18},{3,19},{4,20},{5,21},{6,22},{7,23},{8,24},{9,... | collective-permute-start | bytes 1376264 | tf_op jit(solution)/shard_map/ppermute | solution.py:911
  24.4 4.8 %copy-start.1 = (bf16[1,128,64]{1,2,0:T(8,128)(2,1)S(1)}, bf16[1,128,64]{1,2,0:T(8,128)(2,1)}, u32[]{:S(2)}) copy-start(bf16[1,128,64]{1,2,0:T(8,128)(2,1)} %param.16) | copy-start | bytes 49156
  24.5 4.8 %copy-start.2 = (bf16[1,128,64]{1,2,0:T(8,128)(2,1)S(1)}, bf16[1,128,64]{1,2,0:T(8,128)(2,1)}, u32[]{:S(2)}) copy-start(bf16[1,128,64]{1,2,0:T(8,128)(2,1)} %param.15) | copy-start | bytes 49156
  24.5 4.8 %copy-start.5 = (f32[56]{0:T(128)S(1)}, f32[56]{0:T(128)}, u32[]{:S(2)}) copy-start(f32[56]{0:T(128)} %param.19) | copy-start | bytes 676
  25.5 14.6 %all-to-all-start.1 = ((bf16[32,8,896]{2,1,0:T(8,128)(2,1)}), bf16[32,8,896]{2,1,0:T(8,128)(2,1)S(1)}, u32[]{:S(2)}, u32[]{:S(2)}) async-start(bf16[32,8,896]{2,1,0:T(8,128)(2,1)} %bitcast.17), calls=%async_computation.1 | async-start | bytes 917504 | tf_op jit(solution)/shard_map/all_to_all | solution.py:874
  29.2 4.0 %copy-start.6 = (f32[3584]{0:T(1024)S(1)}, f32[3584]{0:T(1024)}, u32[]{:S(2)}) copy-start(f32[3584]{0:T(1024)} %param.20) | copy-start | bytes 43012
  33.3 0.8 copy-start.8
  40.1 4.5 %copy-start = (bf16[32,8,896]{2,1,0:T(8,128)(2,1)}, bf16[32,8,896]{2,1,0:T(8,128)(2,1)S(1)}, u32[]{:S(2)}) copy-start(bf16[32,8,896]{2,1,0:T(8,128)(2,1)S(1)} %all-to-all-done.1) | copy-start | bytes 1376260
  44.6 17.3 %all-to-all-start.2 = ((bf16[32,8,1024]{2,1,0:T(8,128)(2,1)}), bf16[32,8,1024]{2,1,0:T(8,128)(2,1)S(1)}, u32[]{:S(2)}, u32[]{:S(2)}) async-start(bf16[32,8,1024]{2,1,0:T(8,128)(2,1)} %bitcast.60), calls=%async_computation.2 | async-start | bytes 1048576 | tf_op jit(solution)/shard_map/all_to_all | solution.py:874
  55.0 35.4 %collective-permute-start.1 = (bf16[64,3584]{1,0:T(8,128)(2,1)}, bf16[64,3584]{1,0:T(8,128)(2,1)S(1)}, u32[]{:S(2)}, u32[]{:S(2)}) collective-permute-start(bf16[64,3584]{1,0:T(8,128)(2,1)} %get-tuple-element.54), channel_id=1, source_target_pairs={{0,16},{1,17},{2,18},{3,19},{4,20},{5,21},{6,22},{7,23},{8,24},{9,... | collective-permute-start | bytes 1376264 | tf_op jit(solution)/shard_map/ppermute | solution.py:986
  63.1 14.6 %all-to-all-start.3 = ((bf16[32,8,896]{2,1,0:T(8,128)(2,1)}), bf16[32,8,896]{2,1,0:T(8,128)(2,1)S(1)}, u32[]{:S(2)}, u32[]{:S(2)}) async-start(bf16[32,8,896]{2,1,0:T(8,128)(2,1)} %bitcast.28), calls=%async_computation.3 | async-start | bytes 917504 | tf_op jit(solution)/shard_map/all_to_all | solution.py:874
  83.3 17.7 %all-to-all-start.4 = ((f32[128,1,384]{2,1,0:T(1,128)}), f32[128,1,384]{2,1,0:T(1,128)S(1)}, u32[]{:S(2)}, u32[]{:S(2)}) async-start(f32[128,1,384]{2,1,0:T(1,128)} %get-tuple-element.76), calls=%async_computation.4 | async-start | bytes 393216 | tf_op jit(solution)/shard_map/all_to_all | solution.py:1030
  90.4 0.8 copy-start.7

commit v4 on v3

--- a/solution.py
+++ b/solution.py
@@ -10,7 +10,6 @@
 
 F32 = jnp.float32
 BF16 = jnp.bfloat16
-HIGH = lax.Precision.HIGHEST
 EPSILON = 1e-05
 MASKED = -1e30
 
@@ -75,41 +74,51 @@
     return jnp.transpose(jnp.concatenate([high.astype(F32), low.astype(F32)], axis=0)).astype(BF16)
 
 
+def sums_by(value, chosen):
+    high, low = split(value)
+    lowest = (value - high.astype(F32) - low.astype(F32)).astype(BF16)
+    ones = jnp.where(chosen, 1.0, 0.0).astype(BF16)
+    return dot(jnp.concatenate([high, low, lowest], axis=1), jnp.concatenate([ones] * 3, axis=0))
+
+
 def decay_sums(raw, bias, rate):
     z = pad_heads(raw) + bias
     step = jnp.maximum(z, 0.0) + jnp.log1p(jnp.exp(-jnp.abs(z)))
     neg = -jnp.exp(rate)
-    tri = jnp.where(iota((TOK, TOK), 0) <= iota((TOK, TOK), 1), 1.0, 0.0)
-    running = dot(neg * step, tri, precision=HIGH)
+    running = sums_by(neg * step, iota((TOK, TOK), 0) <= iota((TOK, TOK), 1))
     return z, step, neg, running
 
 
-def chunk(g, size):
-    return pl.ds(g * size if isinstance(g, int) else pl.multiple_of(g * size, size), size)
-
-
-def lanes(g):
-    return chunk(g, GW)
-
-
-def rows64(g):
-    return chunk(g, SIZE)
-
-
-def by_lane(ref, g):
-    return ref.at[:, lanes(g)]
-
-
-def by_lane_top(ref, g):
-    return ref.at[pl.ds(0, TOK), lanes(g)]
-
-
-def by_row(ref, g):
-    return ref.at[rows64(g), :]
-
-
-def by_head(ref, g):
-    return ref.at[pl.ds(AH * g, AH)]
+def chunk(g, size, groups=1):
+    return pl.ds(g * size, groups * size)
+
+
+def lanes(g, groups=1):
+    return chunk(g, GW, groups)
+
+
+def rows64(g, groups=1):
+    return chunk(g, SIZE, groups)
+
+
+def by_lane(ref, g, groups):
+    return ref.at[:, lanes(g, groups)]
+
+
+def by_lane_top(ref, g, groups):
+    return ref.at[pl.ds(0, TOK), lanes(g, groups)]
+
+
+def by_row(ref, g, groups):
+    return ref.at[rows64(g, groups), :]
+
+
+def by_state_row(ref, g, groups):
+    return ref.at[rows64(g, groups), pl.ds(0, GW)]
+
+
+def by_head(ref, g, groups):
+    return ref.at[chunk(g, AH, groups)]
 
 
 def each_group(body, carry):
@@ -119,32 +128,33 @@
 
 
 class Copies:
-    def __init__(self, sem, *pairs):
-        self.sem, self.pairs = sem, pairs
+    def __init__(self, sem, *pairs, span=1):
+        self.sem, self.pairs, self.span = sem, pairs, span
 
     def parts(self, g):
         made = []
         for i, (source, target, view, *other) in enumerate(self.pairs):
             view_to = other[0] if other else view
-            made.append(
-                pltpu.make_async_copy(view(source, g), view_to(target, g), self.sem.at[i, g])
-            )
+            source, target = view(source, g, self.span), view_to(target, g, self.span)
+            made.append(pltpu.make_async_copy(source, target, self.sem.at[i, g]))
         return made
 
     def start(self, g):
-        for copy in self.parts(g):
-            copy.start()
+        if (g + 1) % self.span == 0:
+            for copy in self.parts(g + 1 - self.span):
+                copy.start()
 
     def wait(self, g):
-        for copy in self.parts(g):
-            copy.wait()
-
-    def start_all(self, groups=range(GROUPS)):
-        for g in groups:
+        if g % self.span == 0:
+            for copy in self.parts(g):
+                copy.wait()
+
+    def start_all(self):
+        for g in range(GROUPS):
             self.start(g)
 
-    def wait_all(self, groups=range(GROUPS)):
-        for g in groups:
+    def wait_all(self):
+        for g in range(GROUPS):
             self.wait(g)
 
 
@@ -175,7 +185,7 @@
     ]
     for copy in smalls:
         copy.start()
-    fetch = Copies(sem, (x_hbm, x_ref, by_lane))
+    fetch = Copies(sem, (x_hbm, x_ref, by_lane), span=4)
     fetch.start_all()
     put = Copies(out_sem, (out_ref, out_hbm, by_row))
     for copy in smalls:
@@ -205,10 +215,10 @@
         ones = jnp.ones((16, 8 * blocks), BF16)
         sum_ref[...] = dot(ones, carry_ref[:, GW:])[:1]
     else:
-        carry_ref, out_ref, wide_ref = refs
-        total_ref = carry_ref
+        carry_ref, out_ref, total_ref, wide_ref = refs
+        total_ref[...] = carry_ref[:, GW:]
     group = lax.axis_index("ctx") // 8
-    wide_ref[...] = dot(total_ref[:, GW:], expander(group))
+    wide_ref[...] = dot(total_ref[...], expander(group))
     state = jnp.zeros((8, GW), F32)
     pairs = range(blocks // 2)
     for i in reversed(pairs) if reverse else pairs:
@@ -281,18 +291,15 @@
     in_ref,
     map_ref,
     skip_ref,
-    y_hbm,
+    y_ref,
     grown_ref,
     skips_ref,
     x_ref,
-    y_ref,
     column_ref,
     row_ref,
     sem,
-    out_sem,
 ):
-    fetch = Copies(sem, (x_hbm, x_ref, by_lane))
-    put = Copies(out_sem, (y_ref, y_hbm, by_lane))
+    fetch = Copies(sem, (x_hbm, x_ref, by_lane), span=2)
     fetch.start_all()
     square = (TOK, TOK)
     (skip,) = columns(skip_ref[...])
@@ -318,11 +325,9 @@
             rows = pair_rows(x[:, 128 * i : 128 * (i + 1)])
             inner.append(dot(jnp.concatenate(pair, axis=1), rows))
         y_ref[:, at] = jnp.concatenate(inner, axis=1) + dot(skips, expander(g))[:1] * x.astype(F32)
-        put.start(g)
         return carry
 
     each_group(group, 0)
-    put.wait_all()
 
 
 def weights_kernel(
@@ -341,7 +346,7 @@
     out_sem,
     moved_sem,
 ):
-    fetch = Copies(sem, (q_hbm, q_ref, by_lane), (k_hbm, k_ref, by_lane))
+    fetch = Copies(sem, (q_hbm, q_ref, by_lane), (k_hbm, k_ref, by_lane), span=4)
     put = Copies(out_sem, (probs_ref, probs_hbm, by_head))
     arrive = pltpu.make_async_copy(grad_hbm.at[pl.ds(TOK, SEND), :], rows_ref, moved_sem.at[0])
     leave = pltpu.make_async_copy(rows_ref, moved_hbm, moved_sem.at[1])
@@ -385,12 +390,11 @@
     moved_ref,
     probs_hbm,
     grad_hbm,
-    back_hbm,
+    back_ref,
     gv_hbm,
     home_hbm,
     probs_ref,
     grad_ref,
-    back_ref,
     gv_ref,
     home_ref,
     sem,
@@ -398,9 +402,9 @@
 ):
     fetch = Copies(
         sem,
-        (back_hbm, back_ref, by_lane),
         (grad_hbm, grad_ref, by_lane_top, by_lane),
         (probs_hbm, probs_ref, by_head),
+        span=4,
     )
     put = Copies(out_sem, (gv_ref, gv_hbm, by_lane), (home_ref, home_hbm, by_lane))
     fetch.start_all()
@@ -433,13 +437,12 @@
     map_ref,
     gain_ref,
     start_ref,
-    inner_hbm,
+    inner_ref,
     gv_hbm,
     y_hbm,
     values_hbm,
     low_hbm,
     message_hbm,
-    inner_ref,
     gv_ref,
     y_ref,
     values_ref,
@@ -450,9 +453,11 @@
     sem,
     y_sem,
     out_sem,
+    message_sem,
 ):
-    fetch = Copies(sem, (inner_hbm, inner_ref, by_lane), (gv_hbm, gv_ref, by_lane))
+    fetch = Copies(sem, (gv_hbm, gv_ref, by_lane), span=4)
     put_y = Copies(y_sem, (y_ref, y_hbm, by_lane))
+    put_message = Copies(message_sem, (message_ref, message_hbm, by_state_row))
     put = Copies(out_sem, (values_ref, values_hbm, by_lane), (low_ref, low_hbm, by_lane))
     fetch.start_all()
     grown = grown_ref[...]
@@ -465,13 +470,15 @@
         wide = dot(grown, expander(g))
         wide_ref[:, at] = wide
         carried = dot(out_rows, start_ref[g * SIZE : (g + 1) * SIZE, :]) * wide
-        fetch.wait(g)
         y = inner_ref[:, at] + carried
         y_ref[:, at] = y
         put_y.start(g)
         power = power + jnp.sum(y * y, axis=-1, keepdims=True)
+    for g in range(GROUPS):
+        at = slice(g * GW, (g + 1) * GW)
+        fetch.wait(g)
         scaled = gv_ref[:, at].astype(F32) * gain_ref[:, at]
-        along = along + jnp.sum(scaled * y, axis=-1, keepdims=True)
+        along = along + jnp.sum(scaled * y_ref[:, at], axis=-1, keepdims=True)
     inverse = lax.rsqrt(power * (1.0 / WIDTH) + EPSILON)
     slope = inverse * inverse * inverse * along * (1.0 / WIDTH)
     sums_ref[...] = jnp.zeros_like(sums_ref)
@@ -489,6 +496,7 @@
         put.start(g)
         grown_grad = (wide_ref[:, at] * mixed_grad).astype(BF16)
         message_ref[rows, :GW] = dot(map_in, grown_grad).astype(BF16)
+        put_message.start(g)
     sums = sums_ref[...]
     high, low = split(sums)
     lowest = (sums - high.astype(F32) - low.astype(F32)).astype(BF16)
@@ -496,10 +504,14 @@
     at, source = iota(dims, 0), iota(dims, 1)
     spread = jnp.where((at >> 3 == source & 31) & (at & 7 == source >> 5), 1.0, 0.0).astype(BF16)
     message_ref[:, GW:] = dot(spread, jnp.concatenate([high, low, lowest], axis=0)).astype(BF16)
-    last = pltpu.make_async_copy(message_ref, message_hbm, out_sem.at[2, 0])
+    sums_at = (slice(None), pl.ds(GW, TOK))
+    last = pltpu.make_async_copy(
+        message_ref.at[sums_at], message_hbm.at[sums_at], message_sem.at[1, 0]
+    )
     last.start()
     put_y.wait_all()
     put.wait_all()
+    put_message.wait_all()
     last.wait()
 
 
@@ -565,10 +577,11 @@
 
 
 def attention_grad_kernel(
+    after_ref,
     q_hbm,
     k_hbm,
     dscores_hbm,
-    arrived_hbm,
+    arrived_ref,
     attn_in_hbm,
     gq_hbm,
     gk_hbm,
@@ -578,27 +591,24 @@
     dscores_ref,
     gq_ref,
     gk_ref,
-    rows_ref,
     sem,
     out_sem,
     arrived_sem,
 ):
     del attn_in_hbm
+    del after_ref
     fetch = Copies(
         sem,
         (dscores_hbm, dscores_ref, by_head),
         (k_hbm, k_ref, by_lane),
         (q_hbm, q_ref, by_lane),
+        span=2,
     )
     put = Copies(out_sem, (gq_ref, gq_hbm, by_lane), (gk_ref, gk_hbm, by_lane))
     fetch.start_all()
-    arrive = pltpu.make_async_copy(arrived_hbm, rows_ref, arrived_sem.at[0])
-    leave = pltpu.make_async_copy(rows_ref, attn_hbm.at[pl.ds(TOK, SEND), :], arrived_sem.at[1])
-    arrive.start()
+    leave = pltpu.make_async_copy(arrived_ref, attn_hbm.at[pl.ds(TOK, SEND), :], arrived_sem)
+    leave.start()
     masks = lane_masks()
-
-    arrive.wait()
-    leave.start()
 
     def group(g, carry):
         at = lanes(g)
@@ -621,6 +631,7 @@
 
 
 def inner_back_kernel(
+    after_ref,
     x_hbm,
     decays_ref,
     in_ref,
@@ -646,14 +657,16 @@
     sem,
     out_sem,
 ):
+    del after_ref
     fetch = Copies(
         sem,
         (low_hbm, low_ref, by_lane),
         (x_hbm, x_ref, by_lane),
         (start_hbm, start_ref, by_row),
         (y_hbm, y_ref, by_lane),
-    )
-    put = Copies(out_sem, (dx_ref, dx_hbm, by_lane))
+        span=2,
+    )
+    put = Copies(out_sem, (dx_ref, dx_hbm, by_lane), span=2)
     fetch.start_all()
     square = (TOK, TOK)
     causal = iota(square, 0) >= iota(square, 1)
@@ -712,71 +725,44 @@
 
 
 def late_kernel(
-    x_hbm,
+    x_ref,
     decays_ref,
     tail_ref,
     in_ref,
-    start_hbm,
+    start_ref,
     grad_ref,
-    dx_hbm,
     flow_ref,
     direct_ref,
-    gout_ref,
-    gin_ref,
     skip_ref,
     gain_sum_ref,
-    gx_hbm,
-    gin_out_ref,
-    gout_out_ref,
     step_ref,
     sums_ref,
-    x_ref,
-    start_ref,
-    dx_ref,
-    gx_ref,
-    sem,
-    out_sem,
 ):
-    fetch = Copies(
-        sem,
-        (x_hbm, x_ref, by_lane),
-        (start_hbm, start_ref, by_row),
-        (dx_hbm, dx_ref, by_lane),
-    )
-    put = Copies(out_sem, (gx_ref, gx_hbm, by_lane))
-    fetch.start_all()
     z, step, neg, running = (decays_ref[i] for i in range(4))
     last = running[:, TOK - 1 :]
     tail = tail_ref[...]
     in_rows = jnp.transpose(in_ref[...].astype(F32)).astype(BF16)
     tail_sum = jnp.zeros((TOK, TOK), F32)
     overlap = jnp.zeros((16, TOK), F32)
-    gin = gin_ref[...]
+    lates = []
+    for g in range(GROUPS):
+        grad = grad_ref[g * SIZE : (g + 1) * SIZE, :]
+        lates.append(dot(in_rows, grad) * dot(tail, expander(g)))
     for g in range(GROUPS):
         at = slice(g * GW, (g + 1) * GW)
         rows = slice(g * SIZE, (g + 1) * SIZE)
         grad = grad_ref[rows, :]
         wide = expander(g)
-        weight = dot(tail, wide)
-        late = dot(in_rows, grad) * weight
-        fetch.wait(g)
-        x = x_ref[:, at].astype(F32)
-        gx_ref[:, at] = (dx_ref[:, at] + late).astype(BF16)
-        put.start(g)
-        gin = gin + dot(grad, (x * weight).astype(BF16), NT)
-        high, low = split(x * late)
+        high, low = split(x_ref[:, at].astype(F32) * lates[g])
         tail_sum = tail_sum + dot(high, wide, NT) + dot(low, wide, NT)
         both = jnp.sum(start_ref[rows, :].astype(F32) * grad.astype(F32), axis=0, keepdims=True)
         high, low = split(jnp.broadcast_to(both, (16, GW)))
         overlap = overlap + dot(high, wide, NT) + dot(low, wide, NT)
-    gin_out_ref[...] = gin.astype(BF16)
-    gout_out_ref[...] = gout_ref[...].astype(BF16)
     tail_sum = jnp.transpose(tail_sum)[:SIZE]
     flow = jnp.transpose(flow_ref[...])[:SIZE]
     direct = jnp.transpose(direct_ref[...])[:SIZE]
     overlap = jnp.transpose(jnp.broadcast_to(overlap[:1], (TOK, TOK)))[:SIZE]
-    tri = jnp.where(iota((TOK, TOK), 0) >= iota((TOK, TOK), 1), 1.0, 0.0)
-    ahead = dot(flow - tail_sum, tri, precision=HIGH)
+    ahead = sums_by(flow - tail_sum, iota((TOK, TOK), 0) >= iota((TOK, TOK), 1))
     ahead = ahead + jnp.sum(tail_sum, axis=1, keepdims=True) + jnp.exp(last) * overlap
     step_grad = (direct + tail_sum) / step + neg * ahead
     raw_grad = step_grad * (1.0 / (1.0 + jnp.exp(-z)))
@@ -789,6 +775,42 @@
     sums_ref[:, 0, 0:TOK] = jnp.transpose(jnp.broadcast_to(both, (TOK, TOK)))[:devices]
     sums_ref[:, 0, TOK : 2 * TOK] = jnp.broadcast_to(skip_sum, (devices, TOK))
     sums_ref[:, 0, 2 * TOK :] = jnp.broadcast_to(gain_sum_ref[...], (devices, TOK))
+
+
+def late_rows_kernel(
+    x_hbm,
+    tail_ref,
+    in_ref,
+    grad_ref,
+    dx_hbm,
+    gout_ref,
+    gin_ref,
+    gx_hbm,
+    gin_out_ref,
+    gout_out_ref,
+    x_ref,
+    dx_ref,
+    gx_ref,
+    sem,
+    out_sem,
+):
+    fetch = Copies(sem, (x_hbm, x_ref, by_lane), (dx_hbm, dx_ref, by_lane))
+    put = Copies(out_sem, (gx_ref, gx_hbm, by_lane))
+    fetch.start_all()
+    tail = tail_ref[...]
+    in_rows = jnp.transpose(in_ref[...].astype(F32)).astype(BF16)
+    gin = gin_ref[...]
+    for g in range(GROUPS):
+        at = slice(g * GW, (g + 1) * GW)
+        grad = grad_ref[g * SIZE : (g + 1) * SIZE, :]
+        weight = dot(tail, expander(g))
+        late = dot(in_rows, grad) * weight
+        fetch.wait(g)
+        gin = gin + dot(grad, (x_ref[:, at].astype(F32) * weight).astype(BF16), NT)
+        gx_ref[:, at] = (dx_ref[:, at] + late).astype(BF16)
+        put.start(g)
+    gin_out_ref[...] = gin.astype(BF16)
+    gout_out_ref[...] = gout_ref[...].astype(BF16)
     put.wait_all()
 
 
@@ -825,6 +847,7 @@
     ]
     return pl.pallas_call(
         kernel,
+        name=getattr(kernel, "func", kernel).__name__,
         out_shape=tuple(made[space](dims, dtype) for space, dims, dtype in outs),
         in_specs=[specs[space] for space, _ in args],
         out_specs=tuple(specs[space] for space, _, _ in outs),
@@ -909,10 +932,10 @@
         us=5,
     )
     back = lax.ppermute(moving, "ctx", swap)
-    (firsts,) = call(
+    firsts, totals = call(
         functools.partial(scan_kernel, blocks, False),
         [("a", gathered)],
-        [("a", states_shape, BF16)],
+        [("a", states_shape, BF16), ("a", (rows, TOK), BF16)],
         [vmem(states_shape, F32)],
         mib=8,
         us=2,
@@ -922,21 +945,20 @@
     inner, grown, skips = call(
         inner_kernel,
         [("h", x), decays, ("a", in_map), ("a", map_in), ("a", skip)],
-        [("h", wide, F32), ("a", square, BF16), ("a", (16, TOK), BF16)],
-        [vmem(wide), vmem(wide, F32)] + decay_scratch + [sems(1, GROUPS), sems(1, GROUPS)],
+        [("a", wide, F32), ("a", square, BF16), ("a", (16, TOK), BF16)],
+        [vmem(wide)] + decay_scratch + [sems(1, GROUPS)],
         us=5,
     )
     gv, home = call(
         value_grad_kernel,
-        tables + [("h", probs), ("h", grad), ("h", back)],
+        tables + [("h", probs), ("h", grad), ("a", back)],
         [("h", wide, BF16), ("h", wide, BF16)],
         [
             vmem(probs_shape, F32),
             vmem(wide),
-            vmem(sent),
-            vmem(wide),
-            vmem(wide),
-            sems(3, GROUPS),
+            vmem(wide),
+            vmem(wide),
+            sems(2, GROUPS),
             sems(2, GROUPS),
         ],
         us=4,
@@ -948,12 +970,11 @@
             ("a", map_in),
             ("a", norm_gain[None]),
             ("a", start),
-            ("h", inner),
+            ("a", inner),
             ("h", gv),
         ],
         [("h", wide, F32), ("h", wide, BF16), ("h", wide, BF16), ("h", message_shape, BF16)],
         [
-            vmem(wide, F32),
             vmem(wide),
             vmem(wide, F32),
             vmem(wide),
@@ -961,9 +982,10 @@
             vmem(message_shape),
             vmem(wide, F32),
             vmem((32, TOK), F32),
+            sems(1, GROUPS),
+            sems(1, GROUPS),
             sems(2, GROUPS),
-            sems(1, GROUPS),
-            sems(3, GROUPS),
+            sems(2, GROUPS),
         ],
         us=4,
     )
@@ -987,7 +1009,7 @@
     received = exchange(message)
     lasts, gain_sum = call(
         functools.partial(scan_kernel, blocks, True),
-        [("a", received), ("a", gathered)],
+        [("a", received), ("a", totals)],
         [("a", states_shape, BF16), ("a", (1, TOK), F32)],
         [vmem(states_shape, F32)],
         mib=8,
@@ -996,7 +1018,7 @@
     state_grad = exchange(lasts)
     dx, *partial = call(
         inner_back_kernel,
-        [("h", x), decays, ("a", in_map), ("a", map_in), ("a", skips), ("a", grown)]
+        [("a", gain_sum), ("h", x), decays, ("a", in_map), ("a", map_in), ("a", skips), ("a", grown)]
         + [("h", start), ("h", y), ("h", low)],
         [
             ("h", wide, F32),
@@ -1005,32 +1027,33 @@
             ("a", maps, F32),
             ("a", maps, F32),
             ("a", (1, TOK), F32),
+            ("a", wide, BF16),
+            ("a", states_shape, BF16),
         ],
-        [vmem(wide), vmem(states_shape), vmem(wide, F32), vmem(wide), vmem(wide, F32)]
+        [vmem(wide, F32), vmem(wide), vmem(wide, F32)]
         + decay_scratch
         + [sems(4, GROUPS), sems(1, GROUPS)],
         us=8,
     )
-    gx, gin, gout, gstep, sums = call(
+    flow, direct, gout, gin, skip_sum, same_x, same_start = partial
+    gstep, sums = call(
         late_kernel,
-        [("h", x), decays, tail, ("a", in_map), ("h", start)]
-        + [("a", state_grad), ("h", dx)]
-        + [("a", part) for part in partial]
-        + [("a", gain_sum)],
-        [
-            ("h", wide, BF16),
-            ("a", maps, BF16),
-            ("a", maps, BF16),
-            ("a", (HEADS, TOK), F32),
-            ("a", (devices, 1, 3 * TOK), F32),
-        ],
-        [vmem(wide), vmem(states_shape), vmem(wide, F32), vmem(wide), sems(3, GROUPS), sems(1, GROUPS)],
-        us=5,
+        [("a", same_x), decays, tail, ("a", in_map), ("a", same_start), ("a", state_grad)]
+        + [("a", flow), ("a", direct), ("a", skip_sum), ("a", gain_sum)],
+        [("a", (HEADS, TOK), F32), ("a", (devices, 1, 3 * TOK), F32)],
+        us=4,
     )
     sums = lax.all_to_all(sums, ("dp", "ctx"), 0, 0, tiled=True)
+    gx, gin, gout = call(
+        late_rows_kernel,
+        [("h", x), tail, ("a", in_map), ("a", state_grad), ("h", dx), ("a", gout), ("a", gin)],
+        [("h", wide, BF16), ("a", maps, BF16), ("a", maps, BF16)],
+        [vmem(wide), vmem(wide, F32), vmem(wide), sems(2, GROUPS), sems(1, GROUPS)],
+        us=3,
+    )
     gq, gk, attn = call(
         attention_grad_kernel,
-        [("h", q), ("h", k), ("h", dscores), ("h", arrived), ("h", attn)],
+        [("a", gstep), ("h", q), ("h", k), ("h", dscores), ("a", arrived), ("h", attn)],
         [("h", wide, BF16), ("h", wide, BF16), ("h", (TOK + SEND, WIDTH), BF16)],
         [
             vmem(wide),
@@ -1038,13 +1061,12 @@
             vmem(probs_shape),
             vmem(wide),
             vmem(wide),
-            vmem(sent),
             sems(3, GROUPS),
             sems(2, GROUPS),
-            sems(2),
+            pltpu.SemaphoreType.DMA,
         ],
         us=6,
-        aliases={4: 2},
+        aliases={5: 2},
     )
     heads, gain = call(
         functools.partial(last_kernel, blocks),

time: 102 us -> 96.8 us (0.949)
  Pallas kernels: 46.5 us -> 43.3 us
  starting transfers between devices: 34.7 us -> 32.8 us
    pallas_call x12 -> x13, Pallas kernels: 46.5 us -> 43.3 us  [call(): pl.pallas_call(kernel, name=getattr(kernel, 'func', kernel).__name__, out...]
    all_to_all x4, waiting for transfers between devices: 12.5 us -> 15.6 us  [exchange(): value = lax.all_to_all(value, 'ctx', 0, 0, tiled=True)]
    all_to_all x1, waiting for transfers between devices: 5.56 us -> 2.56 us  [local(): sums = lax.all_to_all(sums, ('dp', 'ctx'), 0, 0, tiled=True)]
    all_to_all x4, starting transfers between devices: 21.6 us -> 19.8 us  [exchange(): value = lax.all_to_all(value, 'ctx', 0, 0, tiled=True)]
where the time goes in v4:
time: 96.8 us; the launch traced here: 96 us
  Pallas kernels  43.3 us (45%)
  starting transfers between devices  32.8 us (34%)
  waiting for transfers between devices  18.2 us (19%)
    pallas_call x13, Pallas kernels, call(): pl.pallas_call(kernel, name=getattr(kernel, 'func', kernel).__name__, out...  43.3 us
    all_to_all x4, starting transfers between devices, exchange(): value = lax.all_to_all(value, 'ctx', 0, 0, tiled=True)  19.8 us
    all_to_all x4, waiting for transfers between devices, exchange(): value = lax.all_to_all(value, 'ctx', 0, 0, tiled=True)  15.6 us
    all_to_all x1, starting transfers between devices, local(): sums = lax.all_to_all(sums, ('dp', 'ctx'), 0, 0, tiled=True)  7.11 us
    ppermute x1, starting transfers between devices, local(): back = lax.ppermute(moving, 'ctx', swap)  2.97 us
    ppermute x1, starting transfers between devices, local(): arrived = lax.ppermute(packed, 'ctx', swap)  2.93 us
    all_to_all x1, waiting for transfers between devices, local(): sums = lax.all_to_all(sums, ('dp', 'ctx'), 0, 0, tiled=True)  2.56 us
  transfers between devices with their start and end apart: 7, of which 5 were waited for; matrix products, arithmetic and copies ran while one was open for 0% of the time, Pallas kernels for 37%

profile of v4, /device:TPU:1, one launch (start us, length us, event | category | flops | bytes accessed | tf_op | source)
XLA Modules:
  0.0 96.0 jit_solution(3845451634931313423)
XLA Ops:
  0.6 0.0 copy-start.3
  0.7 0.0 copy-start.4
  0.7 3.0 %states_kernel.1 = (bf16[256,1024]{1,0:T(8,128)(2,1)}, f32[4,64,128]{2,1,0:T(8,128)S(1)}, bf16[128,128]{1,0:T(8,128)(2,1)S(1)}) custom-call(bf16[128,3584]{1,0:T(8,128)(2,1)} %bitcast.69, f32[56,128]{1,0:T(8,128)} %bitcast.73, bf16[64,128]{1,0:T(8,128)(2,1)} %bitcast.48, f32[1,56]{1,0:T(1,128)} %bitcast.74, f32[1,56]{1,0:T(1,128)} %bitcast.75), custom_call_target="tpu_custom_call" | custom-call | flops 3000000000 | bytes 8388608 | tf_op jit(solution)/shard_map/states_kernel/pallas_call | solution.py:848
  3.7 8.6 %all-to-all-start = ((bf16[32,8,1024]{2,1,0:T(8,128)(2,1)}), bf16[32,8,1024]{2,1,0:T(8,128)(2,1)S(1)}, u32[]{:S(2)}, u32[]{:S(2)}) async-start(bf16[32,8,1024]{2,1,0:T(8,128)(2,1)} %bitcast.62), calls=%async_computation | async-start | bytes 1048576 | tf_op jit(solution)/shard_map/all_to_all | solution.py:897
  12.3 0.0 copy-done.3
  12.3 0.0 copy-done.4
  12.3 4.0 %weights_kernel.1 = (f32[16,128,128]{2,1,0:T(8,128)}, bf16[64,3584]{1,0:T(8,128)(2,1)}) custom-call(s32[8,32]{1,0:T(8,128)S(1)} %bitcast.53, s32[8,32]{1,0:T(8,128)S(1)} %bitcast.56, bf16[128,3584]{1,0:T(8,128)(2,1)} %bitcast.65, bf16[128,3584]{1,0:T(8,128)(2,1)} %bitcast.67, bf16[192,3584]{1,0:T(8,128)(2,1)} %bitcast.63), custom_call_target="tpu_custom_call" | custom-call | flops 5000000000 | bytes 8388608 | tf_op jit(solution)/shard_map/weights_kernel/pallas_call | solution.py:848
  16.3 3.0 %collective-permute-start = (bf16[64,3584]{1,0:T(8,128)(2,1)}, bf16[64,3584]{1,0:T(8,128)(2,1)S(1)}, u32[]{:S(2)}, u32[]{:S(2)}) collective-permute-start(bf16[64,3584]{1,0:T(8,128)(2,1)} %get-tuple-element.54), channel_id=1, source_target_pairs={{0,16},{1,17},{2,18},{3,19},{4,20},{5,21},{6,22},{7,23},{8,24},{9,... | collective-permute-start | bytes 1376264 | tf_op jit(solution)/shard_map/ppermute | solution.py:934
  19.3 4.8 %all-to-all-done = bf16[32,8,1024]{2,1,0:T(8,128)(2,1)S(1)} async-done(((bf16[32,8,1024]{2,1,0:T(8,128)(2,1)}), bf16[32,8,1024]{2,1,0:T(8,128)(2,1)S(1)}, u32[]{:S(2)}, u32[]{:S(2)}) %all-to-all-start) | async-done | bytes 524320 | tf_op jit(solution)/shard_map/all_to_all | solution.py:897
  24.0 0.0 copy-start.1
  24.0 0.0 copy-start.2
  24.0 0.0 copy-start.5
  24.0 1.1 %scan_kernel.2 = (bf16[256,896]{1,0:T(8,128)(2,1)}, bf16[256,128]{1,0:T(8,128)(2,1)S(1)}) custom-call(bf16[256,1024]{1,0:T(8,128)(2,1)S(1)} %bitcast.40), custom_call_target="tpu_custom_call" | custom-call | flops 2000000000 | bytes 8388608 | tf_op jit(solution)/shard_map/scan_kernel/pallas_call | solution.py:848
  25.1 3.7 %all-to-all-start.1 = ((bf16[32,8,896]{2,1,0:T(8,128)(2,1)}), bf16[32,8,896]{2,1,0:T(8,128)(2,1)S(1)}, u32[]{:S(2)}, u32[]{:S(2)}) async-start(bf16[32,8,896]{2,1,0:T(8,128)(2,1)} %bitcast.11), calls=%async_computation.1 | async-start | bytes 917504 | tf_op jit(solution)/shard_map/all_to_all | solution.py:897
  28.8 0.0 copy-done.1
  28.8 0.0 copy-done.2
  28.8 0.0 copy-done.5
  28.8 0.0 copy-start.9
  28.8 2.8 %inner_kernel.1 = (f32[128,3584]{1,0:T(8,128)S(1)}, bf16[128,128]{1,0:T(8,128)(2,1)S(1)}, bf16[16,128]{1,0:T(8,128)(2,1)S(1)}) custom-call(bf16[128,3584]{1,0:T(8,128)(2,1)} %bitcast.70, f32[4,64,128]{2,1,0:T(8,128)S(1)} %get-tuple-element.48.decays_ref, bf16[64,128]{1,0:T(8,128)(2,1)S(1)} %bitcast.49, bf16[64,128]{1,0:T(8,128)(2,1)S(1)} %bitcast.45, ...), custom_call_target="tpu_custom_call" | custom-call | flops 5000000000 | bytes 8388608 | tf_op jit(solution)/shard_map/inner_kernel/pallas_call | solution.py:848
  31.7 0.0 copy-done.9
  31.7 0.0 copy-start.7
  31.7 0.0 collective-permute-done.back_ref
  31.7 4.2 %value_grad_kernel.1 = (bf16[128,3584]{1,0:T(8,128)(2,1)}, bf16[128,3584]{1,0:T(8,128)(2,1)}) custom-call(s32[8,32]{1,0:T(8,128)S(1)} %bitcast.54, s32[8,32]{1,0:T(8,128)S(1)} %bitcast.57, f32[16,128,128]{2,1,0:T(8,128)} %get-tuple-element.53.probs_hbm, bf16[192,3584]{1,0:T(8,128)(2,1)} %bitcast.64, bf16[64,3584]{1,0:T(8,128)(2,1)S(1)} %collective-permute-done.back_ref), custom_call_target="tpu_custom_call" | custom-call | flops 4000000000 | bytes 8388608 | tf_op jit(solution)/shard_map/value_grad_kernel/pallas_call | solution.py:848
  36.0 3.6 %all-to-all-done.1 = bf16[32,8,896]{2,1,0:T(8,128)(2,1)S(1)} async-done(((bf16[32,8,896]{2,1,0:T(8,128)(2,1)}), bf16[32,8,896]{2,1,0:T(8,128)(2,1)S(1)}, u32[]{:S(2)}, u32[]{:S(2)}) %all-to-all-start.1) | async-done | bytes 458784 | tf_op jit(solution)/shard_map/all_to_all | solution.py:897
  39.6 0.0 copy-start
  39.6 0.0 copy-done.7
  39.6 4.0 %norm_kernel.1 = (f32[128,3584]{1,0:T(8,128)}, bf16[128,3584]{1,0:T(8,128)(2,1)}, bf16[128,3584]{1,0:T(8,128)(2,1)}, bf16[256,1024]{1,0:T(8,128)(2,1)}) custom-call(bf16[128,128]{1,0:T(8,128)(2,1)S(1)} %get-tuple-element.49.grown_ref, bf16[64,128]{1,0:T(8,128)(2,1)S(1)} %bitcast.46, f32[1,3584]{1,0:T(1,128)S(1)} %broadcast_in_dim.36.gain_ref, ...), custom_call_target="tpu_custom_call" | custom-call | flops 4000000000 | bytes 8388608 | tf_op jit(solution)/shard_map/norm_kernel/pallas_call | solution.py:848
  43.6 0.0 copy-done
  43.6 3.7 %all-to-all-start.2 = ((bf16[32,8,1024]{2,1,0:T(8,128)(2,1)}), bf16[32,8,1024]{2,1,0:T(8,128)(2,1)S(1)}, u32[]{:S(2)}, u32[]{:S(2)}) async-start(bf16[32,8,1024]{2,1,0:T(8,128)(2,1)} %bitcast.61), calls=%async_computation.2 | async-start | bytes 1048576 | tf_op jit(solution)/shard_map/all_to_all | solution.py:897
  47.3 4.7 %attention_kernel.1 = (bf16[192,3584]{1,0:T(8,128)(2,1)}, bf16[64,3584]{1,0:T(8,128)(2,1)}, bf16[16,128,128]{2,1,0:T(8,128)(2,1)}) custom-call(s32[8,32]{1,0:T(8,128)S(1)} %bitcast.55, s32[8,32]{1,0:T(8,128)S(1)} %bitcast.58, bf16[128,3584]{1,0:T(8,128)(2,1)} %get-tuple-element.70.values_hbm, f32[16,128,128]{2,1,0:T(8,128)} %get-tuple-element.53.probs_hbm, ...), custom_call_target="tpu_custom_call" | custom-call | flops 5000000000 | bytes 8388608 | tf_op jit(solution)/shard_map/attention_kernel/pallas_call | solution.py:848
  52.1 2.9 %collective-permute-start.1 = (bf16[64,3584]{1,0:T(8,128)(2,1)}, bf16[64,3584]{1,0:T(8,128)(2,1)S(1)}, u32[]{:S(2)}, u32[]{:S(2)}) collective-permute-start(bf16[64,3584]{1,0:T(8,128)(2,1)} %get-tuple-element.73), channel_id=1, source_target_pairs={{0,16},{1,17},{2,18},{3,19},{4,20},{5,21},{6,22},{7,23},{8,24},{9,... | collective-permute-start | bytes 1376264 | tf_op jit(solution)/shard_map/ppermute | solution.py:1008
  55.0 3.9 %all-to-all-done.2 = bf16[32,8,1024]{2,1,0:T(8,128)(2,1)S(1)} async-done(((bf16[32,8,1024]{2,1,0:T(8,128)(2,1)}), bf16[32,8,1024]{2,1,0:T(8,128)(2,1)S(1)}, u32[]{:S(2)}, u32[]{:S(2)}) %all-to-all-start.2) | async-done | bytes 524320 | tf_op jit(solution)/shard_map/all_to_all | solution.py:897
  58.9 0.0 copy-start.8
  58.9 1.2 %scan_kernel.3 = (bf16[256,896]{1,0:T(8,128)(2,1)}, f32[1,128]{1,0:T(1,128)S(1)}) custom-call(bf16[256,1024]{1,0:T(8,128)(2,1)S(1)} %bitcast.39, bf16[256,128]{1,0:T(8,128)(2,1)S(1)} %get-tuple-element.57.refs_1_), custom_call_target="tpu_custom_call" | custom-call | flops 2000000000 | bytes 8388608 | tf_op jit(solution)/shard_map/scan_kernel/pallas_call | solution.py:848
  60.0 3.9 %all-to-all-start.3 = ((bf16[32,8,896]{2,1,0:T(8,128)(2,1)}), bf16[32,8,896]{2,1,0:T(8,128)(2,1)S(1)}, u32[]{:S(2)}, u32[]{:S(2)}) async-start(bf16[32,8,896]{2,1,0:T(8,128)(2,1)} %bitcast.24), calls=%async_computation.3 | async-start | bytes 917504 | tf_op jit(solution)/shard_map/all_to_all | solution.py:897
  63.9 0.0 copy-done.8
  63.9 7.4 %inner_back_kernel.1 = (f32[128,3584]{1,0:T(8,128)}, f32[128,128]{1,0:T(8,128)S(1)}, f32[128,128]{1,0:T(8,128)S(1)}, f32[64,128]{1,0:T(8,128)S(1)}, f32[64,128]{...) custom-call(f32[1,128]{1,0:T(1,128)S(1)} %get-tuple-element.58.after_ref.gain_su, ...), custom_call_target="tpu_custom_call" | custom-call | flops 8000000000 | bytes 8388608 | tf_op jit(solution)/shard_map/inner_back_kernel/pallas_call | solution.py:848
  71.3 3.3 %all-to-all-done.3 = bf16[32,8,896]{2,1,0:T(8,128)(2,1)S(1)} async-done(((bf16[32,8,896]{2,1,0:T(8,128)(2,1)}), bf16[32,8,896]{2,1,0:T(8,128)(2,1)S(1)}, u32[]{:S(2)}, u32[]{:S(2)}) %all-to-all-start.3) | async-done | bytes 458784 | tf_op jit(solution)/shard_map/all_to_all | solution.py:897
  74.6 3.0 %late_kernel.1 = (f32[56,128]{1,0:T(8,128)}, f32[128,1,384]{2,1,0:T(1,128)}) custom-call(bf16[128,3584]{1,0:T(8,128)(2,1)S(1)} %get-tuple-element.62.x_ref, f32[4,64,128]{2,1,0:T(8,128)S(1)} %get-tuple-element.48.decays_ref, bf16[128,128]{1,0:T(8,128)(2,1)S(1)} %get-tuple-element.63.tail_ref, bf16[64,128]{1,0:T(8,128)(2,1)S(1)} %bitcast.51, ...), custom_call_target="tpu_custom_call" | custom-call | flops 4000000000 | bytes 8388608 | tf_op jit(solution)/shard_map/late_kernel/pallas_call | solution.py:848
  77.6 7.1 %all-to-all-start.4 = ((f32[128,1,384]{2,1,0:T(1,128)}), f32[128,1,384]{2,1,0:T(1,128)S(1)}, u32[]{:S(2)}, u32[]{:S(2)}) async-start(f32[128,1,384]{2,1,0:T(1,128)} %get-tuple-element.84), calls=%async_computation.4 | async-start | bytes 393216 | tf_op jit(solution)/shard_map/all_to_all | solution.py:1046
  84.8 0.0 collective-permute-done.1.arrived_ref
  84.8 0.0 copy-start.6
  84.8 0.7 copy-done.6
  85.5 3.4 %attention_grad_kernel.1 = (bf16[128,3584]{1,0:T(8,128)(2,1)}, bf16[128,3584]{1,0:T(8,128)(2,1)}, bf16[192,3584]{1,0:T(8,128)(2,1)}) custom-call(f32[56,128]{1,0:T(8,128)S(1)} %copy-done.6, bf16[128,3584]{1,0:T(8,128)(2,1)} %bitcast.66, bf16[128,3584]{1,0:T(8,128)(2,1)} %bitcast.68, ...), custom_call_target="tpu_custom_call", output_to_operand_aliasing={{2}: (5, {})} | custom-call | flops 6000000000 | bytes 8388608 | tf_op jit(solution)/shard_map/attention_grad_kernel/pallas_call | solution.py:848
  88.9 3.8 %late_rows_kernel.1 = (bf16[128,3584]{1,0:T(8,128)(2,1)}, bf16[64,128]{1,0:T(8,128)(2,1)}, bf16[64,128]{1,0:T(8,128)(2,1)}) custom-call(bf16[128,3584]{1,0:T(8,128)(2,1)} %bitcast.72, bf16[128,128]{1,0:T(8,128)(2,1)S(1)} %get-tuple-element.63.tail_ref, bf16[64,128]{1,0:T(8,128)(2,1)S(1)} %bitcast.52, bf16[256,896]{1,0:T(8,128)(2,1)S(1)} %bitcast.44, ...), custom_call_target="tpu_custom_call" | custom-call | flops 3000000000 | bytes 8388608 | tf_op jit(solution)/shard_map/late_rows_kernel/pallas_call | solution.py:848
  92.7 2.6 %all-to-all-done.4.sums_ref = f32[128,1,384]{2,1,0:T(1,128)S(1)} async-done(((f32[128,1,384]{2,1,0:T(1,128)}), f32[128,1,384]{2,1,0:T(1,128)S(1)}, u32[]{:S(2)}, u32[]{:S(2)}) %all-to-all-start.4) | async-done | bytes 196640 | tf_op jit(solution)/shard_map/all_to_all | solution.py:1046
  95.3 0.7 last_kernel.1
  (1 shorter events, 0.0 us)
Async XLA Ops:
  0.6 11.6 %copy-start.3 = (s32[1,32,8]{1,2,0:T(8,128)S(1)}, s32[1,32,8]{1,2,0:T(8,128)}, u32[]{:S(2)}) copy-start(s32[1,32,8]{1,2,0:T(8,128)} %param.21) | copy-start | bytes 3076
  0.7 11.6 %copy-start.4 = (s32[1,32,8]{1,2,0:T(8,128)S(1)}, s32[1,32,8]{1,2,0:T(8,128)}, u32[]{:S(2)}) copy-start(s32[1,32,8]{1,2,0:T(8,128)} %param.22) | copy-start | bytes 3076
  3.7 20.3 %all-to-all-start = ((bf16[32,8,1024]{2,1,0:T(8,128)(2,1)}), bf16[32,8,1024]{2,1,0:T(8,128)(2,1)S(1)}, u32[]{:S(2)}, u32[]{:S(2)}) async-start(bf16[32,8,1024]{2,1,0:T(8,128)(2,1)} %bitcast.62), calls=%async_computation | async-start | bytes 1048576 | tf_op jit(solution)/shard_map/all_to_all | solution.py:897
  16.3 15.4 %collective-permute-start = (bf16[64,3584]{1,0:T(8,128)(2,1)}, bf16[64,3584]{1,0:T(8,128)(2,1)S(1)}, u32[]{:S(2)}, u32[]{:S(2)}) collective-permute-start(bf16[64,3584]{1,0:T(8,128)(2,1)} %get-tuple-element.54), channel_id=1, source_target_pairs={{0,16},{1,17},{2,18},{3,19},{4,20},{5,21},{6,22},{7,23},{8,24},{9,... | collective-permute-start | bytes 1376264 | tf_op jit(solution)/shard_map/ppermute | solution.py:934
  24.0 4.8 %copy-start.1 = (bf16[1,128,64]{1,2,0:T(8,128)(2,1)S(1)}, bf16[1,128,64]{1,2,0:T(8,128)(2,1)}, u32[]{:S(2)}) copy-start(bf16[1,128,64]{1,2,0:T(8,128)(2,1)} %param.16) | copy-start | bytes 49156
  24.0 4.8 %copy-start.2 = (bf16[1,128,64]{1,2,0:T(8,128)(2,1)S(1)}, bf16[1,128,64]{1,2,0:T(8,128)(2,1)}, u32[]{:S(2)}) copy-start(bf16[1,128,64]{1,2,0:T(8,128)(2,1)} %param.15) | copy-start | bytes 49156
  24.0 4.8 %copy-start.5 = (f32[56]{0:T(128)S(1)}, f32[56]{0:T(128)}, u32[]{:S(2)}) copy-start(f32[56]{0:T(128)} %param.19) | copy-start | bytes 676
  25.1 14.5 %all-to-all-start.1 = ((bf16[32,8,896]{2,1,0:T(8,128)(2,1)}), bf16[32,8,896]{2,1,0:T(8,128)(2,1)S(1)}, u32[]{:S(2)}, u32[]{:S(2)}) async-start(bf16[32,8,896]{2,1,0:T(8,128)(2,1)} %bitcast.11), calls=%async_computation.1 | async-start | bytes 917504 | tf_op jit(solution)/shard_map/all_to_all | solution.py:897
  28.8 2.8 %copy-start.9 = (f32[3584]{0:T(1024)S(1)}, f32[3584]{0:T(1024)}, u32[]{:S(2)}) copy-start(f32[3584]{0:T(1024)} %param.20) | copy-start | bytes 43012
  31.7 7.9 %copy-start.7 = (bf16[128,128]{1,0:T(8,128)(2,1)}, bf16[128,128]{1,0:T(8,128)(2,1)S(1)}, u32[]{:S(2)}) copy-start(bf16[128,128]{1,0:T(8,128)(2,1)S(1)} %get-tuple-element.49.grown_ref) | copy-start | bytes 98308
  39.6 4.0 %copy-start = (bf16[32,8,896]{2,1,0:T(8,128)(2,1)}, bf16[32,8,896]{2,1,0:T(8,128)(2,1)S(1)}, u32[]{:S(2)}) copy-start(bf16[32,8,896]{2,1,0:T(8,128)(2,1)S(1)} %all-to-all-done.1) | copy-start | bytes 1376260
  43.6 15.3 %all-to-all-start.2 = ((bf16[32,8,1024]{2,1,0:T(8,128)(2,1)}), bf16[32,8,1024]{2,1,0:T(8,128)(2,1)S(1)}, u32[]{:S(2)}, u32[]{:S(2)}) async-start(bf16[32,8,1024]{2,1,0:T(8,128)(2,1)} %bitcast.61), calls=%async_computation.2 | async-start | bytes 1048576 | tf_op jit(solution)/shard_map/all_to_all | solution.py:897
  52.1 32.7 %collective-permute-start.1 = (bf16[64,3584]{1,0:T(8,128)(2,1)}, bf16[64,3584]{1,0:T(8,128)(2,1)S(1)}, u32[]{:S(2)}, u32[]{:S(2)}) collective-permute-start(bf16[64,3584]{1,0:T(8,128)(2,1)} %get-tuple-element.73), channel_id=1, source_target_pairs={{0,16},{1,17},{2,18},{3,19},{4,20},{5,21},{6,22},{7,23},{8,24},{9,... | collective-permute-start | bytes 1376264 | tf_op jit(solution)/shard_map/ppermute | solution.py:1008
  58.9 5.0 %copy-start.8 = (bf16[128,128]{1,0:T(8,128)(2,1)S(1)}, bf16[128,128]{1,0:T(8,128)(2,1)}, u32[]{:S(2)}) copy-start(bf16[128,128]{1,0:T(8,128)(2,1)} %copy-done.7) | copy-start | bytes 98308
  60.0 14.6 %all-to-all-start.3 = ((bf16[32,8,896]{2,1,0:T(8,128)(2,1)}), bf16[32,8,896]{2,1,0:T(8,128)(2,1)S(1)}, u32[]{:S(2)}, u32[]{:S(2)}) async-start(bf16[32,8,896]{2,1,0:T(8,128)(2,1)} %bitcast.24), calls=%async_computation.3 | async-start | bytes 917504 | tf_op jit(solution)/shard_map/all_to_all | solution.py:897
  77.6 17.7 %all-to-all-start.4 = ((f32[128,1,384]{2,1,0:T(1,128)}), f32[128,1,384]{2,1,0:T(1,128)S(1)}, u32[]{:S(2)}, u32[]{:S(2)}) async-start(f32[128,1,384]{2,1,0:T(1,128)} %get-tuple-element.84), calls=%async_computation.4 | async-start | bytes 393216 | tf_op jit(solution)/shard_map/all_to_all | solution.py:1046
  84.8 0.8 copy-start.6
